TPU v7x, 128 devices: a whole 4x4x4 slice. The times are simulated.
128 devices in a mesh: label: 32 (over y, x, z_hi), sub: 4 (over z_lo, core).
Axes of the slice: x: 4, y: 4, z: 4 (z_hi: 2, z_lo: 2; z = z_hi * 2 + z_lo), core: 2. Of those that a mesh axis runs over, the one named last changes fastest.
Arguments:
- features: bfloat16 [2048, 768], P(('label', 'sub')), may hold values from -6 to 6
- label_weight: bfloat16 [262144, 768], P(('label', 'sub')), may hold values from -0.21875 to 0.21875
- label_bias: float32 [262144], P(('label', 'sub')), may hold values from -5 to -1
- positive_ids: int32 [2048, 16], replicated, may hold values from 0 to 262143
- positive_counts: int32 [2048], replicated, may hold values from 1 to 16
Outputs:
- weight_grad: bfloat16 [262144, 768], P(('label', 'sub'))
- feature_grad: float32 [2048, 768], P(('label', 'sub'))
Inputs may be any that keep to these rules, and one draw needn't show every extreme that they name: `positive_ids`: only the first positive_counts[q] entries of row q name positive labels; entries may repeat.
All inputs are finite; a program needn't handle non-finite values.
Results may differ from a plain program's by a relative error of at most 0.0075.
Values may be sent and summed in bfloat16 or wider, within the bound.
No kernel may reach another device: no remote copies, remote signals or barrier semaphores. Data moves between devices by JAX's collectives and lax.ppermute only.
A program may use at most 128 MiB of HBM per device.

v0:
```python
import jax
import jax.numpy as jnp
from jax import lax
from jax.sharding import PartitionSpec as P

BLK = 512


def on_device(features, label_weight, label_bias, positive_ids, positive_counts):
    gathered = lax.all_gather(features, ("label", "sub"), axis=0, tiled=True)
    rows_dev = label_weight.shape[0]
    width = label_weight.shape[1]
    queries = gathered.shape[0]
    nblocks = rows_dev // BLK
    base = lax.axis_index(("label", "sub")) * rows_dev
    slots = jnp.arange(positive_ids.shape[1], dtype=jnp.int32)
    masked_ids = jnp.where(slots[None, :] < positive_counts[:, None], positive_ids, -1)
    weight_blocks = label_weight.reshape(nblocks, BLK, width)
    bias_blocks = label_bias.reshape(nblocks, BLK)
    offsets = jnp.arange(nblocks, dtype=jnp.int32) * BLK

    def step(accum, item):
        wblock, bblock, offset = item
        logits = (
            lax.dot_general(
                gathered, wblock, (((1,), (1,)), ((), ())), preferred_element_type=jnp.float32
            )
            + bblock[None, :]
        )
        labels_here = base + offset + jnp.arange(BLK, dtype=jnp.int32)
        hits = jnp.any(masked_ids[:, :, None] == labels_here[None, None, :], axis=1)
        targets = hits.astype(jnp.float32)
        residual_grad = (jax.nn.sigmoid(logits) - targets).astype(jnp.bfloat16)
        wgrad = lax.dot_general(
            residual_grad, gathered, (((0,), (0,)), ((), ())), preferred_element_type=jnp.float32
        ).astype(jnp.bfloat16)
        accum = accum + jnp.dot(residual_grad, wblock, preferred_element_type=jnp.float32)
        return (accum, wgrad)

    init = jnp.zeros((queries, width), jnp.float32)
    partial_grad, wgrads = lax.scan(step, init, (weight_blocks, bias_blocks, offsets))
    feature_grad = lax.psum_scatter(partial_grad, ("label", "sub"), scatter_dimension=0, tiled=True)
    return (wgrads.reshape(rows_dev, width), feature_grad)


def solution(mesh):
    placed = (P(("label", "sub"), None), P(("label", "sub"), None), P(("label", "sub")), P(), P())
    return jax.shard_map(
        on_device,
        mesh=mesh,
        in_specs=placed,
        out_specs=(P(("label", "sub"), None), P(("label", "sub"), None)),
        check_vma=False,
    )
```

profile of v0, /device:TPU:0, one launch (start us, length us, event | category | flops | bytes accessed | tf_op | source)
XLA Modules:
  0.0 422.0 jit_solution(14437868638265663291)
XLA Ops:
  7.2 0.0 all-gather.2.cloned.1.call-start
  7.2 0.7 all-gather.2.cloned.1.call-update
  7.9 0.0 reduce-scatter.2.cloned.1.call-start
  8.0 0.7 reshape.20
  8.7 1.2 copy.9
  9.9 1.0 fusion.9
  11.0 68.3 %all-gather.2.cloned.1.call-done = bf16[2048,768]{1,0:T(8,128)(2,1)} async-done(((bf16[16,768]{1,0:T(8,128)(2,1)}), bf16[2048,768]{1,0:T(8,128)(2,1)}) %all-gather.2.cloned.1.call-update) | async-done | bytes 3145744 | tf_op jit(solution)/shard_map/all_gather | solution.py:10
  79.3 125.6 %while.13 = (s32[]{:T(128)}, f32[2048,768]{1,0:T(8,128)}, bf16[4,512,768]{2,1,0:T(8,128)(2,1)}, bf16[4,512,768]{2,1,0:T(8,128)(2,1)}, bf16[2048,768]{1,0:T(8,128...) while((s32[]{:T(128)}, f32[2048,768]{1,0:T(8,128)}, ...), condition=%wide.region_2.3_spmd.clone, body=%wide.region_0.2_spmd.clone.sunk | while | flops 4875223552 | bytes 88484112 | solution.py:41
  79.3 0.6 dynamic_slice.31
  80.6 14.3 %compare_reduce_fusion.2 = pred[2048,512]{1,0:T(8,128)(4,1)S(1)} fusion(s32[512]{0:T(512)S(1)} %iota_add_fusion.2, s32[2048,16]{1,0:T(8,128)S(1)} %get-tuple-element.183), kind=kLoop, calls=%fused_computation.clone.1 | loop fusion | flops 32505856 | bytes 1181696 | tf_op jit(solution)/shard_map/while/body/eval_jaxpr/reduce_or | solution.py:31
  94.9 0.0 slice-start
  94.9 1.2 copy.11
  96.1 0.0 slice-start.1
  96.1 4.6 %fusion.28 = bf16[2048,512]{0,1:T(8,128)(2,1)S(1)} fusion(pred[2048,512]{0,1:T(32,128)(4,1)S(1)} %copy.11, bf16[2048,768]{1,0:T(8,128)(2,1)} %get-tuple-element.181, f32[512]{0:T(512)S(1)} %bitcast.44, bf16[4,512,768]{2,1,0:T(8,128)(2,1)} %get-tuple-element.180, s32[]{:T(128)S(6)} %copy.16), kind=kOutput, calls=%fused_computation.3.clone.1 | convolution fusion | flops 1617952768 | bytes 7079940 | tf_op jit(solution)/shard_map/while/body/eval_jaxpr/dot_general | solution.py:25
  100.7 2.7 fusion.29
  103.4 4.6 %select_add_fusion.2 = f32[2048,768]{1,0:T(8,128)S(1)} fusion(f32[2048,768]{1,0:T(8,128)S(1)} %bitcast.42, bf16[2048,512]{0,1:T(8,128)(2,1)S(1)} %fusion.28, pred[]{:T(512)S(6)} %compare.3, bf16[4,512,768]{2,1,0:T(8,128)(2,1)} %get-tuple-element.180, s32[]{:T(128)S(6)} %copy.16), kind=kOutput, calls=%fused_computation.1.clone.1 | convolution fusion | flops 1613758464 | bytes 15466501 | tf_op jit(solution)/shard_map/while/body/eval_jaxpr/dot_general | solution.py:37
  108.1 2.6 copy-done
  110.7 0.6 dynamic_slice.31
  112.0 14.3 %compare_reduce_fusion.2 = pred[2048,512]{1,0:T(8,128)(4,1)S(1)} fusion(s32[512]{0:T(512)S(1)} %iota_add_fusion.2, s32[2048,16]{1,0:T(8,128)S(1)} %get-tuple-element.183), kind=kLoop, calls=%fused_computation.clone.1 | loop fusion | flops 32505856 | bytes 1181696 | tf_op jit(solution)/shard_map/while/body/eval_jaxpr/reduce_or | solution.py:31
  126.3 0.0 slice-start
  126.3 1.2 copy.11
  127.5 0.0 slice-start.1
  127.5 4.6 %fusion.28 = bf16[2048,512]{0,1:T(8,128)(2,1)S(1)} fusion(pred[2048,512]{0,1:T(32,128)(4,1)S(1)} %copy.11, bf16[2048,768]{1,0:T(8,128)(2,1)} %get-tuple-element.181, f32[512]{0:T(512)S(1)} %bitcast.44, bf16[4,512,768]{2,1,0:T(8,128)(2,1)} %get-tuple-element.180, s32[]{:T(128)S(6)} %copy.16), kind=kOutput, calls=%fused_computation.3.clone.1 | convolution fusion | flops 1617952768 | bytes 7079940 | tf_op jit(solution)/shard_map/while/body/eval_jaxpr/dot_general | solution.py:25
  132.1 2.7 fusion.29
  134.8 4.6 %select_add_fusion.2 = f32[2048,768]{1,0:T(8,128)S(1)} fusion(f32[2048,768]{1,0:T(8,128)S(1)} %bitcast.42, bf16[2048,512]{0,1:T(8,128)(2,1)S(1)} %fusion.28, pred[]{:T(512)S(6)} %compare.3, bf16[4,512,768]{2,1,0:T(8,128)(2,1)} %get-tuple-element.180, s32[]{:T(128)S(6)} %copy.16), kind=kOutput, calls=%fused_computation.1.clone.1 | convolution fusion | flops 1613758464 | bytes 15466501 | tf_op jit(solution)/shard_map/while/body/eval_jaxpr/dot_general | solution.py:37
  139.5 2.6 copy-done
  142.1 0.6 dynamic_slice.31
  143.4 14.3 %compare_reduce_fusion.2 = pred[2048,512]{1,0:T(8,128)(4,1)S(1)} fusion(s32[512]{0:T(512)S(1)} %iota_add_fusion.2, s32[2048,16]{1,0:T(8,128)S(1)} %get-tuple-element.183), kind=kLoop, calls=%fused_computation.clone.1 | loop fusion | flops 32505856 | bytes 1181696 | tf_op jit(solution)/shard_map/while/body/eval_jaxpr/reduce_or | solution.py:31
  157.7 0.0 slice-start
  157.7 1.2 copy.11
  158.9 0.0 slice-start.1
  158.9 4.6 %fusion.28 = bf16[2048,512]{0,1:T(8,128)(2,1)S(1)} fusion(pred[2048,512]{0,1:T(32,128)(4,1)S(1)} %copy.11, bf16[2048,768]{1,0:T(8,128)(2,1)} %get-tuple-element.181, f32[512]{0:T(512)S(1)} %bitcast.44, bf16[4,512,768]{2,1,0:T(8,128)(2,1)} %get-tuple-element.180, s32[]{:T(128)S(6)} %copy.16), kind=kOutput, calls=%fused_computation.3.clone.1 | convolution fusion | flops 1617952768 | bytes 7079940 | tf_op jit(solution)/shard_map/while/body/eval_jaxpr/dot_general | solution.py:25
  163.5 2.7 fusion.29
  166.2 4.6 %select_add_fusion.2 = f32[2048,768]{1,0:T(8,128)S(1)} fusion(f32[2048,768]{1,0:T(8,128)S(1)} %bitcast.42, bf16[2048,512]{0,1:T(8,128)(2,1)S(1)} %fusion.28, pred[]{:T(512)S(6)} %compare.3, bf16[4,512,768]{2,1,0:T(8,128)(2,1)} %get-tuple-element.180, s32[]{:T(128)S(6)} %copy.16), kind=kOutput, calls=%fused_computation.1.clone.1 | convolution fusion | flops 1613758464 | bytes 15466501 | tf_op jit(solution)/shard_map/while/body/eval_jaxpr/dot_general | solution.py:37
  170.9 2.6 copy-done
  173.5 0.6 dynamic_slice.31
  174.8 14.3 %compare_reduce_fusion.2 = pred[2048,512]{1,0:T(8,128)(4,1)S(1)} fusion(s32[512]{0:T(512)S(1)} %iota_add_fusion.2, s32[2048,16]{1,0:T(8,128)S(1)} %get-tuple-element.183), kind=kLoop, calls=%fused_computation.clone.1 | loop fusion | flops 32505856 | bytes 1181696 | tf_op jit(solution)/shard_map/while/body/eval_jaxpr/reduce_or | solution.py:31
  189.1 0.0 slice-start
  189.1 1.2 copy.11
  190.3 0.0 slice-start.1
  190.3 4.6 %fusion.28 = bf16[2048,512]{0,1:T(8,128)(2,1)S(1)} fusion(pred[2048,512]{0,1:T(32,128)(4,1)S(1)} %copy.11, bf16[2048,768]{1,0:T(8,128)(2,1)} %get-tuple-element.181, f32[512]{0:T(512)S(1)} %bitcast.44, bf16[4,512,768]{2,1,0:T(8,128)(2,1)} %get-tuple-element.180, s32[]{:T(128)S(6)} %copy.16), kind=kOutput, calls=%fused_computation.3.clone.1 | convolution fusion | flops 1617952768 | bytes 7079940 | tf_op jit(solution)/shard_map/while/body/eval_jaxpr/dot_general | solution.py:25
  194.9 0.0 copy-done.1
  194.9 2.7 fusion.29
  197.7 4.6 %select_add_fusion.2 = f32[2048,768]{1,0:T(8,128)S(1)} fusion(f32[2048,768]{1,0:T(8,128)S(1)} %bitcast.42, bf16[2048,512]{0,1:T(8,128)(2,1)S(1)} %fusion.28, pred[]{:T(512)S(6)} %compare.3, bf16[4,512,768]{2,1,0:T(8,128)(2,1)} %get-tuple-element.180, s32[]{:T(128)S(6)} %copy.16), kind=kOutput, calls=%fused_computation.1.clone.1 | convolution fusion | flops 1613758464 | bytes 15466501 | tf_op jit(solution)/shard_map/while/body/eval_jaxpr/dot_general | solution.py:37
  202.3 0.0 copy-start
  202.3 2.6 copy-done
  204.9 0.0 reduce-scatter.2.cloned.1.call-update
  205.0 210.2 %reduce-scatter.2.cloned.1.call-done = f32[16,768]{1,0:T(8,128)} async-done(((f32[2048,768]{1,0:T(8,128)}), f32[16,768]{1,0:T(8,128)}) %reduce-scatter.2.cloned.1.call-update) | async-done | bytes 49168 | tf_op jit(solution)/shard_map/reduce_scatter | solution.py:42
  (33 shorter events, 0.1 us)
Async XLA Ops:
  7.2 72.2 %all-gather.2.cloned.1.call-start = ((), (), s32[]{:S(2)}) async-start(), calls=%async_computation.1 | async-start | bytes 3170304 | tf_op jit(solution)/shard_map/all_gather | solution.py:10
  7.9 407.3 %reduce-scatter.2.cloned.1.call-start = ((), (), s32[]{:S(2)}) async-start(), calls=%async_computation.2 | async-start | bytes 6340608 | tf_op jit(solution)/shard_map/reduce_scatter | solution.py:42
  94.9 8.5 %slice-start = ((s8[6291456]{0:T(1024)(128)(4,1)}), s8[4194304]{0:T(1024)(128)(4,1)S(1)}, s32[]{:S(2)}) async-start(s8[6291456]{0:T(1024)(128)(4,1)} %bitcast.41), calls=%async_computation.3 | async-start | bytes 8388608 | tf_op jit(solution)/shard_map/while
  96.1 4.6 %copy-start.1 = (bf16[2048,768]{1,0:T(8,128)(2,1)S(1)}, bf16[2048,768]{1,0:T(8,128)(2,1)}, u32[]{:S(2)}) copy-start(bf16[2048,768]{1,0:T(8,128)(2,1)} %get-tuple-element.181) | copy-start | bytes 9437188 | tf_op jit(solution)/shard_map/while
  96.1 7.3 %slice-start.1 = ((s8[6291456]{0:T(1024)(128)(4,1)}), s8[2097152]{0:T(1024)(128)(4,1)S(1)}, s32[]{:S(2)}) async-start(s8[6291456]{0:T(1024)(128)(4,1)} %bitcast.41), calls=%async_computation.4 | async-start | bytes 4194304 | tf_op jit(solution)/shard_map/while
  108.1 2.7 copy-start
  126.3 8.5 %slice-start = ((s8[6291456]{0:T(1024)(128)(4,1)}), s8[4194304]{0:T(1024)(128)(4,1)S(1)}, s32[]{:S(2)}) async-start(s8[6291456]{0:T(1024)(128)(4,1)} %bitcast.41), calls=%async_computation.3 | async-start | bytes 8388608 | tf_op jit(solution)/shard_map/while
  127.5 4.6 %copy-start.1 = (bf16[2048,768]{1,0:T(8,128)(2,1)S(1)}, bf16[2048,768]{1,0:T(8,128)(2,1)}, u32[]{:S(2)}) copy-start(bf16[2048,768]{1,0:T(8,128)(2,1)} %get-tuple-element.181) | copy-start | bytes 9437188 | tf_op jit(solution)/shard_map/while
  127.5 7.3 %slice-start.1 = ((s8[6291456]{0:T(1024)(128)(4,1)}), s8[2097152]{0:T(1024)(128)(4,1)S(1)}, s32[]{:S(2)}) async-start(s8[6291456]{0:T(1024)(128)(4,1)} %bitcast.41), calls=%async_computation.4 | async-start | bytes 4194304 | tf_op jit(solution)/shard_map/while
  139.5 2.7 copy-start
  157.7 8.5 %slice-start = ((s8[6291456]{0:T(1024)(128)(4,1)}), s8[4194304]{0:T(1024)(128)(4,1)S(1)}, s32[]{:S(2)}) async-start(s8[6291456]{0:T(1024)(128)(4,1)} %bitcast.41), calls=%async_computation.3 | async-start | bytes 8388608 | tf_op jit(solution)/shard_map/while
  158.9 4.6 %copy-start.1 = (bf16[2048,768]{1,0:T(8,128)(2,1)S(1)}, bf16[2048,768]{1,0:T(8,128)(2,1)}, u32[]{:S(2)}) copy-start(bf16[2048,768]{1,0:T(8,128)(2,1)} %get-tuple-element.181) | copy-start | bytes 9437188 | tf_op jit(solution)/shard_map/while
  158.9 7.3 %slice-start.1 = ((s8[6291456]{0:T(1024)(128)(4,1)}), s8[2097152]{0:T(1024)(128)(4,1)S(1)}, s32[]{:S(2)}) async-start(s8[6291456]{0:T(1024)(128)(4,1)} %bitcast.41), calls=%async_computation.4 | async-start | bytes 4194304 | tf_op jit(solution)/shard_map/while
  170.9 2.7 copy-start
  189.1 8.5 %slice-start = ((s8[6291456]{0:T(1024)(128)(4,1)}), s8[4194304]{0:T(1024)(128)(4,1)S(1)}, s32[]{:S(2)}) async-start(s8[6291456]{0:T(1024)(128)(4,1)} %bitcast.41), calls=%async_computation.3 | async-start | bytes 8388608 | tf_op jit(solution)/shard_map/while
  190.3 4.6 %copy-start.1 = (bf16[2048,768]{1,0:T(8,128)(2,1)S(1)}, bf16[2048,768]{1,0:T(8,128)(2,1)}, u32[]{:S(2)}) copy-start(bf16[2048,768]{1,0:T(8,128)(2,1)} %get-tuple-element.181) | copy-start | bytes 9437188 | tf_op jit(solution)/shard_map/while
  190.3 7.4 %slice-start.1 = ((s8[6291456]{0:T(1024)(128)(4,1)}), s8[2097152]{0:T(1024)(128)(4,1)S(1)}, s32[]{:S(2)}) async-start(s8[6291456]{0:T(1024)(128)(4,1)} %bitcast.41), calls=%async_computation.4 | async-start | bytes 4194304 | tf_op jit(solution)/shard_map/while
  202.3 2.7 copy-start
Sparse Core Ops, SparseCore 0:
  11.0 68.2 all-gather.1
  205.1 210.0 reduce-scatter.1
where the time goes:
time: 422 us
  waiting for transfers between devices  279 us (66%)
  other arithmetic  58.2 us (14%)
  matrix products  47.7 us (11%)
  local copies, waits for them, and re-layouts  19.8 us (5%)
  between operations  14.1 us (3%)
    reduce_scatter x1, waiting for transfers between devices, on_device(): lax.psum_scatter(partial_grad, ('label', 'sub'), scatter_dimension=0, til...  210 us
    all_gather x1, waiting for transfers between devices, on_device(): gathered = lax.all_gather(features, ('label', 'sub'), axis=0, tiled=True)  68.3 us
    reduce_or x4, other arithmetic, step(): hits = jnp.any(masked_ids[:, :, None] == labels_here[None, None, :], axis=1)  57.1 us
    dot_general x4, matrix products, step(): lax.dot_general(gathered, wblock, (((1,), (1,)), ((), ())), preferred_ele...  18.5 us
    dot_general x4, matrix products, step(): jnp.dot(residual_grad, wblock, preferred_element_type=jnp.float32)  18.4 us
    dot_general x4, matrix products, step(): lax.dot_general(residual_grad, gathered, (((0,), (0,)), ((), ())), prefer...  10.8 us
    while x32, local copies, waits for them, and re-layouts  10.7 us
  transfers between devices with their start and end apart: 2, of which 2 were waited for; matrix products, arithmetic and copies ran while one was open for 1% of the time, Pallas kernels for 0%

commit v1 on v0

v1 whole, which is shorter than its diff:
```python
import functools

import jax
import jax.numpy as jnp
from jax import lax
from jax.experimental import pallas as pl
from jax.experimental.pallas import tpu as pltpu
from jax.sharding import PartitionSpec as P

AXES = ("label", "sub")
N = 4
STRIDE = {"y": 32, "x": 8, "z": 2}
LANES = 128
SUB = 1024
WSUB = 512
VMEM = pltpu.VMEM
WHOLE = pl.BlockSpec(memory_space=VMEM)


def vmem(x):
    return pltpu.with_memory_space_constraint(x, VMEM)


STAGES = {"first": ("z", "z"), "second": ("y", "x"), "third": ("x", "y")}


def shifted(stage, k):
    pairs = []
    for d in range(2 * N * N * N):
        step = STRIDE[STAGES[stage][d % 2]]
        at = d // step % N
        pairs.append((d, d + ((at + k) % N - at) * step))
    return pairs


def fetch(x, stage, k):
    return lax.ppermute(x, AXES, shifted(stage, -k))


def push(x, stage, k):
    return lax.ppermute(x, AXES, shifted(stage, k))


def swap(x):
    return lax.ppermute(x, AXES, [(d, d ^ 1) for d in range(2 * N * N * N)])


def words_kernel(rows, pos_ref, ids_ref, out_ref):
    core, base, own = pos_ref[0], pos_ref[1], pos_ref[2]
    pos3, pos2, pos1 = pos_ref[3], pos_ref[4], pos_ref[5]
    stride3 = jnp.where(core == 0, 8, 32)
    stride2 = jnp.where(core == 0, 32, 8)
    lane = lax.broadcasted_iota(jnp.int32, (rows, LANES), 1)

    def piece(p, carry):
        k, a, b = p // (N * N), p // N % N, p % N
        device = (pos3 + k) % N * stride3 + (pos2 + a) % N * stride2 + (pos1 + b) % N * 2 + core
        ids = ids_ref[pl.ds(pl.multiple_of(device * rows, rows), rows), :]
        rel = ids - base
        valid = jnp.logical_and(rel >= 0, rel < 2 * own)
        rel = jnp.where(valid, rel, 0) ^ (core * own)
        bit = jnp.where(valid, lax.shift_left(jnp.ones_like(rel), rel >> 7), 0)
        low = rel & (LANES - 1)
        words = jnp.zeros((rows, LANES), jnp.int32)
        for j in range(ids.shape[1]):
            words = words | jnp.where(lane == low[:, j : j + 1], bit[:, j : j + 1], 0)
        out_ref[pl.ds(pl.multiple_of(p * rows, rows), rows), :] = words
        return carry

    lax.fori_loop(0, N * N * N, piece, 0)


def label_words(pos, masked_ids, rows):
    return pl.pallas_call(
        functools.partial(words_kernel, rows),
        in_specs=[pl.BlockSpec(memory_space=pltpu.SMEM), WHOLE],
        out_specs=WHOLE,
        out_shape=VMEM((N * N * N * rows, LANES), jnp.int32),
        name="label_words",
        compiler_params=pltpu.CompilerParams(vmem_limit_bytes=8 << 20),
    )(pos, masked_ids)


def residual_kernel(chunk, f_ref, w0_ref, w1_ref, b0_ref, b1_ref, words_ref, r_ref, o_ref):
    f = f_ref[...]
    rows = f.shape[0]
    own = w0_ref.shape[0]
    words = words_ref[chunk * rows : (chunk + 1) * rows, :]
    for half, (w_ref, b_ref) in enumerate(((w0_ref, b0_ref), (w1_ref, b1_ref))):
        for s in range(0, own, SUB):
            logits = lax.dot_general(
                f, w_ref[s : s + SUB, :], (((1,), (1,)), ((), ())), preferred_element_type=jnp.float32
            )
            for g in range(0, SUB, LANES):
                at = half * own + s + g
                half_logits = logits[:, g : g + LANES] + b_ref[:, s + g : s + g + LANES]
                mark = jnp.int32(1 << (at // LANES) if at // LANES < 31 else -(1 << 31))
                offset = jnp.where((words & mark) != 0, -1.0, 1.0)
                r_ref[:, at : at + LANES] = (jnp.tanh(half_logits) + offset).astype(jnp.bfloat16)
    total = jnp.dot(r_ref[:, :own], w0_ref[...], preferred_element_type=jnp.float32)
    total = total + jnp.dot(r_ref[:, own:], w1_ref[...], preferred_element_type=jnp.float32)
    o_ref[...] = (total * 0.5).astype(o_ref.dtype)


def residual(chunk, f, w0, w1, b0, b1, words, out_type):
    rows, width = f.shape
    labels = 2 * w0.shape[0]
    return pl.pallas_call(
        functools.partial(residual_kernel, chunk),
        in_specs=[WHOLE] * 6,
        out_specs=[WHOLE, WHOLE],
        out_shape=[VMEM((rows, labels), jnp.bfloat16), VMEM((rows, width), out_type)],
        name="residual",
        cost_estimate=pl.CostEstimate(flops=4 * rows * labels * width, bytes_accessed=8 << 20, transcendentals=0),
        compiler_params=pltpu.CompilerParams(vmem_limit_bytes=12 << 20),
    )(vmem(f), vmem(w0), vmem(w1), vmem(b0), vmem(b1), vmem(words))


def weight_kernel(start, add, *refs):
    r_refs, f_refs, out_ref = refs[:N], refs[N : 2 * N], refs[-1]
    f = jnp.concatenate([ref[...] for ref in f_refs], axis=0)
    for s in range(0, out_ref.shape[0], WSUB):
        r = jnp.concatenate([ref[:, start + s : start + s + WSUB] for ref in r_refs], axis=0)
        total = lax.dot_general(r, f, (((0,), (0,)), ((), ())), preferred_element_type=jnp.float32)
        if add:
            total = total + refs[2 * N][s : s + WSUB, :].astype(jnp.float32)
        out_ref[s : s + WSUB, :] = total.astype(jnp.bfloat16)


def weight_product(rs, fs, start, count, other=None):
    rows, width = fs[0].shape
    extra = () if other is None else (vmem(other),)
    return pl.pallas_call(
        functools.partial(weight_kernel, start, other is not None),
        in_specs=[WHOLE] * (2 * N + len(extra)),
        out_specs=WHOLE,
        out_shape=VMEM((count, width), jnp.bfloat16),
        name="weight_product",
        cost_estimate=pl.CostEstimate(flops=2 * N * rows * count * width, bytes_accessed=4 << 20, transcendentals=0),
        compiler_params=pltpu.CompilerParams(vmem_limit_bytes=12 << 20),
    )(*[vmem(r) for r in rs], *[vmem(f) for f in fs], *extra)


def on_device(features, label_weight, label_bias, positive_ids, positive_counts):
    own, width = label_weight.shape
    rows = features.shape[0]
    me = lax.axis_index(AXES)
    core, z, x, y = me % 2, me // 2 % N, me // 8 % N, me // 32
    pos = jnp.stack([core, me // 2 * 2 * own, own, jnp.where(core == 0, x, y), jnp.where(core == 0, y, x), z])
    slots = jnp.arange(positive_ids.shape[1], dtype=jnp.int32)
    masked_ids = jnp.where(slots[None, :] < positive_counts[:, None], positive_ids, -1)

    f16 = features * jnp.bfloat16(0.5)
    f64 = jnp.concatenate([f16] + [fetch(f16, "first", k) for k in (1, 2, 3)], axis=0)
    f256 = jnp.concatenate([f64] + [fetch(f64, "second", k) for k in (1, 2, 3)], axis=0)
    fs = [f256] + [fetch(f256, "third", k) for k in (1, 2, 3)]

    b0 = (label_bias * 0.5).reshape(1, own)
    w0, w1, b1 = label_weight, swap(label_weight), swap(b0)
    words = label_words(pos, masked_ids, rows)

    rs, sums = [None] * N, None
    for k in (0, 1, 3, 2):
        rs[k], part = residual(k, fs[k], w0, w1, b0, b1, words, jnp.float32 if k == 0 else jnp.bfloat16)
        if k == 0:
            sums = part
        else:
            sums = sums + push(part, "third", k).astype(jnp.float32)

    half = own // 2
    others = [swap(weight_product(rs, fs, own + s, half)) for s in (0, half)]
    mine = [weight_product(rs, fs, s, half, other) for s, other in zip((0, half), others)]
    weight_grad = jnp.concatenate(mine, axis=0)

    for stage in ("second", "first"):
        count = sums.shape[0] // N
        sent = sums.astype(jnp.bfloat16)
        arrived = [push(sent[k * count : (k + 1) * count], stage, k) for k in (1, 2, 3)]
        sums = sums[:count]
        for part in arrived:
            sums = sums + part.astype(jnp.float32)
    return weight_grad, sums


def solution(mesh):
    split = P(AXES, None)
    return jax.shard_map(
        on_device,
        mesh=mesh,
        in_specs=(split, split, P(AXES), P(), P()),
        out_specs=(split, split),
        check_vma=False,
    )
```

time: 422 us -> 97.8 us (0.23)
  waiting for transfers between devices: 279 us -> 14.3 us
  other arithmetic: 58.2 us -> 4.5 us
  matrix products: 47.7 us -> 0 us
  Pallas kernels: 0 us -> 44 us
  starting transfers between devices: 0.08 us -> 29.9 us
  local copies, waits for them, and re-layouts: 19.8 us -> 3.27 us
  between operations: 14.1 us -> 0.94 us
    reduce_scatter x1 -> x0, waiting for transfers between devices: 210 us -> none  [on_device(): lax.psum_scatter(partial_grad, ('label', 'sub'), scatter_dimension=0, til...]
    all_gather x1 -> x0, waiting for transfers between devices: 68.3 us -> none  [on_device(): gathered = lax.all_gather(features, ('label', 'sub'), axis=0, tiled=True)]
    reduce_or x4 -> x0, other arithmetic: 57.1 us -> none  [step(): hits = jnp.any(masked_ids[:, :, None] == labels_here[None, None, :], axis=1)]
    dot_general x12 -> x0, matrix products: 47.7 us -> none  [the longest x4 18.5 us: step(): lax.dot_general(gathered, wblock, (((1,), (1,)), ((), ())), preferred_ele...]
    pallas_call x0 -> x9, Pallas kernels: none -> 44 us  [the longest x4 24.5 us: residual(): pl.pallas_call(functools.partial(residual_kernel, chunk), in_specs=[WHOLE...]
    ppermute x0 -> x22, starting transfers between devices: none -> 29.9 us  [the longest x9 18.3 us: fetch(): return lax.ppermute(x, AXES, shifted(stage, -k))]
    ppermute x0 -> x22, waiting for transfers between devices: none -> 14.3 us  [the longest x9 10.2 us: push(): return lax.ppermute(x, AXES, shifted(stage, k))]
    while x32 -> x0, local copies, waits for them, and re-layouts: 10.7 us -> none
  transfers between devices with their start and end apart: 2 -> 22, of which waited for: 2 -> 6; matrix products, arithmetic and copies ran while one was open for 1% -> 4% of each run, Pallas kernels for 0% -> 43%
where the time goes in v1:
time: 97.8 us; the launch traced here: 97 us
  Pallas kernels  44 us (45%)
  starting transfers between devices  29.9 us (31%)
  waiting for transfers between devices  14.3 us (15%)
  other arithmetic  4.5 us (5%)
  local copies, waits for them, and re-layouts  3.27 us (3%)
    pallas_call x4, Pallas kernels, residual(): pl.pallas_call(functools.partial(residual_kernel, chunk), in_specs=[WHOLE...  24.5 us
    ppermute x9, starting transfers between devices, fetch(): return lax.ppermute(x, AXES, shifted(stage, -k))  18.3 us
    pallas_call x1, Pallas kernels, label_words(): pl.pallas_call(functools.partial(words_kernel, rows), in_specs=[pl.BlockS...  12.2 us
    ppermute x9, starting transfers between devices, push(): return lax.ppermute(x, AXES, shifted(stage, k))  10.9 us
    ppermute x9, waiting for transfers between devices, push(): return lax.ppermute(x, AXES, shifted(stage, k))  10.2 us
    pallas_call x4, Pallas kernels, weight_product(): pl.pallas_call(functools.partial(weight_kernel, start, other is not None)...  7.31 us
    ppermute x9, waiting for transfers between devices, fetch(): return lax.ppermute(x, AXES, shifted(stage, -k))  4.13 us
    unnamed x10, local copies, waits for them, and re-layouts  3.14 us
  transfers between devices with their start and end apart: 22, of which 6 were waited for; matrix products, arithmetic and copies ran while one was open for 4% of the time, Pallas kernels for 43%

profile of v1, /device:TPU:0, one launch (start us, length us, event | category | flops | bytes accessed | tf_op | source)
XLA Modules:
  0.0 97.0 jit_solution(597515935334293770)
XLA Ops:
  0.6 0.1 collective-permute-start.6
  0.7 0.7 broadcast_multiply_fusion
  1.5 2.0 %collective-permute-start.2 = (bf16[16,768]{1,0:T(8,128)(2,1)S(1)}, bf16[16,768]{1,0:T(8,128)(2,1)S(1)}, u32[]{:S(2)}, u32[]{:S(2)}) collective-permute-start(bf16[16,768]{1,0:T(8,128)(2,1)S(1)} %get-tuple-element.28), channel_id=1, source_target_pairs={{0,2},{1,3},{2,4},{3,5},{4,6},{5,7},{6,0},{7,1},{8,10},{9,11},{10,... | collective-permute-start | bytes 73736 | tf_op jit(solution)/shard_map/ppermute | solution.py:37
  3.5 3.6 %collective-permute-start.1 = (bf16[16,768]{1,0:T(8,128)(2,1)S(1)}, bf16[16,768]{1,0:T(8,128)(2,1)S(1)}, u32[]{:S(2)}, u32[]{:S(2)}) collective-permute-start(bf16[16,768]{1,0:T(8,128)(2,1)S(1)} %get-tuple-element.28), channel_id=1, source_target_pairs={{0,4},{1,5},{2,6},{3,7},{4,0},{5,1},{6,2},{7,3},{8,12},{9,13},{10,... | collective-permute-start | bytes 73736 | tf_op jit(solution)/shard_map/ppermute | solution.py:37
  7.1 1.0 %collective-permute-start = (bf16[16,768]{1,0:T(8,128)(2,1)S(1)}, bf16[16,768]{1,0:T(8,128)(2,1)S(1)}, u32[]{:S(2)}, u32[]{:S(2)}) collective-permute-start(bf16[16,768]{1,0:T(8,128)(2,1)S(1)} %get-tuple-element.28), channel_id=1, source_target_pairs={{0,6},{1,7},{2,0},{3,1},{4,2},{5,3},{6,4},{7,5},{8,14},{9,15},{10,... | collective-permute-start | bytes 73736 | tf_op jit(solution)/shard_map/ppermute | solution.py:37
  8.1 0.7 broadcast_multiply_fusion.1
  8.8 0.0 collective-permute-start.7
  8.8 1.2 %copy.7 = s32[2048,16]{1,0:T(8,128)S(1)} copy(s32[2048,16]{0,1:T(8,128)} %param.8) | data formatting | bytes 262144 | tf_op args[3]
  10.0 0.0 collective-permute-done.1
  10.0 0.9 collective-permute-done
  10.9 1.6 %collective-permute-start.5 = (bf16[64,768]{1,0:T(8,128)(2,1)S(1)}, bf16[64,768]{1,0:T(8,128)(2,1)S(1)}, u32[]{:S(2)}, u32[]{:S(2)}) collective-permute-start(bf16[64,768]{1,0:T(8,128)(2,1)S(1)} %pad_maximum_fusion.1), channel_id=1, source_target_pairs={{0,32},{1,9},{2,34},{3,11},{4,36},{5,13},{6,38},{7,15},{8,40},{9,1... | collective-permute-start | bytes 294920 | tf_op jit(solution)/shard_map/ppermute | solution.py:37
  12.5 2.9 %collective-permute-start.4 = (bf16[64,768]{1,0:T(8,128)(2,1)S(1)}, bf16[64,768]{1,0:T(8,128)(2,1)S(1)}, u32[]{:S(2)}, u32[]{:S(2)}) collective-permute-start(bf16[64,768]{1,0:T(8,128)(2,1)S(1)} %pad_maximum_fusion.1), channel_id=1, source_target_pairs={{0,64},{1,17},{2,66},{3,19},{4,68},{5,21},{6,70},{7,23},{8,72},{9,... | collective-permute-start | bytes 294920 | tf_op jit(solution)/shard_map/ppermute | solution.py:37
  15.5 1.3 %collective-permute-start.3 = (bf16[64,768]{1,0:T(8,128)(2,1)S(1)}, bf16[64,768]{1,0:T(8,128)(2,1)S(1)}, u32[]{:S(2)}, u32[]{:S(2)}) collective-permute-start(bf16[64,768]{1,0:T(8,128)(2,1)S(1)} %pad_maximum_fusion.1), channel_id=1, source_target_pairs={{0,96},{1,25},{2,98},{3,27},{4,100},{5,29},{6,102},{7,31},{8,104},... | collective-permute-start | bytes 294920 | tf_op jit(solution)/shard_map/ppermute | solution.py:37
  16.8 3.3 %collective-permute-done.3 = bf16[64,768]{1,0:T(8,128)(2,1)S(1)} collective-permute-done((bf16[64,768]{1,0:T(8,128)(2,1)S(1)}, bf16[64,768]{1,0:T(8,128)(2,1)S(1)}, u32[]{:S(2)}, u32[]{:S(2)}) %collective-permute-start.3) | collective-permute-done | bytes 98336 | tf_op jit(solution)/shard_map/ppermute | solution.py:37
  20.1 1.6 %collective-permute-start.10 = (bf16[256,768]{1,0:T(8,128)(2,1)S(1)}, bf16[256,768]{1,0:T(8,128)(2,1)S(1)}, u32[]{:S(2)}, u32[]{:S(2)}) collective-permute-start(bf16[256,768]{1,0:T(8,128)(2,1)S(1)} %constant_dynamic-update-slice_fusion.f_ref.refs_4_), channel_id=1, source_target_pairs={{0,8},{1,33},{2,10},{3,35},{4,12},{5,37},{6,14},{7,39},{8,16},{9,4... | collective-permute-start | bytes 1179656 | tf_op jit(solution)/shard_map/ppermute | solution.py:37
  21.7 2.7 %collective-permute-start.9 = (bf16[256,768]{1,0:T(8,128)(2,1)S(1)}, bf16[256,768]{1,0:T(8,128)(2,1)S(1)}, u32[]{:S(2)}, u32[]{:S(2)}) collective-permute-start(bf16[256,768]{1,0:T(8,128)(2,1)S(1)} %constant_dynamic-update-slice_fusion.f_ref.refs_4_), channel_id=1, source_target_pairs={{0,16},{1,65},{2,18},{3,67},{4,20},{5,69},{6,22},{7,71},{8,24},{9,... | collective-permute-start | bytes 1179656 | tf_op jit(solution)/shard_map/ppermute | solution.py:37
  24.4 0.3 fusion.ids_ref
  24.8 0.1 stack.23.pos_ref
  24.9 12.2 %label_words.1.words_ref = s32[1024,128]{1,0:T(8,128)S(1)} custom-call(s32[6]{0:T(128)S(1)} %stack.23.pos_ref, s32[2048,16]{1,0:T(8,128)S(1)} %fusion.ids_ref), custom_call_target="tpu_custom_call" | custom-call | tf_op jit(solution)/shard_map/label_words/pallas_call | solution.py:74
  37.1 1.5 %collective-permute-start.8 = (bf16[256,768]{1,0:T(8,128)(2,1)S(1)}, bf16[256,768]{1,0:T(8,128)(2,1)S(1)}, u32[]{:S(2)}, u32[]{:S(2)}) collective-permute-start(bf16[256,768]{1,0:T(8,128)(2,1)S(1)} %constant_dynamic-update-slice_fusion.f_ref.refs_4_), channel_id=1, source_target_pairs={{0,24},{1,97},{2,26},{3,99},{4,28},{5,101},{6,30},{7,103},{8,0},{9... | collective-permute-start | bytes 1179656 | tf_op jit(solution)/shard_map/ppermute | solution.py:37
  38.6 0.0 copy-start
  38.6 1.9 %copy-done = bf16[2048,768]{1,0:T(8,128)(2,1)S(1)} copy-done((bf16[2048,768]{1,0:T(8,128)(2,1)S(1)}, bf16[2048,768]{1,0:T(8,128)(2,1)}, u32[]{:S(2)}) %copy-start) | copy-done | bytes 3145752
  40.5 6.1 %residual.7 = (bf16[256,4096]{1,0:T(8,128)(2,1)S(1)}, bf16[256,768]{1,0:T(8,128)(2,1)S(1)}) custom-call(bf16[256,768]{1,0:T(8,128)(2,1)S(1)} %collective-permute-done.10.f_ref.refs_7_, bf16[2048,768]{1,0:T(8,128)(2,1)S(1)} %copy-done, bf16[2048,768]{1,0:T(8,128)(2,1)} %collective-permute-done.6.w1_ref, f32[1,2048]{1,0:T(1,128)S(1)} %bitcast.7, ...), custom_call_target="tpu_custom_call" | custom-call | flops 3221225472 | bytes 8388608 | tf_op jit(solution)/shard_map/residual/pallas_call | solution.py:108
  46.6 0.1 collective-permute-start.14
  46.7 6.1 %residual.6 = (bf16[256,4096]{1,0:T(8,128)(2,1)S(1)}, bf16[256,768]{1,0:T(8,128)(2,1)S(1)}) custom-call(bf16[256,768]{1,0:T(8,128)(2,1)S(1)} %collective-permute-done.9.f_ref.refs_6_, bf16[2048,768]{1,0:T(8,128)(2,1)S(1)} %copy-done, bf16[2048,768]{1,0:T(8,128)(2,1)} %collective-permute-done.6.w1_ref, f32[1,2048]{1,0:T(1,128)S(1)} %bitcast.8, ...), custom_call_target="tpu_custom_call" | custom-call | flops 3221225472 | bytes 8388608 | tf_op jit(solution)/shard_map/residual/pallas_call | solution.py:108
  52.9 2.9 %collective-permute-start.15 = (bf16[256,768]{1,0:T(8,128)(2,1)S(1)}, bf16[256,768]{1,0:T(8,128)(2,1)S(1)}, u32[]{:S(2)}, u32[]{:S(2)}) collective-permute-start(bf16[256,768]{1,0:T(8,128)(2,1)S(1)} %get-tuple-element.17), channel_id=1, source_target_pairs={{0,16},{1,65},{2,18},{3,67},{4,20},{5,69},{6,22},{7,71},{8,24},{9,... | collective-permute-start | bytes 1179656 | tf_op jit(solution)/shard_map/ppermute | solution.py:41
  55.8 6.1 %residual.5 = (bf16[256,4096]{1,0:T(8,128)(2,1)S(1)}, bf16[256,768]{1,0:T(8,128)(2,1)S(1)}) custom-call(bf16[256,768]{1,0:T(8,128)(2,1)S(1)} %collective-permute-done.8.f_ref.refs_5_, bf16[2048,768]{1,0:T(8,128)(2,1)S(1)} %copy-done, bf16[2048,768]{1,0:T(8,128)(2,1)} %collective-permute-done.6.w1_ref, f32[1,2048]{1,0:T(1,128)S(1)} %bitcast.9, ...), custom_call_target="tpu_custom_call" | custom-call | flops 3221225472 | bytes 8388608 | tf_op jit(solution)/shard_map/residual/pallas_call | solution.py:108
  61.9 0.1 collective-permute-start.13
  62.0 6.1 %residual.4 = (bf16[256,4096]{1,0:T(8,128)(2,1)S(1)}, f32[256,768]{1,0:T(8,128)S(1)}) custom-call(bf16[256,768]{1,0:T(8,128)(2,1)S(1)} %constant_dynamic-update-slice_fusion.f_ref.refs_4_, bf16[2048,768]{1,0:T(8,128)(2,1)S(1)} %copy-done, bf16[2048,768]{1,0:T(8,128)(2,1)} %collective-permute-done.6.w1_ref, f32[1,2048]{1,0:T(1,128)S(1)} %bitcast.10, ...), custom_call_target="tpu_custom_call" | custom-call | flops 3221225472 | bytes 8388608 | tf_op jit(solution)/shard_map/residual/pallas_call | solution.py:108
  68.1 1.8 %weight_product.4 = bf16[1024,768]{1,0:T(8,128)(2,1)S(1)} custom-call(bf16[256,4096]{1,0:T(8,128)(2,1)S(1)} %get-tuple-element.10.refs_0_, bf16[256,4096]{1,0:T(8,128)(2,1)S(1)} %get-tuple-element.11.refs_1_, bf16[256,4096]{1,0:T(8,128)(2,1)S(1)} %get-tuple-element.12.refs_2_, bf16[256,4096]{1,0:T(8,128)(2,1)S(1)} %get-tuple-element.13.refs_3_, ...), custom_call_target="tpu_custom_call" | custom-call | flops 1610612736 | bytes 4194304 | tf_op jit(solution)/shard_map/weight_product/pallas_call | solution.py:133
  69.9 0.1 collective-permute-start.11
  70.0 1.8 %weight_product.6 = bf16[1024,768]{1,0:T(8,128)(2,1)S(1)} custom-call(bf16[256,4096]{1,0:T(8,128)(2,1)S(1)} %get-tuple-element.10.refs_0_, bf16[256,4096]{1,0:T(8,128)(2,1)S(1)} %get-tuple-element.11.refs_1_, bf16[256,4096]{1,0:T(8,128)(2,1)S(1)} %get-tuple-element.12.refs_2_, bf16[256,4096]{1,0:T(8,128)(2,1)S(1)} %get-tuple-element.13.refs_3_, ...), custom_call_target="tpu_custom_call" | custom-call | flops 1610612736 | bytes 4194304 | tf_op jit(solution)/shard_map/weight_product/pallas_call | solution.py:133
  71.9 0.6 collective-permute-start.12
  72.4 0.2 fusion.7
  72.6 0.8 collective-permute-start.16
  73.4 2.5 %collective-permute-start.18 = (bf16[64,768]{1,0:T(8,128)(2,1)S(1)}, bf16[64,768]{1,0:T(8,128)(2,1)S(1)}, u32[]{:S(2)}, u32[]{:S(2)}) collective-permute-start(bf16[64,768]{1,0:T(8,128)(2,1)S(1)} %get-tuple-element.23), channel_id=1, source_target_pairs={{0,96},{1,25},{2,98},{3,27},{4,100},{5,29},{6,102},{7,31},{8,104},... | collective-permute-start | bytes 294920 | tf_op jit(solution)/shard_map/ppermute | solution.py:41
  76.0 0.8 collective-permute-start.17
  76.7 1.8 %collective-permute-done.16 = bf16[64,768]{1,0:T(8,128)(2,1)S(1)} collective-permute-done((bf16[64,768]{1,0:T(8,128)(2,1)S(1)}, bf16[64,768]{1,0:T(8,128)(2,1)S(1)}, u32[]{:S(2)}, u32[]{:S(2)}) %collective-permute-start.16) | collective-permute-done | bytes 98336 | tf_op jit(solution)/shard_map/ppermute | solution.py:41
  78.5 3.5 %collective-permute-done.17 = bf16[64,768]{1,0:T(8,128)(2,1)S(1)} collective-permute-done((bf16[64,768]{1,0:T(8,128)(2,1)S(1)}, bf16[64,768]{1,0:T(8,128)(2,1)S(1)}, u32[]{:S(2)}, u32[]{:S(2)}) %collective-permute-start.17) | collective-permute-done | bytes 98336 | tf_op jit(solution)/shard_map/ppermute | solution.py:41
  82.1 0.2 collective-permute-start.19
  82.4 3.1 %collective-permute-start.21 = (bf16[16,768]{1,0:T(8,128)(2,1)S(1)}, bf16[16,768]{1,0:T(8,128)(2,1)S(1)}, u32[]{:S(2)}, u32[]{:S(2)}) collective-permute-start(bf16[16,768]{1,0:T(8,128)(2,1)S(1)} %get-tuple-element.26), channel_id=1, source_target_pairs={{0,6},{1,7},{2,0},{3,1},{4,2},{5,3},{6,4},{7,5},{8,14},{9,15},{10,... | collective-permute-start | bytes 73736 | tf_op jit(solution)/shard_map/ppermute | solution.py:41
  85.4 0.5 collective-permute-start.20
  85.9 1.3 %collective-permute-done.19 = bf16[16,768]{1,0:T(8,128)(2,1)S(1)} collective-permute-done((bf16[16,768]{1,0:T(8,128)(2,1)S(1)}, bf16[16,768]{1,0:T(8,128)(2,1)S(1)}, u32[]{:S(2)}, u32[]{:S(2)}) %collective-permute-start.19) | collective-permute-done | bytes 24608 | tf_op jit(solution)/shard_map/ppermute | solution.py:41
  87.2 3.5 %collective-permute-done.20 = bf16[16,768]{1,0:T(8,128)(2,1)S(1)} collective-permute-done((bf16[16,768]{1,0:T(8,128)(2,1)S(1)}, bf16[16,768]{1,0:T(8,128)(2,1)S(1)}, u32[]{:S(2)}, u32[]{:S(2)}) %collective-permute-start.20) | collective-permute-done | bytes 24608 | tf_op jit(solution)/shard_map/ppermute | solution.py:41
  90.8 0.6 fusion.4
  91.4 1.8 %weight_product.5 = bf16[1024,768]{1,0:T(8,128)(2,1)S(1)} custom-call(bf16[256,4096]{1,0:T(8,128)(2,1)S(1)} %get-tuple-element.10.refs_0_, bf16[256,4096]{1,0:T(8,128)(2,1)S(1)} %get-tuple-element.11.refs_1_, bf16[256,4096]{1,0:T(8,128)(2,1)S(1)} %get-tuple-element.12.refs_2_, bf16[256,4096]{1,0:T(8,128)(2,1)S(1)} %get-tuple-element.13.refs_3_, ...), custom_call_target="tpu_custom_call" | custom-call | flops 1610612736 | bytes 4194304 | tf_op jit(solution)/shard_map/weight_product/pallas_call | solution.py:133
  93.3 1.8 %weight_product.7 = bf16[1024,768]{1,0:T(8,128)(2,1)S(1)} custom-call(bf16[256,4096]{1,0:T(8,128)(2,1)S(1)} %get-tuple-element.10.refs_0_, bf16[256,4096]{1,0:T(8,128)(2,1)S(1)} %get-tuple-element.11.refs_1_, bf16[256,4096]{1,0:T(8,128)(2,1)S(1)} %get-tuple-element.12.refs_2_, bf16[256,4096]{1,0:T(8,128)(2,1)S(1)} %get-tuple-element.13.refs_3_, ...), custom_call_target="tpu_custom_call" | custom-call | flops 1610612736 | bytes 4194304 | tf_op jit(solution)/shard_map/weight_product/pallas_call | solution.py:133
  95.1 1.9 %pad_maximum_fusion = bf16[2048,768]{1,0:T(8,128)(2,1)} fusion(bf16[1024,768]{1,0:T(8,128)(2,1)S(1)} %weight_product.7, bf16[1024,768]{1,0:T(8,128)(2,1)S(1)} %weight_product.5), kind=kLoop, calls=%fused_computation | loop fusion | flops 6291456 | bytes 6291456 | tf_op jit(solution)/shard_map/concatenate | solution.py:173
  (27 shorter events, 0.2 us)
Async XLA Ops:
  0.6 23.8 %copy-start.1 = (s32[2048]{0:T(1024)S(1)}, s32[2048]{0:T(1024)}, u32[]{:S(2)}) copy-start(s32[2048]{0:T(1024)} %param.9) | copy-start | bytes 24580
  0.6 38.0 %collective-permute-start.6 = (bf16[2048,768]{1,0:T(8,128)(2,1)}, bf16[2048,768]{1,0:T(8,128)(2,1)}, u32[]{:S(2)}, u32[]{:S(2)}) collective-permute-start(bf16[2048,768]{1,0:T(8,128)(2,1)} %w0_ref.7), channel_id=1, source_target_pairs={{0,1},{1,0},{2,3},{3,2},{4,5},{5,4},{6,7},{7,6},{8,9},{9,8},{10,11... | collective-permute-start | bytes 9437192 | tf_op jit(solution)/shard_map/ppermute | solution.py:45
  1.5 8.5 %collective-permute-start.2 = (bf16[16,768]{1,0:T(8,128)(2,1)S(1)}, bf16[16,768]{1,0:T(8,128)(2,1)S(1)}, u32[]{:S(2)}, u32[]{:S(2)}) collective-permute-start(bf16[16,768]{1,0:T(8,128)(2,1)S(1)} %get-tuple-element.28), channel_id=1, source_target_pairs={{0,2},{1,3},{2,4},{3,5},{4,6},{5,7},{6,0},{7,1},{8,10},{9,11},{10,... | collective-permute-start | bytes 73736 | tf_op jit(solution)/shard_map/ppermute | solution.py:37
  3.5 6.5 %collective-permute-start.1 = (bf16[16,768]{1,0:T(8,128)(2,1)S(1)}, bf16[16,768]{1,0:T(8,128)(2,1)S(1)}, u32[]{:S(2)}, u32[]{:S(2)}) collective-permute-start(bf16[16,768]{1,0:T(8,128)(2,1)S(1)} %get-tuple-element.28), channel_id=1, source_target_pairs={{0,4},{1,5},{2,6},{3,7},{4,0},{5,1},{6,2},{7,3},{8,12},{9,13},{10,... | collective-permute-start | bytes 73736 | tf_op jit(solution)/shard_map/ppermute | solution.py:37
  7.1 3.8 %collective-permute-start = (bf16[16,768]{1,0:T(8,128)(2,1)S(1)}, bf16[16,768]{1,0:T(8,128)(2,1)S(1)}, u32[]{:S(2)}, u32[]{:S(2)}) collective-permute-start(bf16[16,768]{1,0:T(8,128)(2,1)S(1)} %get-tuple-element.28), channel_id=1, source_target_pairs={{0,6},{1,7},{2,0},{3,1},{4,2},{5,3},{6,4},{7,5},{8,14},{9,15},{10,... | collective-permute-start | bytes 73736 | tf_op jit(solution)/shard_map/ppermute | solution.py:37
  8.8 29.8 %collective-permute-start.7 = (f32[1,2048]{1,0:T(1,128)S(1)}, f32[1,2048]{1,0:T(1,128)S(1)}, u32[]{:S(2)}, u32[]{:S(2)}) collective-permute-start(f32[1,2048]{1,0:T(1,128)S(1)} %bitcast.6), channel_id=1, source_target_pairs={{0,1},{1,0},{2,3},{3,2},{4,5},{5,4},{6,7},{7,6},{8,9},{9,8},{10,11... | collective-permute-start | bytes 24584 | tf_op jit(solution)/shard_map/ppermute | solution.py:45
  10.9 9.2 %collective-permute-start.5 = (bf16[64,768]{1,0:T(8,128)(2,1)S(1)}, bf16[64,768]{1,0:T(8,128)(2,1)S(1)}, u32[]{:S(2)}, u32[]{:S(2)}) collective-permute-start(bf16[64,768]{1,0:T(8,128)(2,1)S(1)} %pad_maximum_fusion.1), channel_id=1, source_target_pairs={{0,32},{1,9},{2,34},{3,11},{4,36},{5,13},{6,38},{7,15},{8,40},{9,1... | collective-permute-start | bytes 294920 | tf_op jit(solution)/shard_map/ppermute | solution.py:37
  12.5 7.5 %collective-permute-start.4 = (bf16[64,768]{1,0:T(8,128)(2,1)S(1)}, bf16[64,768]{1,0:T(8,128)(2,1)S(1)}, u32[]{:S(2)}, u32[]{:S(2)}) collective-permute-start(bf16[64,768]{1,0:T(8,128)(2,1)S(1)} %pad_maximum_fusion.1), channel_id=1, source_target_pairs={{0,64},{1,17},{2,66},{3,19},{4,68},{5,21},{6,70},{7,23},{8,72},{9,... | collective-permute-start | bytes 294920 | tf_op jit(solution)/shard_map/ppermute | solution.py:37
  15.5 4.6 %collective-permute-start.3 = (bf16[64,768]{1,0:T(8,128)(2,1)S(1)}, bf16[64,768]{1,0:T(8,128)(2,1)S(1)}, u32[]{:S(2)}, u32[]{:S(2)}) collective-permute-start(bf16[64,768]{1,0:T(8,128)(2,1)S(1)} %pad_maximum_fusion.1), channel_id=1, source_target_pairs={{0,96},{1,25},{2,98},{3,27},{4,100},{5,29},{6,102},{7,31},{8,104},... | collective-permute-start | bytes 294920 | tf_op jit(solution)/shard_map/ppermute | solution.py:37
  20.1 18.5 %collective-permute-start.10 = (bf16[256,768]{1,0:T(8,128)(2,1)S(1)}, bf16[256,768]{1,0:T(8,128)(2,1)S(1)}, u32[]{:S(2)}, u32[]{:S(2)}) collective-permute-start(bf16[256,768]{1,0:T(8,128)(2,1)S(1)} %constant_dynamic-update-slice_fusion.f_ref.refs_4_), channel_id=1, source_target_pairs={{0,8},{1,33},{2,10},{3,35},{4,12},{5,37},{6,14},{7,39},{8,16},{9,4... | collective-permute-start | bytes 1179656 | tf_op jit(solution)/shard_map/ppermute | solution.py:37
  21.7 25.0 %collective-permute-start.9 = (bf16[256,768]{1,0:T(8,128)(2,1)S(1)}, bf16[256,768]{1,0:T(8,128)(2,1)S(1)}, u32[]{:S(2)}, u32[]{:S(2)}) collective-permute-start(bf16[256,768]{1,0:T(8,128)(2,1)S(1)} %constant_dynamic-update-slice_fusion.f_ref.refs_4_), channel_id=1, source_target_pairs={{0,16},{1,65},{2,18},{3,67},{4,20},{5,69},{6,22},{7,71},{8,24},{9,... | collective-permute-start | bytes 1179656 | tf_op jit(solution)/shard_map/ppermute | solution.py:37
  37.1 18.7 %collective-permute-start.8 = (bf16[256,768]{1,0:T(8,128)(2,1)S(1)}, bf16[256,768]{1,0:T(8,128)(2,1)S(1)}, u32[]{:S(2)}, u32[]{:S(2)}) collective-permute-start(bf16[256,768]{1,0:T(8,128)(2,1)S(1)} %constant_dynamic-update-slice_fusion.f_ref.refs_4_), channel_id=1, source_target_pairs={{0,24},{1,97},{2,26},{3,99},{4,28},{5,101},{6,30},{7,103},{8,0},{9... | collective-permute-start | bytes 1179656 | tf_op jit(solution)/shard_map/ppermute | solution.py:37
  38.6 1.9 %copy-start = (bf16[2048,768]{1,0:T(8,128)(2,1)S(1)}, bf16[2048,768]{1,0:T(8,128)(2,1)}, u32[]{:S(2)}) copy-start(bf16[2048,768]{1,0:T(8,128)(2,1)} %w0_ref.7) | copy-start | bytes 9437188
  46.6 25.8 %collective-permute-start.14 = (bf16[256,768]{1,0:T(8,128)(2,1)S(1)}, bf16[256,768]{1,0:T(8,128)(2,1)S(1)}, u32[]{:S(2)}, u32[]{:S(2)}) collective-permute-start(bf16[256,768]{1,0:T(8,128)(2,1)S(1)} %get-tuple-element.16), channel_id=1, source_target_pairs={{0,24},{1,97},{2,26},{3,99},{4,28},{5,101},{6,30},{7,103},{8,0},{9... | collective-permute-start | bytes 1179656 | tf_op jit(solution)/shard_map/ppermute | solution.py:41
  52.9 19.6 %collective-permute-start.15 = (bf16[256,768]{1,0:T(8,128)(2,1)S(1)}, bf16[256,768]{1,0:T(8,128)(2,1)S(1)}, u32[]{:S(2)}, u32[]{:S(2)}) collective-permute-start(bf16[256,768]{1,0:T(8,128)(2,1)S(1)} %get-tuple-element.17), channel_id=1, source_target_pairs={{0,16},{1,65},{2,18},{3,67},{4,20},{5,69},{6,22},{7,71},{8,24},{9,... | collective-permute-start | bytes 1179656 | tf_op jit(solution)/shard_map/ppermute | solution.py:41
  61.9 10.6 %collective-permute-start.13 = (bf16[256,768]{1,0:T(8,128)(2,1)S(1)}, bf16[256,768]{1,0:T(8,128)(2,1)S(1)}, u32[]{:S(2)}, u32[]{:S(2)}) collective-permute-start(bf16[256,768]{1,0:T(8,128)(2,1)S(1)} %get-tuple-element.15), channel_id=1, source_target_pairs={{0,8},{1,33},{2,10},{3,35},{4,12},{5,37},{6,14},{7,39},{8,16},{9,4... | collective-permute-start | bytes 1179656 | tf_op jit(solution)/shard_map/ppermute | solution.py:41
  69.9 21.5 %collective-permute-start.11 = (bf16[1024,768]{1,0:T(8,128)(2,1)S(1)}, bf16[1024,768]{1,0:T(8,128)(2,1)S(1)}, u32[]{:S(2)}, u32[]{:S(2)}) collective-permute-start(bf16[1024,768]{1,0:T(8,128)(2,1)S(1)} %weight_product.4), channel_id=1, source_target_pairs={{0,1},{1,0},{2,3},{3,2},{4,5},{5,4},{6,7},{7,6},{8,9},{9,8},{10,11... | collective-permute-start | bytes 4718600 | tf_op jit(solution)/shard_map/ppermute | solution.py:45
  71.9 21.4 %collective-permute-start.12 = (bf16[1024,768]{1,0:T(8,128)(2,1)S(1)}, bf16[1024,768]{1,0:T(8,128)(2,1)S(1)}, u32[]{:S(2)}, u32[]{:S(2)}) collective-permute-start(bf16[1024,768]{1,0:T(8,128)(2,1)S(1)} %weight_product.6), channel_id=1, source_target_pairs={{0,1},{1,0},{2,3},{3,2},{4,5},{5,4},{6,7},{7,6},{8,9},{9,8},{10,11... | collective-permute-start | bytes 4718600 | tf_op jit(solution)/shard_map/ppermute | solution.py:45
  72.6 5.9 %collective-permute-start.16 = (bf16[64,768]{1,0:T(8,128)(2,1)S(1)}, bf16[64,768]{1,0:T(8,128)(2,1)S(1)}, u32[]{:S(2)}, u32[]{:S(2)}) collective-permute-start(bf16[64,768]{1,0:T(8,128)(2,1)S(1)} %get-tuple-element.22), channel_id=1, source_target_pairs={{0,32},{1,9},{2,34},{3,11},{4,36},{5,13},{6,38},{7,15},{8,40},{9,1... | collective-permute-start | bytes 294920 | tf_op jit(solution)/shard_map/ppermute | solution.py:41
  73.4 5.1 %collective-permute-start.18 = (bf16[64,768]{1,0:T(8,128)(2,1)S(1)}, bf16[64,768]{1,0:T(8,128)(2,1)S(1)}, u32[]{:S(2)}, u32[]{:S(2)}) collective-permute-start(bf16[64,768]{1,0:T(8,128)(2,1)S(1)} %get-tuple-element.23), channel_id=1, source_target_pairs={{0,96},{1,25},{2,98},{3,27},{4,100},{5,29},{6,102},{7,31},{8,104},... | collective-permute-start | bytes 294920 | tf_op jit(solution)/shard_map/ppermute | solution.py:41
  76.0 6.1 %collective-permute-start.17 = (bf16[64,768]{1,0:T(8,128)(2,1)S(1)}, bf16[64,768]{1,0:T(8,128)(2,1)S(1)}, u32[]{:S(2)}, u32[]{:S(2)}) collective-permute-start(bf16[64,768]{1,0:T(8,128)(2,1)S(1)} %get-tuple-element.24), channel_id=1, source_target_pairs={{0,64},{1,17},{2,66},{3,19},{4,68},{5,21},{6,70},{7,23},{8,72},{9,... | collective-permute-start | bytes 294920 | tf_op jit(solution)/shard_map/ppermute | solution.py:41
  82.1 5.1 %collective-permute-start.19 = (bf16[16,768]{1,0:T(8,128)(2,1)S(1)}, bf16[16,768]{1,0:T(8,128)(2,1)S(1)}, u32[]{:S(2)}, u32[]{:S(2)}) collective-permute-start(bf16[16,768]{1,0:T(8,128)(2,1)S(1)} %get-tuple-element.25), channel_id=1, source_target_pairs={{0,2},{1,3},{2,4},{3,5},{4,6},{5,7},{6,0},{7,1},{8,10},{9,11},{10,... | collective-permute-start | bytes 73736 | tf_op jit(solution)/shard_map/ppermute | solution.py:41
  82.4 4.9 %collective-permute-start.21 = (bf16[16,768]{1,0:T(8,128)(2,1)S(1)}, bf16[16,768]{1,0:T(8,128)(2,1)S(1)}, u32[]{:S(2)}, u32[]{:S(2)}) collective-permute-start(bf16[16,768]{1,0:T(8,128)(2,1)S(1)} %get-tuple-element.26), channel_id=1, source_target_pairs={{0,6},{1,7},{2,0},{3,1},{4,2},{5,3},{6,4},{7,5},{8,14},{9,15},{10,... | collective-permute-start | bytes 73736 | tf_op jit(solution)/shard_map/ppermute | solution.py:41
  85.4 5.3 %collective-permute-start.20 = (bf16[16,768]{1,0:T(8,128)(2,1)S(1)}, bf16[16,768]{1,0:T(8,128)(2,1)S(1)}, u32[]{:S(2)}, u32[]{:S(2)}) collective-permute-start(bf16[16,768]{1,0:T(8,128)(2,1)S(1)} %get-tuple-element.27), channel_id=1, source_target_pairs={{0,4},{1,5},{2,6},{3,7},{4,0},{5,1},{6,2},{7,3},{8,12},{9,13},{10,... | collective-permute-start | bytes 73736 | tf_op jit(solution)/shard_map/ppermute | solution.py:41

commit v2 on v1

v2 whole, which is shorter than its diff:
```python
import functools

import jax
import jax.numpy as jnp
from jax import lax
from jax.experimental import pallas as pl
from jax.experimental.pallas import tpu as pltpu
from jax.sharding import PartitionSpec as P

AXES = ("label", "sub")
N = 4
STRIDE = {"y": 32, "x": 8, "z": 2}
LANES = 128
SUB = 1024
WSUB = 512
VMEM = pltpu.VMEM
WHOLE = pl.BlockSpec(memory_space=VMEM)
SCALARS = pl.BlockSpec(memory_space=pltpu.SMEM)
ORDER = pl.BlockSpec(memory_space=pl.ANY)
STAYS = pl.BlockSpec(memory_space=pltpu.HBM)


def vmem(x):
    return pltpu.with_memory_space_constraint(x, VMEM)


def hbm(x):
    return pltpu.with_memory_space_constraint(x, pltpu.HBM)


def params(mebibytes):
    return pltpu.CompilerParams(vmem_limit_bytes=mebibytes << 20)


def cost(flops):
    return pl.CostEstimate(flops=flops // 8, bytes_accessed=0, transcendentals=0)


STAGES = {"first": ("z", "z"), "second": ("y", "x"), "third": ("x", "y")}


def shifted(stage, k):
    pairs = []
    for d in range(2 * N * N * N):
        step = STRIDE[STAGES[stage][d % 2]]
        at = d // step % N
        pairs.append((d, d + ((at + k) % N - at) * step))
    return pairs


def fetch(x, stage, k):
    return lax.ppermute(x, AXES, shifted(stage, -k))


def push(x, stage, k):
    return lax.ppermute(x, AXES, shifted(stage, k))


def swap(x):
    return lax.ppermute(x, AXES, [(d, d ^ 1) for d in range(2 * N * N * N)])


def prepare_kernel(piece, pos_ref, b1_ref, w_ref, ids_hbm, counts_hbm, b0_hbm, *refs):
    w_out, words_out, half_out, ids_ref, counts_ref, b0_ref, sems = refs[-7:]
    pairs = ((ids_hbm, ids_ref), (counts_hbm, counts_ref), (b0_hbm, b0_ref), (w_ref, w_out))
    copies = [pltpu.make_async_copy(src, dst, sems.at[i]) for i, (src, dst) in enumerate(pairs)]
    for copy in copies:
        copy.start()
    copies[0].wait()
    copies[1].wait()
    core, base, own = pos_ref[0], pos_ref[1], pos_ref[2]
    slots, queries = ids_ref.shape
    row = lax.broadcasted_iota(jnp.int32, (8, LANES), 0)
    slot = lax.broadcasted_iota(jnp.int32, (slots, LANES), 0)
    lane = lax.broadcasted_iota(jnp.int32, (slots, LANES), 1)
    kept = (lane // piece) % 2 == core
    shift = jnp.where(core == 0, piece, LANES - piece)

    def packed(ref, q):
        other = pltpu.roll(jnp.broadcast_to(ref[:, q + LANES : q + 2 * LANES], (slots, LANES)), shift, 1)
        return jnp.where(kept, jnp.broadcast_to(ref[:, q : q + LANES], (slots, LANES)), other)

    for q in range(0, queries, 2 * LANES):
        rel = packed(ids_ref, q) - base
        valid = jnp.logical_and(rel >= 0, rel < 2 * own)
        valid = jnp.logical_and(valid, slot < packed(counts_ref, q))
        rel = jnp.where(valid, rel, 0) ^ (core * own)
        bit = jnp.where(valid, lax.shift_left(jnp.ones_like(rel), rel >> 7), 0)
        low = rel & (LANES - 1)
        parts = []
        for g in range(0, LANES, 8):
            word = jnp.zeros((8, LANES), jnp.int32)
            for j in range(slots):
                word = word | jnp.where(low[j : j + 1, :] == row + g, bit[j : j + 1, :], 0)
            parts.append(word)
        words_out[q // 2 : q // 2 + LANES, :] = jnp.concatenate(parts, axis=0).T
    copies[2].wait()
    half_out[...] = 0.5 * jnp.concatenate([b0_ref[...], b1_ref[...]], axis=1)
    copies[3].wait()


def prepare(piece, pos, w, ids, counts, b0, b1, after=()):
    return pl.pallas_call(
        functools.partial(prepare_kernel, piece),
        in_specs=[SCALARS, WHOLE] + [STAYS] * 4 + [ORDER] * len(after),
        out_specs=[WHOLE] * 3,
        out_shape=[
            VMEM(w.shape, w.dtype),
            VMEM((ids.shape[1] // 2, LANES), jnp.int32),
            VMEM((1, 2 * b0.shape[1]), jnp.float32),
        ],
        scratch_shapes=[
            VMEM(ids.shape, ids.dtype),
            VMEM(counts.shape, counts.dtype),
            VMEM(b0.shape, b0.dtype),
            pltpu.SemaphoreType.DMA((4,)),
        ],
        name="prepare",
        cost_estimate=cost(0),
        compiler_params=params(8),
    )(pos, b1, *[hbm(x) for x in (w, ids, counts, b0)], *after)


def load_kernel(x_ref, *refs):
    refs[-1][...] = x_ref[...]


def load(x, after):
    return pl.pallas_call(
        load_kernel,
        in_specs=[WHOLE] + [ORDER] * len(after),
        out_specs=WHOLE,
        out_shape=VMEM(x.shape, x.dtype),
        name="load",
        cost_estimate=cost(0),
        compiler_params=params(4),
    )(hbm(x), *after)


def join_kernel(count, factor, *refs):
    refs[-1][...] = jnp.concatenate([ref[...] for ref in refs[:count]], axis=0) * jnp.bfloat16(factor)


def join(parts, factor=1.0, after=()):
    rows, width = parts[0].shape
    return pl.pallas_call(
        functools.partial(join_kernel, len(parts), factor),
        in_specs=[WHOLE] * len(parts) + [ORDER] * len(after),
        out_specs=WHOLE,
        out_shape=VMEM((len(parts) * rows, width), parts[0].dtype),
        name="join",
        cost_estimate=cost(0),
        compiler_params=params(4),
    )(*[vmem(x) for x in parts], *after)


def residual_kernel(chunk, piece, again, pos_ref, f_ref, w0_ref, w1_ref, b_ref, words_ref, *refs):
    r_ref, o_ref = refs[-3:-1] if again else refs[-2:]
    f = f_ref[...]
    if again:
        refs[-1][...] = f
    own = w0_ref.shape[0]
    core, third, second, first = pos_ref[0], pos_ref[3], pos_ref[4], pos_ref[5]
    stride3 = jnp.where(core == 0, STRIDE["x"], STRIDE["y"]) // 2
    stride2 = jnp.where(core == 0, STRIDE["y"], STRIDE["x"]) // 2
    words = []
    for a in range(N):
        for b in range(N):
            chip = (third + chunk) % N * stride3 + (second + a) % N * stride2 + (first + b) % N
            near = chip % 8 < 4
            place = chip // 8 * 8 + chip % 4 * 2 + jnp.where(near, core, 1 - core)
            words.append(words_ref[pl.ds(pl.multiple_of(place * piece, piece), piece), :])
    words = jnp.concatenate(words, axis=0)
    for half, w_ref in enumerate((w0_ref, w1_ref)):
        for s in range(0, own, SUB):
            logits = lax.dot_general(
                f, w_ref[s : s + SUB, :], (((1,), (1,)), ((), ())), preferred_element_type=jnp.float32
            )
            for g in range(0, SUB, LANES):
                at = half * own + s + g
                half_logits = logits[:, g : g + LANES] + b_ref[:, at : at + LANES]
                mark = jnp.int32(1 << (at // LANES) if at // LANES < 31 else -(1 << 31))
                offset = jnp.where((words & mark) != 0, -1.0, 1.0)
                r_ref[:, at : at + LANES] = (jnp.tanh(half_logits) + offset).astype(jnp.bfloat16)
    w = jnp.concatenate([w0_ref[...], w1_ref[...]], axis=0)
    total = jnp.dot(r_ref[...], w, preferred_element_type=jnp.float32)
    o_ref[...] = (total * 0.5).astype(o_ref.dtype)


def residual(chunk, piece, pos, f, w0, w1, b, words, out_type, after=(), again=False):
    rows, width = f.shape
    labels = 2 * w0.shape[0]
    return pl.pallas_call(
        functools.partial(residual_kernel, chunk, piece, again),
        in_specs=[SCALARS] + [WHOLE] * 5 + [ORDER] * len(after),
        out_specs=[WHOLE] * (3 if again else 2),
        out_shape=[VMEM((rows, labels), jnp.bfloat16), VMEM((rows, width), out_type)] + [VMEM(f.shape, f.dtype)] * again,
        name="residual",
        cost_estimate=cost(4 * rows * labels),
        compiler_params=params(12),
    )(pos, *[vmem(x) for x in (f, w0, w1, b, words)], *after)


def weight_partial_kernel(start, *refs):
    r_refs, f_refs, out_ref = refs[:N], refs[N : 2 * N], refs[-1]
    f = jnp.concatenate([ref[...] for ref in f_refs], axis=0)
    for s in range(0, out_ref.shape[0], WSUB):
        r = jnp.concatenate([ref[:, start + s : start + s + WSUB] for ref in r_refs], axis=0)
        total = lax.dot_general(r, f, (((0,), (0,)), ((), ())), preferred_element_type=jnp.float32)
        out_ref[s : s + WSUB, :] = total.astype(jnp.bfloat16)


def weight_partial(rs, fs, start, count, after):
    rows, width = fs[0].shape
    return pl.pallas_call(
        functools.partial(weight_partial_kernel, start),
        in_specs=[WHOLE] * (2 * N) + [ORDER] * len(after),
        out_specs=WHOLE,
        out_shape=VMEM((count, width), jnp.bfloat16),
        name="weight_partial",
        cost_estimate=cost(2 * rows * count),
        compiler_params=params(12),
    )(*[vmem(x) for x in rs], *[vmem(x) for x in fs], *after)


def weight_rows_kernel(start, *refs):
    r_refs, f_refs, other_ref = refs[:N], refs[N : 2 * N], refs[2 * N]
    out_ref, done_ref, rows_ref, sems = refs[-4:]
    f = jnp.concatenate([ref[...] for ref in f_refs], axis=0)
    copies = []
    for s in range(0, rows_ref.shape[0], WSUB):
        r = jnp.concatenate([ref[:, start + s : start + s + WSUB] for ref in r_refs], axis=0)
        total = lax.dot_general(r, f, (((0,), (0,)), ((), ())), preferred_element_type=jnp.float32)
        total = total + other_ref[s : s + WSUB, :].astype(jnp.float32)
        rows_ref[s : s + WSUB, :] = total.astype(jnp.bfloat16)
        copy = pltpu.make_async_copy(
            rows_ref.at[pl.ds(s, WSUB)], out_ref.at[pl.ds(start + s, WSUB)], sems.at[s // WSUB]
        )
        copy.start()
        copies.append(copy)
    done_ref[...] = jnp.zeros_like(done_ref)
    for copy in copies:
        copy.wait()


def weight_rows(rs, fs, start, count, own, other, whole, after):
    rows, width = fs[0].shape
    extra, aliases = tuple(after), {}
    if whole is not None:
        extra, aliases = (whole,) + extra, {2 * N + 1: 0}
    return pl.pallas_call(
        functools.partial(weight_rows_kernel, start),
        in_specs=[WHOLE] * (2 * N + 1) + [ORDER] * len(extra),
        out_specs=[ORDER, WHOLE],
        out_shape=[jax.ShapeDtypeStruct((own, width), jnp.bfloat16), VMEM((8, LANES), jnp.float32)],
        scratch_shapes=[VMEM((count, width), jnp.bfloat16), pltpu.SemaphoreType.DMA((count // WSUB,))],
        input_output_aliases=aliases,
        name="weight_rows",
        cost_estimate=cost(16 * N * rows * count * width),
        compiler_params=params(12),
    )(*[vmem(x) for x in rs], *[vmem(x) for x in fs], vmem(other), *extra)


def add_kernel(count, own_ref, a_ref, b_ref, c_ref, *refs):
    rows = a_ref.shape[0]
    total = own_ref[:rows, :] + a_ref[...].astype(jnp.float32)
    total = total + b_ref[...].astype(jnp.float32) + c_ref[...].astype(jnp.float32)
    outs = refs[len(refs) - count :]
    step = rows // count
    outs[0][...] = total[:step, :]
    for k in range(1, count):
        outs[k][...] = total[k * step : (k + 1) * step, :].astype(jnp.bfloat16)


def add(own, parts, count, after=()):
    rows, width = parts[0].shape
    kinds = [jnp.float32] + [jnp.bfloat16] * (count - 1)
    return pl.pallas_call(
        functools.partial(add_kernel, count),
        in_specs=[WHOLE] * 4 + [ORDER] * len(after),
        out_specs=[WHOLE] * count,
        out_shape=[VMEM((rows // count, width), kind) for kind in kinds],
        name="add",
        cost_estimate=cost(3 * 10**11),
        compiler_params=params(4),
    )(vmem(own), *[vmem(x) for x in parts], *after)


def on_device(features, label_weight, label_bias, positive_ids, positive_counts):
    own, width = label_weight.shape
    piece = features.shape[0]
    me = lax.axis_index(AXES)
    core, z, x, y = me % 2, me // 2 % N, me // 8 % N, me // 32
    pos = jnp.stack([core, me // 2 * 2 * own, own, jnp.where(core == 0, x, y), jnp.where(core == 0, y, x), z])

    b0 = label_bias.reshape(1, own)
    w1, b1 = swap(label_weight), swap(b0)
    f64 = join([load(features, (b1,))] + [fetch(features, "first", k) for k in (1, 2, 3)], factor=0.5)
    w0, words, b = prepare(piece, pos, label_weight, positive_ids.T, positive_counts.reshape(1, -1), b0, b1, after=(f64,))
    f256 = join([f64] + [fetch(f64, "second", k) for k in (1, 2, 3)], after=(words,))
    fs = [f256, fetch(f256, "third", 1), None, fetch(f256, "third", 3)]

    rs = [None] * N
    rs[0], sums, again = residual(0, piece, pos, f256, w0, w1, b, words, jnp.float32, again=True)
    fs[2] = fetch(again, "third", 2)
    arrived, after = [], (sums,)
    for k in (1, 3, 2):
        rs[k], part = residual(k, piece, pos, fs[k], w0, w1, b, words, jnp.bfloat16, after)
        after = (part,)
        arrived.append(push(part, "third", k))

    half = own // 2
    theirs = [swap(weight_partial(rs, fs, own + s, half, x)) for s, x in zip((0, half), ((), arrived[:2]))]
    sums, *sent = add(sums, arrived, N)
    arrived = [push(x, "second", k) for k, x in zip((1, 2, 3), sent)]
    weight_grad, done = weight_rows(rs, fs, 0, half, own, theirs[0], None, sent)
    sums, *sent = add(sums, arrived, N, after=(done,))
    arrived = [push(x, "first", k) for k, x in zip((1, 2, 3), sent)]
    weight_grad, _ = weight_rows(rs, fs, half, half, own, theirs[1], weight_grad, sent)
    for x in arrived:
        sums = sums + x.astype(jnp.float32)
    return weight_grad, sums


def solution(mesh):
    split = P(AXES, None)
    return jax.shard_map(
        on_device,
        mesh=mesh,
        in_specs=(split, split, P(AXES), P(), P()),
        out_specs=(split, split),
        check_vma=False,
    )
```

time: 97.8 us -> 73.5 us (0.75)
  Pallas kernels: 44 us -> 30.8 us
  waiting for transfers between devices: 14.3 us -> 9.61 us
  other arithmetic: 4.5 us -> 0.64 us
  local copies, waits for them, and re-layouts: 3.27 us -> 0.08 us
  starting transfers between devices: 29.9 us -> 31.4 us
    pallas_call x9 -> x14, Pallas kernels: 44 us -> 30.8 us  [the longest x4 17.2 us: residual(): pl.pallas_call(functools.partial(residual_kernel, chunk, piece, again), i...]
    ppermute x9, waiting for transfers between devices: 10.2 us -> 6.28 us  [push(): return lax.ppermute(x, AXES, shifted(stage, k))]
    unnamed x10 -> x0, local copies, waits for them, and re-layouts: 3.14 us -> none
    ppermute x9, waiting for transfers between devices: 4.13 us -> 1.95 us  [fetch(): return lax.ppermute(x, AXES, shifted(stage, -k))]
    ppermute x9, starting transfers between devices: 10.9 us -> 12.8 us  [push(): return lax.ppermute(x, AXES, shifted(stage, k))]
    concatenate x2 -> x0, other arithmetic: 1.88 us -> none  [the longest x1 1.87 us: on_device(): weight_grad = jnp.concatenate(mine, axis=0)]
    mul x2 -> x0, other arithmetic: 1.44 us -> none  [the longest x1 0.75 us: on_device(): f16 = features * jnp.bfloat16(0.5)]
    ppermute x4, waiting for transfers between devices: 0.01 us -> 1.39 us  [swap(): return lax.ppermute(x, AXES, [(d, d ^ 1) for d in range(2 * N * N * N)])]
  transfers between devices with their start and end apart: 22 -> 22, of which waited for: 6 -> 8; matrix products, arithmetic and copies ran while one was open for 4% -> 0% of each run, Pallas kernels for 43% -> 42%
where the time goes in v2:
time: 73.5 us; the launch traced here: 73.3 us
  starting transfers between devices  31.4 us (43%)
  Pallas kernels  30.8 us (42%)
  waiting for transfers between devices  9.61 us (13%)
  between operations  0.81 us (1%)
    ppermute x9, starting transfers between devices, fetch(): return lax.ppermute(x, AXES, shifted(stage, -k))  17.9 us
    pallas_call x4, Pallas kernels, residual(): pl.pallas_call(functools.partial(residual_kernel, chunk, piece, again), i...  17.2 us
    ppermute x9, starting transfers between devices, push(): return lax.ppermute(x, AXES, shifted(stage, k))  12.8 us
    ppermute x9, waiting for transfers between devices, push(): return lax.ppermute(x, AXES, shifted(stage, k))  6.28 us
    pallas_call x2, Pallas kernels, weight_rows(): pl.pallas_call(functools.partial(weight_rows_kernel, start), in_specs=[WH...  6.15 us
    pallas_call x2, Pallas kernels, weight_partial(): pl.pallas_call(functools.partial(weight_partial_kernel, start), in_specs=...  3.68 us
    pallas_call x1, Pallas kernels, prepare(): pl.pallas_call(functools.partial(prepare_kernel, piece), in_specs=[SCALAR...  2.77 us
    ppermute x9, waiting for transfers between devices, fetch(): return lax.ppermute(x, AXES, shifted(stage, -k))  1.95 us
  transfers between devices with their start and end apart: 22, of which 8 were waited for; matrix products, arithmetic and copies ran while one was open for 0% of the time, Pallas kernels for 42%

profile of v2, /device:TPU:0, one launch (start us, length us, event | category | flops | bytes accessed | tf_op | source)
XLA Modules:
  0.0 73.3 jit_solution(15053421635630480105)
XLA Ops:
  0.6 0.1 collective-permute-start.7
  0.7 4.2 %collective-permute-start.1 = (bf16[16,768]{1,0:T(8,128)(2,1)}, bf16[16,768]{1,0:T(8,128)(2,1)S(1)}, u32[]{:S(2)}, u32[]{:S(2)}) collective-permute-start(bf16[16,768]{1,0:T(8,128)(2,1)} %x_ref.1), channel_id=1, source_target_pairs={{0,6},{1,7},{2,0},{3,1},{4,2},{5,3},{6,4},{7,5},{8,14},{9,15},{10,... | collective-permute-start | bytes 73736 | tf_op jit(solution)/shard_map/ppermute | solution.py:52
  4.9 1.9 %collective-permute-start.2 = (bf16[16,768]{1,0:T(8,128)(2,1)}, bf16[16,768]{1,0:T(8,128)(2,1)S(1)}, u32[]{:S(2)}, u32[]{:S(2)}) collective-permute-start(bf16[16,768]{1,0:T(8,128)(2,1)} %x_ref.1), channel_id=1, source_target_pairs={{0,4},{1,5},{2,6},{3,7},{4,0},{5,1},{6,2},{7,3},{8,12},{9,13},{10,... | collective-permute-start | bytes 73736 | tf_op jit(solution)/shard_map/ppermute | solution.py:52
  6.8 0.0 collective-permute-start
  6.8 1.4 %collective-permute-done.refs_0_.b1_ref = f32[1,2048]{1,0:T(1,128)S(1)} collective-permute-done((f32[1,2048]{1,0:T(1,128)}, f32[1,2048]{1,0:T(1,128)S(1)}, u32[]{:S(2)}, u32[]{:S(2)}) %collective-permute-start) | collective-permute-done | bytes 8224 | tf_op jit(solution)/shard_map/ppermute | solution.py:60
  8.2 0.7 %load.1.refs_0_ = bf16[16,768]{1,0:T(8,128)(2,1)S(1)} custom-call(bf16[16,768]{1,0:T(8,128)(2,1)} %x_ref.1, f32[1,2048]{1,0:T(1,128)S(1)} %collective-permute-done.refs_0_.b1_ref), custom_call_target="tpu_custom_call" | custom-call | tf_op jit(solution)/shard_map/load/pallas_call | solution.py:129
  8.9 0.0 collective-permute-done.1.refs_1_
  8.9 1.3 %collective-permute-done.3.refs_3_ = bf16[16,768]{1,0:T(8,128)(2,1)S(1)} collective-permute-done((bf16[16,768]{1,0:T(8,128)(2,1)}, bf16[16,768]{1,0:T(8,128)(2,1)S(1)}, u32[]{:S(2)}, u32[]{:S(2)}) %collective-permute-start.3) | collective-permute-done | bytes 24608 | tf_op jit(solution)/shard_map/ppermute | solution.py:52
  10.2 0.3 collective-permute-done.2.refs_2_
  10.5 1.6 %collective-permute-start.6 = (bf16[64,768]{1,0:T(8,128)(2,1)S(1)}, bf16[64,768]{1,0:T(8,128)(2,1)S(1)}, u32[]{:S(2)}, u32[]{:S(2)}) collective-permute-start(bf16[64,768]{1,0:T(8,128)(2,1)S(1)} %join.2.refs_0_), channel_id=1, source_target_pairs={{0,32},{1,9},{2,34},{3,11},{4,36},{5,13},{6,38},{7,15},{8,40},{9,1... | collective-permute-start | bytes 294920 | tf_op jit(solution)/shard_map/ppermute | solution.py:52
  12.1 2.9 %collective-permute-start.5 = (bf16[64,768]{1,0:T(8,128)(2,1)S(1)}, bf16[64,768]{1,0:T(8,128)(2,1)S(1)}, u32[]{:S(2)}, u32[]{:S(2)}) collective-permute-start(bf16[64,768]{1,0:T(8,128)(2,1)S(1)} %join.2.refs_0_), channel_id=1, source_target_pairs={{0,64},{1,17},{2,66},{3,19},{4,68},{5,21},{6,70},{7,23},{8,72},{9,... | collective-permute-start | bytes 294920 | tf_op jit(solution)/shard_map/ppermute | solution.py:52
  15.0 1.3 %collective-permute-start.4 = (bf16[64,768]{1,0:T(8,128)(2,1)S(1)}, bf16[64,768]{1,0:T(8,128)(2,1)S(1)}, u32[]{:S(2)}, u32[]{:S(2)}) collective-permute-start(bf16[64,768]{1,0:T(8,128)(2,1)S(1)} %join.2.refs_0_), channel_id=1, source_target_pairs={{0,96},{1,25},{2,98},{3,27},{4,100},{5,29},{6,102},{7,31},{8,104},... | collective-permute-start | bytes 294920 | tf_op jit(solution)/shard_map/ppermute | solution.py:52
  16.4 0.1 stack.23.pos_ref
  16.5 2.8 %prepare.1 = (bf16[2048,768]{1,0:T(8,128)(2,1)S(1)}, s32[1024,128]{1,0:T(8,128)S(1)}, f32[1,4096]{1,0:T(1,128)S(1)}) custom-call(s32[6]{0:T(128)S(1)} %stack.23.pos_ref, f32[1,2048]{1,0:T(1,128)S(1)} %collective-permute-done.refs_0_.b1_ref, bf16[2048,768]{1,0:T(8,128)(2,1)} %w_ref.1, s32[16,2048]{1,0:T(8,128)} %bitcast.8, s32[1,2048]{1,0:T(1,128)} %bitcast.11, ...), custom_call_target="tpu_custom_call" | custom-call | tf_op jit(solution)/shard_map/prepare/pallas_call | solution.py:103
  19.2 0.0 collective-permute-done.6.refs_3_
  19.3 0.4 collective-permute-done.4.refs_1_
  19.7 3.2 %collective-permute-start.8 = (bf16[256,768]{1,0:T(8,128)(2,1)S(1)}, bf16[256,768]{1,0:T(8,128)(2,1)S(1)}, u32[]{:S(2)}, u32[]{:S(2)}) collective-permute-start(bf16[256,768]{1,0:T(8,128)(2,1)S(1)} %join.3.f_ref.refs_4_), channel_id=1, source_target_pairs={{0,24},{1,97},{2,26},{3,99},{4,28},{5,101},{6,30},{7,103},{8,0},{9... | collective-permute-start | bytes 1179656 | tf_op jit(solution)/shard_map/ppermute | solution.py:52
  22.9 0.0 collective-permute-start.10
  22.9 0.0 collective-permute-done.7.w1_ref
  22.9 4.3 %residual.4 = (bf16[256,4096]{1,0:T(8,128)(2,1)S(1)}, f32[256,768]{1,0:T(8,128)S(1)}, bf16[256,768]{1,0:T(8,128)(2,1)S(1)}) custom-call(s32[6]{0:T(128)S(1)} %stack.23.pos_ref, bf16[256,768]{1,0:T(8,128)(2,1)S(1)} %join.3.f_ref.refs_4_, bf16[2048,768]{1,0:T(8,128)(2,1)S(1)} %get-tuple-element.26.w0_ref, bf16[2048,768]{1,0:T(8,128)(2,1)S(1)} %collective-permute-done.7.w1_ref, ...), custom_call_target="tpu_custom_call" | custom-call | flops 524288 | tf_op jit(solution)/shard_map/residual/pallas_call | solution.py:193
  27.2 2.7 %collective-permute-start.9 = (bf16[256,768]{1,0:T(8,128)(2,1)S(1)}, bf16[256,768]{1,0:T(8,128)(2,1)S(1)}, u32[]{:S(2)}, u32[]{:S(2)}) collective-permute-start(bf16[256,768]{1,0:T(8,128)(2,1)S(1)} %get-tuple-element.31), channel_id=1, source_target_pairs={{0,16},{1,65},{2,18},{3,67},{4,20},{5,69},{6,22},{7,71},{8,24},{9,... | collective-permute-start | bytes 1179656 | tf_op jit(solution)/shard_map/ppermute | solution.py:52
  29.9 0.0 collective-permute-done.8.f_ref.refs_5_
  29.9 4.3 %residual.5 = (bf16[256,4096]{1,0:T(8,128)(2,1)S(1)}, bf16[256,768]{1,0:T(8,128)(2,1)S(1)}) custom-call(s32[6]{0:T(128)S(1)} %stack.23.pos_ref, bf16[256,768]{1,0:T(8,128)(2,1)S(1)} %collective-permute-done.8.f_ref.refs_5_, bf16[2048,768]{1,0:T(8,128)(2,1)S(1)} %get-tuple-element.26.w0_ref, bf16[2048,768]{1,0:T(8,128)(2,1)S(1)} %collective-permute-done.7.w1_ref, ...), custom_call_target="tpu_custom_call" | custom-call | flops 524288 | tf_op jit(solution)/shard_map/residual/pallas_call | solution.py:193
  34.2 1.8 %collective-permute-start.11 = (bf16[256,768]{1,0:T(8,128)(2,1)S(1)}, bf16[256,768]{1,0:T(8,128)(2,1)S(1)}, u32[]{:S(2)}, u32[]{:S(2)}) collective-permute-start(bf16[256,768]{1,0:T(8,128)(2,1)S(1)} %get-tuple-element.32.refs_0_), channel_id=1, source_target_pairs={{0,8},{1,33},{2,10},{3,35},{4,12},{5,37},{6,14},{7,39},{8,16},{9,4... | collective-permute-start | bytes 1179656 | tf_op jit(solution)/shard_map/ppermute | solution.py:56
  36.0 4.3 %residual.6 = (bf16[256,4096]{1,0:T(8,128)(2,1)S(1)}, bf16[256,768]{1,0:T(8,128)(2,1)S(1)}) custom-call(s32[6]{0:T(128)S(1)} %stack.23.pos_ref, bf16[256,768]{1,0:T(8,128)(2,1)S(1)} %collective-permute-done.10.f_ref.refs_7_, bf16[2048,768]{1,0:T(8,128)(2,1)S(1)} %get-tuple-element.26.w0_ref, bf16[2048,768]{1,0:T(8,128)(2,1)S(1)} %collective-permute-done.7.w1_ref, ...), custom_call_target="tpu_custom_call" | custom-call | flops 524288 | tf_op jit(solution)/shard_map/residual/pallas_call | solution.py:193
  40.3 1.7 %collective-permute-start.12 = (bf16[256,768]{1,0:T(8,128)(2,1)S(1)}, bf16[256,768]{1,0:T(8,128)(2,1)S(1)}, u32[]{:S(2)}, u32[]{:S(2)}) collective-permute-start(bf16[256,768]{1,0:T(8,128)(2,1)S(1)} %get-tuple-element.33.refs_0_), channel_id=1, source_target_pairs={{0,24},{1,97},{2,26},{3,99},{4,28},{5,101},{6,30},{7,103},{8,0},{9... | collective-permute-start | bytes 1179656 | tf_op jit(solution)/shard_map/ppermute | solution.py:56
  42.1 4.3 %residual.7 = (bf16[256,4096]{1,0:T(8,128)(2,1)S(1)}, bf16[256,768]{1,0:T(8,128)(2,1)S(1)}) custom-call(s32[6]{0:T(128)S(1)} %stack.23.pos_ref, bf16[256,768]{1,0:T(8,128)(2,1)S(1)} %collective-permute-done.9.f_ref.refs_6_, bf16[2048,768]{1,0:T(8,128)(2,1)S(1)} %get-tuple-element.26.w0_ref, bf16[2048,768]{1,0:T(8,128)(2,1)S(1)} %collective-permute-done.7.w1_ref, ...), custom_call_target="tpu_custom_call" | custom-call | flops 524288 | tf_op jit(solution)/shard_map/residual/pallas_call | solution.py:193
  46.3 0.5 collective-permute-start.15
  46.8 1.8 %weight_partial.3 = bf16[1024,768]{1,0:T(8,128)(2,1)S(1)} custom-call(bf16[256,4096]{1,0:T(8,128)(2,1)S(1)} %get-tuple-element.28.refs_0_, bf16[256,4096]{1,0:T(8,128)(2,1)S(1)} %get-tuple-element.30.refs_1_, bf16[256,4096]{1,0:T(8,128)(2,1)S(1)} %get-tuple-element.34.refs_2_, bf16[256,4096]{1,0:T(8,128)(2,1)S(1)} %get-tuple-element.35.refs_3_, ...), custom_call_target="tpu_custom_call" | custom-call | flops 65536 | tf_op jit(solution)/shard_map/weight_partial/pallas_call | solution.py:215
  48.6 0.1 collective-permute-start.14
  48.7 0.0 collective-permute-done.11.refs_8_.a_ref
  48.8 1.8 %weight_partial.2 = bf16[1024,768]{1,0:T(8,128)(2,1)S(1)} custom-call(bf16[256,4096]{1,0:T(8,128)(2,1)S(1)} %get-tuple-element.28.refs_0_, bf16[256,4096]{1,0:T(8,128)(2,1)S(1)} %get-tuple-element.30.refs_1_, bf16[256,4096]{1,0:T(8,128)(2,1)S(1)} %get-tuple-element.34.refs_2_, bf16[256,4096]{1,0:T(8,128)(2,1)S(1)} %get-tuple-element.35.refs_3_, ...), custom_call_target="tpu_custom_call" | custom-call | flops 65536 | tf_op jit(solution)/shard_map/weight_partial/pallas_call | solution.py:215
  50.6 0.5 collective-permute-start.13
  51.2 4.6 %collective-permute-done.15.c_ref = bf16[256,768]{1,0:T(8,128)(2,1)S(1)} collective-permute-done((bf16[256,768]{1,0:T(8,128)(2,1)S(1)}, bf16[256,768]{1,0:T(8,128)(2,1)S(1)}, u32[]{:S(2)}, u32[]{:S(2)}) %collective-permute-start.15) | collective-permute-done | bytes 393248 | tf_op jit(solution)/shard_map/ppermute | solution.py:56
  55.7 0.2 add.37
  55.9 0.1 collective-permute-start.16
  56.0 3.2 %collective-permute-start.17 = (bf16[64,768]{1,0:T(8,128)(2,1)S(1)}, bf16[64,768]{1,0:T(8,128)(2,1)S(1)}, u32[]{:S(2)}, u32[]{:S(2)}) collective-permute-start(bf16[64,768]{1,0:T(8,128)(2,1)S(1)} %get-tuple-element.38.refs_10_), channel_id=1, source_target_pairs={{0,64},{1,17},{2,66},{3,19},{4,68},{5,21},{6,70},{7,23},{8,72},{9,... | collective-permute-start | bytes 294920 | tf_op jit(solution)/shard_map/ppermute | solution.py:56
  59.2 0.5 collective-permute-start.18
  59.8 0.0 collective-permute-done.14.refs_8_
  59.8 2.8 %weight_rows.2 = (bf16[2048,768]{1,0:T(8,128)(2,1)}, f32[8,128]{1,0:T(8,128)S(1)}) custom-call(bf16[256,4096]{1,0:T(8,128)(2,1)S(1)} %get-tuple-element.28.refs_0_, bf16[256,4096]{1,0:T(8,128)(2,1)S(1)} %get-tuple-element.30.refs_1_, bf16[256,4096]{1,0:T(8,128)(2,1)S(1)} %get-tuple-element.34.refs_2_, bf16[256,4096]{1,0:T(8,128)(2,1)S(1)} %get-tuple-element.35.refs_3_, ...), custom_call_target="tpu_custom_call" | custom-call | flops 1610612736 | tf_op jit(solution)/shard_map/weight_rows/pallas_call | solution.py:251
  62.6 0.3 collective-permute-done.17.b_ref
  62.9 1.0 %collective-permute-done.18.c_ref = bf16[64,768]{1,0:T(8,128)(2,1)S(1)} collective-permute-done((bf16[64,768]{1,0:T(8,128)(2,1)S(1)}, bf16[64,768]{1,0:T(8,128)(2,1)S(1)}, u32[]{:S(2)}, u32[]{:S(2)}) %collective-permute-start.18) | collective-permute-done | bytes 98336 | tf_op jit(solution)/shard_map/ppermute | solution.py:56
  63.9 0.8 %collective-permute-start.19 = (bf16[16,768]{1,0:T(8,128)(2,1)S(1)}, bf16[16,768]{1,0:T(8,128)(2,1)S(1)}, u32[]{:S(2)}, u32[]{:S(2)}) collective-permute-start(bf16[16,768]{1,0:T(8,128)(2,1)S(1)} %get-tuple-element.43.refs_10_), channel_id=1, source_target_pairs={{0,2},{1,3},{2,4},{3,5},{4,6},{5,7},{6,0},{7,1},{8,10},{9,11},{10,... | collective-permute-start | bytes 73736 | tf_op jit(solution)/shard_map/ppermute | solution.py:56
  64.7 4.2 %collective-permute-start.20 = (bf16[16,768]{1,0:T(8,128)(2,1)S(1)}, bf16[16,768]{1,0:T(8,128)(2,1)S(1)}, u32[]{:S(2)}, u32[]{:S(2)}) collective-permute-start(bf16[16,768]{1,0:T(8,128)(2,1)S(1)} %get-tuple-element.44.refs_11_), channel_id=1, source_target_pairs={{0,4},{1,5},{2,6},{3,7},{4,0},{5,1},{6,2},{7,3},{8,12},{9,13},{10,... | collective-permute-start | bytes 73736 | tf_op jit(solution)/shard_map/ppermute | solution.py:56
  68.9 0.0 collective-permute-start.21
  68.9 3.4 %weight_rows.3 = (bf16[2048,768]{1,0:T(8,128)(2,1)}, f32[8,128]{1,0:T(8,128)}) custom-call(bf16[256,4096]{1,0:T(8,128)(2,1)S(1)} %get-tuple-element.28.refs_0_, bf16[256,4096]{1,0:T(8,128)(2,1)S(1)} %get-tuple-element.30.refs_1_, bf16[256,4096]{1,0:T(8,128)(2,1)S(1)} %get-tuple-element.34.refs_2_, ...), custom_call_target="tpu_custom_call", output_to_operand_aliasing={{0}: (9, {})} | custom-call | flops 1610612736 | tf_op jit(solution)/shard_map/weight_rows/pallas_call | solution.py:251
  72.3 0.4 collective-permute-done.21
  72.7 0.6 convert_add_fusion
  (12 shorter events, 0.1 us)
Async XLA Ops:
  0.6 22.3 %collective-permute-start.7 = (bf16[2048,768]{1,0:T(8,128)(2,1)}, bf16[2048,768]{1,0:T(8,128)(2,1)S(1)}, u32[]{:S(2)}, u32[]{:S(2)}) collective-permute-start(bf16[2048,768]{1,0:T(8,128)(2,1)} %w_ref.1), channel_id=1, source_target_pairs={{0,1},{1,0},{2,3},{3,2},{4,5},{5,4},{6,7},{7,6},{8,9},{9,8},{10,11... | collective-permute-start | bytes 9437192 | tf_op jit(solution)/shard_map/ppermute | solution.py:60
  0.7 8.2 %collective-permute-start.1 = (bf16[16,768]{1,0:T(8,128)(2,1)}, bf16[16,768]{1,0:T(8,128)(2,1)S(1)}, u32[]{:S(2)}, u32[]{:S(2)}) collective-permute-start(bf16[16,768]{1,0:T(8,128)(2,1)} %x_ref.1), channel_id=1, source_target_pairs={{0,6},{1,7},{2,0},{3,1},{4,2},{5,3},{6,4},{7,5},{8,14},{9,15},{10,... | collective-permute-start | bytes 73736 | tf_op jit(solution)/shard_map/ppermute | solution.py:52
  4.9 5.2 %collective-permute-start.3 = (bf16[16,768]{1,0:T(8,128)(2,1)}, bf16[16,768]{1,0:T(8,128)(2,1)S(1)}, u32[]{:S(2)}, u32[]{:S(2)}) collective-permute-start(bf16[16,768]{1,0:T(8,128)(2,1)} %x_ref.1), channel_id=1, source_target_pairs={{0,2},{1,3},{2,4},{3,5},{4,6},{5,7},{6,0},{7,1},{8,10},{9,11},{10,... | collective-permute-start | bytes 73736 | tf_op jit(solution)/shard_map/ppermute | solution.py:52
  4.9 5.5 %collective-permute-start.2 = (bf16[16,768]{1,0:T(8,128)(2,1)}, bf16[16,768]{1,0:T(8,128)(2,1)S(1)}, u32[]{:S(2)}, u32[]{:S(2)}) collective-permute-start(bf16[16,768]{1,0:T(8,128)(2,1)} %x_ref.1), channel_id=1, source_target_pairs={{0,4},{1,5},{2,6},{3,7},{4,0},{5,1},{6,2},{7,3},{8,12},{9,13},{10,... | collective-permute-start | bytes 73736 | tf_op jit(solution)/shard_map/ppermute | solution.py:52
  6.8 1.4 %collective-permute-start = (f32[1,2048]{1,0:T(1,128)}, f32[1,2048]{1,0:T(1,128)S(1)}, u32[]{:S(2)}, u32[]{:S(2)}) collective-permute-start(f32[1,2048]{1,0:T(1,128)} %bitcast.9), channel_id=1, source_target_pairs={{0,1},{1,0},{2,3},{3,2},{4,5},{5,4},{6,7},{7,6},{8,9},{9,8},{10,11... | collective-permute-start | bytes 24584 | tf_op jit(solution)/shard_map/ppermute | solution.py:60
  10.5 8.8 %collective-permute-start.6 = (bf16[64,768]{1,0:T(8,128)(2,1)S(1)}, bf16[64,768]{1,0:T(8,128)(2,1)S(1)}, u32[]{:S(2)}, u32[]{:S(2)}) collective-permute-start(bf16[64,768]{1,0:T(8,128)(2,1)S(1)} %join.2.refs_0_), channel_id=1, source_target_pairs={{0,32},{1,9},{2,34},{3,11},{4,36},{5,13},{6,38},{7,15},{8,40},{9,1... | collective-permute-start | bytes 294920 | tf_op jit(solution)/shard_map/ppermute | solution.py:52
  12.1 7.1 %collective-permute-start.5 = (bf16[64,768]{1,0:T(8,128)(2,1)S(1)}, bf16[64,768]{1,0:T(8,128)(2,1)S(1)}, u32[]{:S(2)}, u32[]{:S(2)}) collective-permute-start(bf16[64,768]{1,0:T(8,128)(2,1)S(1)} %join.2.refs_0_), channel_id=1, source_target_pairs={{0,64},{1,17},{2,66},{3,19},{4,68},{5,21},{6,70},{7,23},{8,72},{9,... | collective-permute-start | bytes 294920 | tf_op jit(solution)/shard_map/ppermute | solution.py:52
  15.0 4.6 %collective-permute-start.4 = (bf16[64,768]{1,0:T(8,128)(2,1)S(1)}, bf16[64,768]{1,0:T(8,128)(2,1)S(1)}, u32[]{:S(2)}, u32[]{:S(2)}) collective-permute-start(bf16[64,768]{1,0:T(8,128)(2,1)S(1)} %join.2.refs_0_), channel_id=1, source_target_pairs={{0,96},{1,25},{2,98},{3,27},{4,100},{5,29},{6,102},{7,31},{8,104},... | collective-permute-start | bytes 294920 | tf_op jit(solution)/shard_map/ppermute | solution.py:52
  19.7 10.2 %collective-permute-start.8 = (bf16[256,768]{1,0:T(8,128)(2,1)S(1)}, bf16[256,768]{1,0:T(8,128)(2,1)S(1)}, u32[]{:S(2)}, u32[]{:S(2)}) collective-permute-start(bf16[256,768]{1,0:T(8,128)(2,1)S(1)} %join.3.f_ref.refs_4_), channel_id=1, source_target_pairs={{0,24},{1,97},{2,26},{3,99},{4,28},{5,101},{6,30},{7,103},{8,0},{9... | collective-permute-start | bytes 1179656 | tf_op jit(solution)/shard_map/ppermute | solution.py:52
  22.9 13.1 %collective-permute-start.10 = (bf16[256,768]{1,0:T(8,128)(2,1)S(1)}, bf16[256,768]{1,0:T(8,128)(2,1)S(1)}, u32[]{:S(2)}, u32[]{:S(2)}) collective-permute-start(bf16[256,768]{1,0:T(8,128)(2,1)S(1)} %join.3.f_ref.refs_4_), channel_id=1, source_target_pairs={{0,8},{1,33},{2,10},{3,35},{4,12},{5,37},{6,14},{7,39},{8,16},{9,4... | collective-permute-start | bytes 1179656 | tf_op jit(solution)/shard_map/ppermute | solution.py:52
  27.2 14.9 %collective-permute-start.9 = (bf16[256,768]{1,0:T(8,128)(2,1)S(1)}, bf16[256,768]{1,0:T(8,128)(2,1)S(1)}, u32[]{:S(2)}, u32[]{:S(2)}) collective-permute-start(bf16[256,768]{1,0:T(8,128)(2,1)S(1)} %get-tuple-element.31), channel_id=1, source_target_pairs={{0,16},{1,65},{2,18},{3,67},{4,20},{5,69},{6,22},{7,71},{8,24},{9,... | collective-permute-start | bytes 1179656 | tf_op jit(solution)/shard_map/ppermute | solution.py:52
  34.2 14.5 %collective-permute-start.11 = (bf16[256,768]{1,0:T(8,128)(2,1)S(1)}, bf16[256,768]{1,0:T(8,128)(2,1)S(1)}, u32[]{:S(2)}, u32[]{:S(2)}) collective-permute-start(bf16[256,768]{1,0:T(8,128)(2,1)S(1)} %get-tuple-element.32.refs_0_), channel_id=1, source_target_pairs={{0,8},{1,33},{2,10},{3,35},{4,12},{5,37},{6,14},{7,39},{8,16},{9,4... | collective-permute-start | bytes 1179656 | tf_op jit(solution)/shard_map/ppermute | solution.py:56
  40.3 8.4 %collective-permute-start.12 = (bf16[256,768]{1,0:T(8,128)(2,1)S(1)}, bf16[256,768]{1,0:T(8,128)(2,1)S(1)}, u32[]{:S(2)}, u32[]{:S(2)}) collective-permute-start(bf16[256,768]{1,0:T(8,128)(2,1)S(1)} %get-tuple-element.33.refs_0_), channel_id=1, source_target_pairs={{0,24},{1,97},{2,26},{3,99},{4,28},{5,101},{6,30},{7,103},{8,0},{9... | collective-permute-start | bytes 1179656 | tf_op jit(solution)/shard_map/ppermute | solution.py:56
  46.3 9.4 %collective-permute-start.15 = (bf16[256,768]{1,0:T(8,128)(2,1)S(1)}, bf16[256,768]{1,0:T(8,128)(2,1)S(1)}, u32[]{:S(2)}, u32[]{:S(2)}) collective-permute-start(bf16[256,768]{1,0:T(8,128)(2,1)S(1)} %get-tuple-element.36), channel_id=1, source_target_pairs={{0,16},{1,65},{2,18},{3,67},{4,20},{5,69},{6,22},{7,71},{8,24},{9,... | collective-permute-start | bytes 1179656 | tf_op jit(solution)/shard_map/ppermute | solution.py:56
  48.6 11.1 %collective-permute-start.14 = (bf16[1024,768]{1,0:T(8,128)(2,1)S(1)}, bf16[1024,768]{1,0:T(8,128)(2,1)S(1)}, u32[]{:S(2)}, u32[]{:S(2)}) collective-permute-start(bf16[1024,768]{1,0:T(8,128)(2,1)S(1)} %weight_partial.3), channel_id=1, source_target_pairs={{0,1},{1,0},{2,3},{3,2},{4,5},{5,4},{6,7},{7,6},{8,9},{9,8},{10,11... | collective-permute-start | bytes 4718600 | tf_op jit(solution)/shard_map/ppermute | solution.py:60
  50.6 18.3 %collective-permute-start.13 = (bf16[1024,768]{1,0:T(8,128)(2,1)S(1)}, bf16[1024,768]{1,0:T(8,128)(2,1)S(1)}, u32[]{:S(2)}, u32[]{:S(2)}) collective-permute-start(bf16[1024,768]{1,0:T(8,128)(2,1)S(1)} %weight_partial.2), channel_id=1, source_target_pairs={{0,1},{1,0},{2,3},{3,2},{4,5},{5,4},{6,7},{7,6},{8,9},{9,8},{10,11... | collective-permute-start | bytes 4718600 | tf_op jit(solution)/shard_map/ppermute | solution.py:60
  55.9 6.7 %collective-permute-start.16 = (bf16[64,768]{1,0:T(8,128)(2,1)S(1)}, bf16[64,768]{1,0:T(8,128)(2,1)S(1)}, u32[]{:S(2)}, u32[]{:S(2)}) collective-permute-start(bf16[64,768]{1,0:T(8,128)(2,1)S(1)} %get-tuple-element.37.refs_9_), channel_id=1, source_target_pairs={{0,32},{1,9},{2,34},{3,11},{4,36},{5,13},{6,38},{7,15},{8,40},{9,1... | collective-permute-start | bytes 294920 | tf_op jit(solution)/shard_map/ppermute | solution.py:56
  56.0 6.9 %collective-permute-start.17 = (bf16[64,768]{1,0:T(8,128)(2,1)S(1)}, bf16[64,768]{1,0:T(8,128)(2,1)S(1)}, u32[]{:S(2)}, u32[]{:S(2)}) collective-permute-start(bf16[64,768]{1,0:T(8,128)(2,1)S(1)} %get-tuple-element.38.refs_10_), channel_id=1, source_target_pairs={{0,64},{1,17},{2,66},{3,19},{4,68},{5,21},{6,70},{7,23},{8,72},{9,... | collective-permute-start | bytes 294920 | tf_op jit(solution)/shard_map/ppermute | solution.py:56
  59.2 4.6 %collective-permute-start.18 = (bf16[64,768]{1,0:T(8,128)(2,1)S(1)}, bf16[64,768]{1,0:T(8,128)(2,1)S(1)}, u32[]{:S(2)}, u32[]{:S(2)}) collective-permute-start(bf16[64,768]{1,0:T(8,128)(2,1)S(1)} %get-tuple-element.39.refs_11_), channel_id=1, source_target_pairs={{0,96},{1,25},{2,98},{3,27},{4,100},{5,29},{6,102},{7,31},{8,104},... | collective-permute-start | bytes 294920 | tf_op jit(solution)/shard_map/ppermute | solution.py:56
  63.9 8.4 %collective-permute-start.19 = (bf16[16,768]{1,0:T(8,128)(2,1)S(1)}, bf16[16,768]{1,0:T(8,128)(2,1)S(1)}, u32[]{:S(2)}, u32[]{:S(2)}) collective-permute-start(bf16[16,768]{1,0:T(8,128)(2,1)S(1)} %get-tuple-element.43.refs_10_), channel_id=1, source_target_pairs={{0,2},{1,3},{2,4},{3,5},{4,6},{5,7},{6,0},{7,1},{8,10},{9,11},{10,... | collective-permute-start | bytes 73736 | tf_op jit(solution)/shard_map/ppermute | solution.py:56
  64.7 7.6 %collective-permute-start.20 = (bf16[16,768]{1,0:T(8,128)(2,1)S(1)}, bf16[16,768]{1,0:T(8,128)(2,1)S(1)}, u32[]{:S(2)}, u32[]{:S(2)}) collective-permute-start(bf16[16,768]{1,0:T(8,128)(2,1)S(1)} %get-tuple-element.44.refs_11_), channel_id=1, source_target_pairs={{0,4},{1,5},{2,6},{3,7},{4,0},{5,1},{6,2},{7,3},{8,12},{9,13},{10,... | collective-permute-start | bytes 73736 | tf_op jit(solution)/shard_map/ppermute | solution.py:56
  68.9 3.8 %collective-permute-start.21 = (bf16[16,768]{1,0:T(8,128)(2,1)S(1)}, bf16[16,768]{1,0:T(8,128)(2,1)S(1)}, u32[]{:S(2)}, u32[]{:S(2)}) collective-permute-start(bf16[16,768]{1,0:T(8,128)(2,1)S(1)} %get-tuple-element.45.refs_12_), channel_id=1, source_target_pairs={{0,6},{1,7},{2,0},{3,1},{4,2},{5,3},{6,4},{7,5},{8,14},{9,15},{10,... | collective-permute-start | bytes 73736 | tf_op jit(solution)/shard_map/ppermute | solution.py:56

commit v3 on v2

--- a/solution.py
+++ b/solution.py
@@ -13,6 +13,7 @@
 LANES = 128
 SUB = 1024
 WSUB = 512
+FSUB = 256
 VMEM = pltpu.VMEM
 WHOLE = pl.BlockSpec(memory_space=VMEM)
 SCALARS = pl.BlockSpec(memory_space=pltpu.SMEM)
@@ -72,6 +73,7 @@
     slots, queries = ids_ref.shape
     row = lax.broadcasted_iota(jnp.int32, (8, LANES), 0)
     slot = lax.broadcasted_iota(jnp.int32, (slots, LANES), 0)
+    third, second, first = pos_ref[3], pos_ref[4], pos_ref[5]
     lane = lax.broadcasted_iota(jnp.int32, (slots, LANES), 1)
     kept = (lane // piece) % 2 == core
     shift = jnp.where(core == 0, piece, LANES - piece)
@@ -93,7 +95,15 @@
             for j in range(slots):
                 word = word | jnp.where(low[j : j + 1, :] == row + g, bit[j : j + 1, :], 0)
             parts.append(word)
-        words_out[q // 2 : q // 2 + LANES, :] = jnp.concatenate(parts, axis=0).T
+        words = jnp.concatenate(parts, axis=0).T
+        for place in range(LANES // piece):
+            near = place % 2 == core
+            chip = q // (2 * piece) + place // 2 + jnp.where(near, 0, N)
+            y, x, z = chip // (N * N), chip // N % N, chip % N
+            at3 = (jnp.where(core == 0, x, y) - third + N) % N
+            at2 = (jnp.where(core == 0, y, x) - second + N) % N
+            row_at = ((at3 * N + at2) * N + (z - first + N) % N) * piece
+            words_out[pl.ds(pl.multiple_of(row_at, piece), piece), :] = words[place * piece : (place + 1) * piece, :]
     copies[2].wait()
     half_out[...] = 0.5 * jnp.concatenate([b0_ref[...], b1_ref[...]], axis=1)
     copies[3].wait()
@@ -154,23 +164,13 @@
     )(*[vmem(x) for x in parts], *after)
 
 
-def residual_kernel(chunk, piece, again, pos_ref, f_ref, w0_ref, w1_ref, b_ref, words_ref, *refs):
+def residual_kernel(chunk, again, f_ref, w0_ref, w1_ref, b_ref, words_ref, *refs):
     r_ref, o_ref = refs[-3:-1] if again else refs[-2:]
     f = f_ref[...]
     if again:
         refs[-1][...] = f
-    own = w0_ref.shape[0]
-    core, third, second, first = pos_ref[0], pos_ref[3], pos_ref[4], pos_ref[5]
-    stride3 = jnp.where(core == 0, STRIDE["x"], STRIDE["y"]) // 2
-    stride2 = jnp.where(core == 0, STRIDE["y"], STRIDE["x"]) // 2
-    words = []
-    for a in range(N):
-        for b in range(N):
-            chip = (third + chunk) % N * stride3 + (second + a) % N * stride2 + (first + b) % N
-            near = chip % 8 < 4
-            place = chip // 8 * 8 + chip % 4 * 2 + jnp.where(near, core, 1 - core)
-            words.append(words_ref[pl.ds(pl.multiple_of(place * piece, piece), piece), :])
-    words = jnp.concatenate(words, axis=0)
+    rows, own = f.shape[0], w0_ref.shape[0]
+    words = words_ref[chunk * rows : (chunk + 1) * rows, :]
     for half, w_ref in enumerate((w0_ref, w1_ref)):
         for s in range(0, own, SUB):
             logits = lax.dot_general(
@@ -187,18 +187,18 @@
     o_ref[...] = (total * 0.5).astype(o_ref.dtype)
 
 
-def residual(chunk, piece, pos, f, w0, w1, b, words, out_type, after=(), again=False):
+def residual(chunk, f, w0, w1, b, words, out_type, after=(), again=False):
     rows, width = f.shape
     labels = 2 * w0.shape[0]
     return pl.pallas_call(
-        functools.partial(residual_kernel, chunk, piece, again),
-        in_specs=[SCALARS] + [WHOLE] * 5 + [ORDER] * len(after),
+        functools.partial(residual_kernel, chunk, again),
+        in_specs=[WHOLE] * 5 + [ORDER] * len(after),
         out_specs=[WHOLE] * (3 if again else 2),
         out_shape=[VMEM((rows, labels), jnp.bfloat16), VMEM((rows, width), out_type)] + [VMEM(f.shape, f.dtype)] * again,
         name="residual",
         cost_estimate=cost(4 * rows * labels),
         compiler_params=params(12),
-    )(pos, *[vmem(x) for x in (f, w0, w1, b, words)], *after)
+    )(*[vmem(x) for x in (f, w0, w1, b, words)], *after)
 
 
 def weight_partial_kernel(start, *refs):
@@ -207,16 +207,16 @@
     for s in range(0, out_ref.shape[0], WSUB):
         r = jnp.concatenate([ref[:, start + s : start + s + WSUB] for ref in r_refs], axis=0)
         total = lax.dot_general(r, f, (((0,), (0,)), ((), ())), preferred_element_type=jnp.float32)
-        out_ref[s : s + WSUB, :] = total.astype(jnp.bfloat16)
-
-
-def weight_partial(rs, fs, start, count, after):
+        out_ref[s : s + WSUB, :] = total.astype(out_ref.dtype)
+
+
+def weight_partial(rs, fs, start, count, kind, after=()):
     rows, width = fs[0].shape
     return pl.pallas_call(
         functools.partial(weight_partial_kernel, start),
         in_specs=[WHOLE] * (2 * N) + [ORDER] * len(after),
         out_specs=WHOLE,
-        out_shape=VMEM((count, width), jnp.bfloat16),
+        out_shape=VMEM((count, width), kind),
         name="weight_partial",
         cost_estimate=cost(2 * rows * count),
         compiler_params=params(12),
@@ -243,22 +243,48 @@
         copy.wait()
 
 
-def weight_rows(rs, fs, start, count, own, other, whole, after):
+def weight_rows(rs, fs, start, count, own, other, after):
     rows, width = fs[0].shape
-    extra, aliases = tuple(after), {}
-    if whole is not None:
-        extra, aliases = (whole,) + extra, {2 * N + 1: 0}
     return pl.pallas_call(
         functools.partial(weight_rows_kernel, start),
-        in_specs=[WHOLE] * (2 * N + 1) + [ORDER] * len(extra),
+        in_specs=[WHOLE] * (2 * N + 1) + [ORDER] * len(after),
         out_specs=[ORDER, WHOLE],
         out_shape=[jax.ShapeDtypeStruct((own, width), jnp.bfloat16), VMEM((8, LANES), jnp.float32)],
         scratch_shapes=[VMEM((count, width), jnp.bfloat16), pltpu.SemaphoreType.DMA((count // WSUB,))],
-        input_output_aliases=aliases,
         name="weight_rows",
         cost_estimate=cost(16 * N * rows * count * width),
         compiler_params=params(12),
-    )(*[vmem(x) for x in rs], *[vmem(x) for x in fs], vmem(other), *extra)
+    )(*[vmem(x) for x in rs], *[vmem(x) for x in fs], vmem(other), *after)
+
+
+def finish_kernel(start, mine_ref, other_ref, *refs):
+    out_ref, done_ref, rows_ref, sems = refs[-4:]
+    done_ref[...] = jnp.zeros_like(done_ref)
+    copies = []
+    for i, s in enumerate(range(0, rows_ref.shape[0], FSUB)):
+        total = mine_ref[s : s + FSUB, :] + other_ref[s : s + FSUB, :].astype(jnp.float32)
+        rows_ref[s : s + FSUB, :] = total.astype(jnp.bfloat16)
+        copies.append(
+            pltpu.make_async_copy(rows_ref.at[pl.ds(s, FSUB)], out_ref.at[pl.ds(start + s, FSUB)], sems.at[i])
+        )
+        copies[-1].start()
+    for copy in copies:
+        copy.wait()
+
+
+def finish_rows(mine, other, whole, start, after):
+    count, width = mine.shape
+    return pl.pallas_call(
+        functools.partial(finish_kernel, start),
+        in_specs=[WHOLE] * 2 + [ORDER] * (1 + len(after)),
+        out_specs=[ORDER, WHOLE],
+        out_shape=[jax.ShapeDtypeStruct(whole.shape, whole.dtype), VMEM((8, LANES), jnp.float32)],
+        scratch_shapes=[VMEM((count, width), jnp.bfloat16), pltpu.SemaphoreType.DMA((count // FSUB,))],
+        input_output_aliases={2: 0},
+        name="finish_rows",
+        cost_estimate=cost(16 * N * count * count * width // 4),
+        compiler_params=params(8),
+    )(vmem(mine), vmem(other), whole, *after)
 
 
 def add_kernel(count, own_ref, a_ref, b_ref, c_ref, *refs):
@@ -279,7 +305,7 @@
         functools.partial(add_kernel, count),
         in_specs=[WHOLE] * 4 + [ORDER] * len(after),
         out_specs=[WHOLE] * count,
-        out_shape=[VMEM((rows // count, width), kind) for kind in kinds],
+        out_shape=[(VMEM if count > 1 else jax.ShapeDtypeStruct)((rows // count, width), kind) for kind in kinds],
         name="add",
         cost_estimate=cost(3 * 10**11),
         compiler_params=params(4),
@@ -301,24 +327,26 @@
     fs = [f256, fetch(f256, "third", 1), None, fetch(f256, "third", 3)]
 
     rs = [None] * N
-    rs[0], sums, again = residual(0, piece, pos, f256, w0, w1, b, words, jnp.float32, again=True)
+    rs[0], sums, again = residual(0, f256, w0, w1, b, words, jnp.float32, again=True)
     fs[2] = fetch(again, "third", 2)
     arrived, after = [], (sums,)
     for k in (1, 3, 2):
-        rs[k], part = residual(k, piece, pos, fs[k], w0, w1, b, words, jnp.bfloat16, after)
+        rs[k], part = residual(k, fs[k], w0, w1, b, words, jnp.bfloat16, after)
         after = (part,)
         arrived.append(push(part, "third", k))
 
     half = own // 2
-    theirs = [swap(weight_partial(rs, fs, own + s, half, x)) for s, x in zip((0, half), ((), arrived[:2]))]
-    sums, *sent = add(sums, arrived, N)
+    partial = functools.partial(weight_partial, rs, fs)
+    theirs = [partial(own, half, jnp.bfloat16, arrived[:1]), partial(own + half, half, jnp.bfloat16, arrived[1:2])]
+    mine = partial(half, half, jnp.float32, theirs)
+    theirs = [swap(x) for x in theirs]
+    sums, *sent = add(sums, arrived, N, after=(mine,))
     arrived = [push(x, "second", k) for k, x in zip((1, 2, 3), sent)]
-    weight_grad, done = weight_rows(rs, fs, 0, half, own, theirs[0], None, sent)
+    weight_grad, done = weight_rows(rs, fs, 0, half, own, theirs[0], sent)
     sums, *sent = add(sums, arrived, N, after=(done,))
     arrived = [push(x, "first", k) for k, x in zip((1, 2, 3), sent)]
-    weight_grad, _ = weight_rows(rs, fs, half, half, own, theirs[1], weight_grad, sent)
-    for x in arrived:
-        sums = sums + x.astype(jnp.float32)
+    weight_grad, done = finish_rows(mine, theirs[1], weight_grad, half, sent)
+    (sums,) = add(sums, arrived, 1, after=(done,))
     return weight_grad, sums
 
 

time: 73.5 us -> 69.2 us (0.941)
  starting transfers between devices: 31.4 us -> 27.4 us
  Pallas kernels: 30.8 us -> 28.9 us
  waiting for transfers between devices: 9.61 us -> 11.4 us
    ppermute x9, waiting for transfers between devices: 1.95 us -> 5.88 us  [fetch(): return lax.ppermute(x, AXES, shifted(stage, -k))]
    pallas_call x2 -> x1, Pallas kernels: 6.15 us -> 2.76 us  [weight_rows(): pl.pallas_call(functools.partial(weight_rows_kernel, start), in_specs=[WH...]
    ppermute x9, starting transfers between devices: 17.9 us -> 15.3 us  [fetch(): return lax.ppermute(x, AXES, shifted(stage, -k))]
    ppermute x9, waiting for transfers between devices: 6.28 us -> 4.15 us  [push(): return lax.ppermute(x, AXES, shifted(stage, k))]
    pallas_call x2 -> x3, Pallas kernels: 3.68 us -> 5.47 us  [weight_partial(): pl.pallas_call(functools.partial(weight_partial_kernel, start), in_specs=...]
    pallas_call x4 -> x5, Pallas kernels: 17.2 us -> 15.8 us  [the longest x4 14.6 us: residual(): pl.pallas_call(functools.partial(residual_kernel, chunk, again), in_specs...]
    ppermute x9, starting transfers between devices: 12.8 us -> 11.8 us  [push(): return lax.ppermute(x, AXES, shifted(stage, k))]
  transfers between devices with their start and end apart: 22 -> 22, of which waited for: 8 -> 10; matrix products, arithmetic and copies ran while one was open for 0% -> 0% of each run, Pallas kernels for 42% -> 41%
where the time goes in v3:
time: 69.2 us; the launch traced here: 68.6 us
  Pallas kernels  28.9 us (42%)
  starting transfers between devices  27.4 us (40%)
  waiting for transfers between devices  11.4 us (16%)
  between operations  0.81 us (1%)
    ppermute x9, starting transfers between devices, fetch(): return lax.ppermute(x, AXES, shifted(stage, -k))  15.3 us
    pallas_call x4, Pallas kernels, residual(): pl.pallas_call(functools.partial(residual_kernel, chunk, again), in_specs...  14.6 us
    ppermute x9, starting transfers between devices, push(): return lax.ppermute(x, AXES, shifted(stage, k))  11.8 us
    ppermute x9, waiting for transfers between devices, fetch(): return lax.ppermute(x, AXES, shifted(stage, -k))  5.88 us
    pallas_call x3, Pallas kernels, weight_partial(): pl.pallas_call(functools.partial(weight_partial_kernel, start), in_specs=...  5.47 us
    ppermute x9, waiting for transfers between devices, push(): return lax.ppermute(x, AXES, shifted(stage, k))  4.15 us
    pallas_call x1, Pallas kernels, prepare(): pl.pallas_call(functools.partial(prepare_kernel, piece), in_specs=[SCALAR...  3.23 us
    pallas_call x1, Pallas kernels, weight_rows(): pl.pallas_call(functools.partial(weight_rows_kernel, start), in_specs=[WH...  2.76 us
  transfers between devices with their start and end apart: 22, of which 10 were waited for; matrix products, arithmetic and copies ran while one was open for 0% of the time, Pallas kernels for 41%

profile of v3, /device:TPU:0, one launch (start us, length us, event | category | flops | bytes accessed | tf_op | source)
XLA Modules:
  0.0 68.6 jit_solution(6501960278739258638)
XLA Ops:
  0.6 0.1 collective-permute-start.7
  0.7 4.2 %collective-permute-start.1 = (bf16[16,768]{1,0:T(8,128)(2,1)}, bf16[16,768]{1,0:T(8,128)(2,1)S(1)}, u32[]{:S(2)}, u32[]{:S(2)}) collective-permute-start(bf16[16,768]{1,0:T(8,128)(2,1)} %x_ref.1), channel_id=1, source_target_pairs={{0,6},{1,7},{2,0},{3,1},{4,2},{5,3},{6,4},{7,5},{8,14},{9,15},{10,... | collective-permute-start | bytes 73736 | tf_op jit(solution)/shard_map/ppermute | solution.py:53
  4.9 1.3 %collective-permute-start.3 = (bf16[16,768]{1,0:T(8,128)(2,1)}, bf16[16,768]{1,0:T(8,128)(2,1)S(1)}, u32[]{:S(2)}, u32[]{:S(2)}) collective-permute-start(bf16[16,768]{1,0:T(8,128)(2,1)} %x_ref.1), channel_id=1, source_target_pairs={{0,2},{1,3},{2,4},{3,5},{4,6},{5,7},{6,0},{7,1},{8,10},{9,11},{10,... | collective-permute-start | bytes 73736 | tf_op jit(solution)/shard_map/ppermute | solution.py:53
  6.2 1.4 %collective-permute-done.refs_0_.b1_ref = f32[1,2048]{1,0:T(1,128)S(1)} collective-permute-done((f32[1,2048]{1,0:T(1,128)}, f32[1,2048]{1,0:T(1,128)S(1)}, u32[]{:S(2)}, u32[]{:S(2)}) %collective-permute-start) | collective-permute-done | bytes 8224 | tf_op jit(solution)/shard_map/ppermute | solution.py:61
  7.6 0.7 %load.1.refs_0_ = bf16[16,768]{1,0:T(8,128)(2,1)S(1)} custom-call(bf16[16,768]{1,0:T(8,128)(2,1)} %x_ref.1, f32[1,2048]{1,0:T(1,128)S(1)} %collective-permute-done.refs_0_.b1_ref), custom_call_target="tpu_custom_call" | custom-call | tf_op jit(solution)/shard_map/load/pallas_call | solution.py:139
  8.3 0.0 collective-permute-done.1.refs_1_
  8.3 2.2 %collective-permute-done.2.refs_2_ = bf16[16,768]{1,0:T(8,128)(2,1)S(1)} collective-permute-done((bf16[16,768]{1,0:T(8,128)(2,1)}, bf16[16,768]{1,0:T(8,128)(2,1)S(1)}, u32[]{:S(2)}, u32[]{:S(2)}) %collective-permute-start.2) | collective-permute-done | bytes 24608 | tf_op jit(solution)/shard_map/ppermute | solution.py:53
  10.5 3.1 %collective-permute-start.4 = (bf16[64,768]{1,0:T(8,128)(2,1)S(1)}, bf16[64,768]{1,0:T(8,128)(2,1)S(1)}, u32[]{:S(2)}, u32[]{:S(2)}) collective-permute-start(bf16[64,768]{1,0:T(8,128)(2,1)S(1)} %join.2.refs_0_), channel_id=1, source_target_pairs={{0,96},{1,25},{2,98},{3,27},{4,100},{5,29},{6,102},{7,31},{8,104},... | collective-permute-start | bytes 294920 | tf_op jit(solution)/shard_map/ppermute | solution.py:53
  13.6 0.6 collective-permute-start.5
  14.2 1.0 %collective-permute-start.6 = (bf16[64,768]{1,0:T(8,128)(2,1)S(1)}, bf16[64,768]{1,0:T(8,128)(2,1)S(1)}, u32[]{:S(2)}, u32[]{:S(2)}) collective-permute-start(bf16[64,768]{1,0:T(8,128)(2,1)S(1)} %join.2.refs_0_), channel_id=1, source_target_pairs={{0,32},{1,9},{2,34},{3,11},{4,36},{5,13},{6,38},{7,15},{8,40},{9,1... | collective-permute-start | bytes 294920 | tf_op jit(solution)/shard_map/ppermute | solution.py:53
  15.2 0.1 stack.23.pos_ref
  15.2 3.2 %prepare.1 = (bf16[2048,768]{1,0:T(8,128)(2,1)S(1)}, s32[1024,128]{1,0:T(8,128)S(1)}, f32[1,4096]{1,0:T(1,128)S(1)}) custom-call(s32[6]{0:T(128)S(1)} %stack.23.pos_ref, f32[1,2048]{1,0:T(1,128)S(1)} %collective-permute-done.refs_0_.b1_ref, bf16[2048,768]{1,0:T(8,128)(2,1)} %w_ref.1, s32[16,2048]{1,0:T(8,128)} %bitcast.8, s32[1,2048]{1,0:T(1,128)} %bitcast.11, ...), custom_call_target="tpu_custom_call" | custom-call | tf_op jit(solution)/shard_map/prepare/pallas_call | solution.py:113
  18.5 0.0 collective-permute-done.4.refs_1_
  18.5 1.3 %collective-permute-done.5.refs_2_ = bf16[64,768]{1,0:T(8,128)(2,1)S(1)} collective-permute-done((bf16[64,768]{1,0:T(8,128)(2,1)S(1)}, bf16[64,768]{1,0:T(8,128)(2,1)S(1)}, u32[]{:S(2)}, u32[]{:S(2)}) %collective-permute-start.5) | collective-permute-done | bytes 98336 | tf_op jit(solution)/shard_map/ppermute | solution.py:53
  19.8 1.0 %collective-permute-done.6.refs_3_ = bf16[64,768]{1,0:T(8,128)(2,1)S(1)} collective-permute-done((bf16[64,768]{1,0:T(8,128)(2,1)S(1)}, bf16[64,768]{1,0:T(8,128)(2,1)S(1)}, u32[]{:S(2)}, u32[]{:S(2)}) %collective-permute-start.6) | collective-permute-done | bytes 98336 | tf_op jit(solution)/shard_map/ppermute | solution.py:53
  20.8 2.8 %collective-permute-start.8 = (bf16[256,768]{1,0:T(8,128)(2,1)S(1)}, bf16[256,768]{1,0:T(8,128)(2,1)S(1)}, u32[]{:S(2)}, u32[]{:S(2)}) collective-permute-start(bf16[256,768]{1,0:T(8,128)(2,1)S(1)} %join.3.f_ref.refs_4_), channel_id=1, source_target_pairs={{0,24},{1,97},{2,26},{3,99},{4,28},{5,101},{6,30},{7,103},{8,0},{9... | collective-permute-start | bytes 1179656 | tf_op jit(solution)/shard_map/ppermute | solution.py:53
  23.6 0.0 collective-permute-start.10
  23.6 3.6 %residual.4 = (bf16[256,4096]{1,0:T(8,128)(2,1)S(1)}, f32[256,768]{1,0:T(8,128)S(1)}, bf16[256,768]{1,0:T(8,128)(2,1)S(1)}) custom-call(bf16[256,768]{1,0:T(8,128)(2,1)S(1)} %join.3.f_ref.refs_4_, bf16[2048,768]{1,0:T(8,128)(2,1)S(1)} %get-tuple-element.27.w0_ref, bf16[2048,768]{1,0:T(8,128)(2,1)S(1)} %collective-permute-done.7.w1_ref, ...), custom_call_target="tpu_custom_call" | custom-call | flops 524288 | tf_op jit(solution)/shard_map/residual/pallas_call | solution.py:193
  27.2 2.4 %collective-permute-start.9 = (bf16[256,768]{1,0:T(8,128)(2,1)S(1)}, bf16[256,768]{1,0:T(8,128)(2,1)S(1)}, u32[]{:S(2)}, u32[]{:S(2)}) collective-permute-start(bf16[256,768]{1,0:T(8,128)(2,1)S(1)} %get-tuple-element.32), channel_id=1, source_target_pairs={{0,16},{1,65},{2,18},{3,67},{4,20},{5,69},{6,22},{7,71},{8,24},{9,... | collective-permute-start | bytes 1179656 | tf_op jit(solution)/shard_map/ppermute | solution.py:53
  29.6 3.6 %residual.5 = (bf16[256,4096]{1,0:T(8,128)(2,1)S(1)}, bf16[256,768]{1,0:T(8,128)(2,1)S(1)}) custom-call(bf16[256,768]{1,0:T(8,128)(2,1)S(1)} %collective-permute-done.8.f_ref.refs_5_, bf16[2048,768]{1,0:T(8,128)(2,1)S(1)} %get-tuple-element.27.w0_ref, bf16[2048,768]{1,0:T(8,128)(2,1)S(1)} %collective-permute-done.7.w1_ref, ...), custom_call_target="tpu_custom_call" | custom-call | flops 524288 | tf_op jit(solution)/shard_map/residual/pallas_call | solution.py:193
  33.3 2.0 %collective-permute-start.11 = (bf16[256,768]{1,0:T(8,128)(2,1)S(1)}, bf16[256,768]{1,0:T(8,128)(2,1)S(1)}, u32[]{:S(2)}, u32[]{:S(2)}) collective-permute-start(bf16[256,768]{1,0:T(8,128)(2,1)S(1)} %get-tuple-element.33.refs_0_), channel_id=1, source_target_pairs={{0,8},{1,33},{2,10},{3,35},{4,12},{5,37},{6,14},{7,39},{8,16},{9,4... | collective-permute-start | bytes 1179656 | tf_op jit(solution)/shard_map/ppermute | solution.py:57
  35.3 1.5 %collective-permute-done.10.f_ref.refs_7_ = bf16[256,768]{1,0:T(8,128)(2,1)S(1)} collective-permute-done((bf16[256,768]{1,0:T(8,128)(2,1)S(1)}, bf16[256,768]{1,0:T(8,128)(2,1)S(1)}, u32[]{:S(2)}, u32[]{:S(2)}) %collective-permute-start.10) | collective-permute-done | bytes 393248 | tf_op jit(solution)/shard_map/ppermute | solution.py:53
  36.8 3.6 %residual.6 = (bf16[256,4096]{1,0:T(8,128)(2,1)S(1)}, bf16[256,768]{1,0:T(8,128)(2,1)S(1)}) custom-call(bf16[256,768]{1,0:T(8,128)(2,1)S(1)} %collective-permute-done.10.f_ref.refs_7_, bf16[2048,768]{1,0:T(8,128)(2,1)S(1)} %get-tuple-element.27.w0_ref, bf16[2048,768]{1,0:T(8,128)(2,1)S(1)} %collective-permute-done.7.w1_ref, ...), custom_call_target="tpu_custom_call" | custom-call | flops 524288 | tf_op jit(solution)/shard_map/residual/pallas_call | solution.py:193
  40.4 0.1 collective-permute-start.12
  40.5 3.6 %residual.7 = (bf16[256,4096]{1,0:T(8,128)(2,1)S(1)}, bf16[256,768]{1,0:T(8,128)(2,1)S(1)}) custom-call(bf16[256,768]{1,0:T(8,128)(2,1)S(1)} %collective-permute-done.9.f_ref.refs_6_, bf16[2048,768]{1,0:T(8,128)(2,1)S(1)} %get-tuple-element.27.w0_ref, bf16[2048,768]{1,0:T(8,128)(2,1)S(1)} %collective-permute-done.7.w1_ref, ...), custom_call_target="tpu_custom_call" | custom-call | flops 524288 | tf_op jit(solution)/shard_map/residual/pallas_call | solution.py:193
  44.2 1.2 %collective-permute-start.15 = (bf16[256,768]{1,0:T(8,128)(2,1)S(1)}, bf16[256,768]{1,0:T(8,128)(2,1)S(1)}, u32[]{:S(2)}, u32[]{:S(2)}) collective-permute-start(bf16[256,768]{1,0:T(8,128)(2,1)S(1)} %get-tuple-element.37), channel_id=1, source_target_pairs={{0,16},{1,65},{2,18},{3,67},{4,20},{5,69},{6,22},{7,71},{8,24},{9,... | collective-permute-start | bytes 1179656 | tf_op jit(solution)/shard_map/ppermute | solution.py:57
  45.4 1.8 %weight_partial.3.refs_8_ = bf16[1024,768]{1,0:T(8,128)(2,1)S(1)} custom-call(bf16[256,4096]{1,0:T(8,128)(2,1)S(1)} %get-tuple-element.29.refs_0_, bf16[256,4096]{1,0:T(8,128)(2,1)S(1)} %get-tuple-element.31.refs_1_, bf16[256,4096]{1,0:T(8,128)(2,1)S(1)} %get-tuple-element.35.refs_2_, bf16[256,4096]{1,0:T(8,128)(2,1)S(1)} %get-tuple-element.36.refs_3_, ...), custom_call_target="tpu_custom_call" | custom-call | flops 65536 | tf_op jit(solution)/shard_map/weight_partial/pallas_call | solution.py:215
  47.2 0.1 collective-permute-start.14
  47.3 0.9 %collective-permute-done.12.refs_8_.b_ref = bf16[256,768]{1,0:T(8,128)(2,1)S(1)} collective-permute-done((bf16[256,768]{1,0:T(8,128)(2,1)S(1)}, bf16[256,768]{1,0:T(8,128)(2,1)S(1)}, u32[]{:S(2)}, u32[]{:S(2)}) %collective-permute-start.12) | collective-permute-done | bytes 393248 | tf_op jit(solution)/shard_map/ppermute | solution.py:57
  48.3 1.8 %weight_partial.4.refs_9_ = bf16[1024,768]{1,0:T(8,128)(2,1)S(1)} custom-call(bf16[256,4096]{1,0:T(8,128)(2,1)S(1)} %get-tuple-element.29.refs_0_, bf16[256,4096]{1,0:T(8,128)(2,1)S(1)} %get-tuple-element.31.refs_1_, bf16[256,4096]{1,0:T(8,128)(2,1)S(1)} %get-tuple-element.35.refs_2_, bf16[256,4096]{1,0:T(8,128)(2,1)S(1)} %get-tuple-element.36.refs_3_, ...), custom_call_target="tpu_custom_call" | custom-call | flops 65536 | tf_op jit(solution)/shard_map/weight_partial/pallas_call | solution.py:215
  50.1 0.1 collective-permute-start.13
  50.2 1.8 %weight_partial.5.refs_0_.mine_ref = f32[1024,768]{1,0:T(8,128)S(1)} custom-call(bf16[256,4096]{1,0:T(8,128)(2,1)S(1)} %get-tuple-element.29.refs_0_, bf16[256,4096]{1,0:T(8,128)(2,1)S(1)} %get-tuple-element.31.refs_1_, bf16[256,4096]{1,0:T(8,128)(2,1)S(1)} %get-tuple-element.35.refs_2_, bf16[256,4096]{1,0:T(8,128)(2,1)S(1)} %get-tuple-element.36.refs_3_, ...), custom_call_target="tpu_custom_call" | custom-call | flops 65536 | tf_op jit(solution)/shard_map/weight_partial/pallas_call | solution.py:215
  52.0 1.5 %collective-permute-done.15.c_ref = bf16[256,768]{1,0:T(8,128)(2,1)S(1)} collective-permute-done((bf16[256,768]{1,0:T(8,128)(2,1)S(1)}, bf16[256,768]{1,0:T(8,128)(2,1)S(1)}, u32[]{:S(2)}, u32[]{:S(2)}) %collective-permute-start.15) | collective-permute-done | bytes 393248 | tf_op jit(solution)/shard_map/ppermute | solution.py:57
  53.5 0.2 add.23
  53.7 0.1 collective-permute-start.16
  53.8 2.0 %collective-permute-start.17 = (bf16[64,768]{1,0:T(8,128)(2,1)S(1)}, bf16[64,768]{1,0:T(8,128)(2,1)S(1)}, u32[]{:S(2)}, u32[]{:S(2)}) collective-permute-start(bf16[64,768]{1,0:T(8,128)(2,1)S(1)} %get-tuple-element.39.refs_10_), channel_id=1, source_target_pairs={{0,64},{1,17},{2,66},{3,19},{4,68},{5,21},{6,70},{7,23},{8,72},{9,... | collective-permute-start | bytes 294920 | tf_op jit(solution)/shard_map/ppermute | solution.py:57
  55.8 1.6 %collective-permute-start.18 = (bf16[64,768]{1,0:T(8,128)(2,1)S(1)}, bf16[64,768]{1,0:T(8,128)(2,1)S(1)}, u32[]{:S(2)}, u32[]{:S(2)}) collective-permute-start(bf16[64,768]{1,0:T(8,128)(2,1)S(1)} %get-tuple-element.40.refs_11_), channel_id=1, source_target_pairs={{0,96},{1,25},{2,98},{3,27},{4,100},{5,29},{6,102},{7,31},{8,104},... | collective-permute-start | bytes 294920 | tf_op jit(solution)/shard_map/ppermute | solution.py:57
  57.4 0.0 collective-permute-done.14.refs_8_
  57.4 2.8 %weight_rows.1 = (bf16[2048,768]{1,0:T(8,128)(2,1)}, f32[8,128]{1,0:T(8,128)S(1)}) custom-call(bf16[256,4096]{1,0:T(8,128)(2,1)S(1)} %get-tuple-element.29.refs_0_, bf16[256,4096]{1,0:T(8,128)(2,1)S(1)} %get-tuple-element.31.refs_1_, bf16[256,4096]{1,0:T(8,128)(2,1)S(1)} %get-tuple-element.35.refs_2_, bf16[256,4096]{1,0:T(8,128)(2,1)S(1)} %get-tuple-element.36.refs_3_, ...), custom_call_target="tpu_custom_call" | custom-call | flops 1610612736 | tf_op jit(solution)/shard_map/weight_rows/pallas_call | solution.py:248
  60.2 0.5 collective-permute-done.16.a_ref
  60.7 0.9 %collective-permute-done.18.c_ref = bf16[64,768]{1,0:T(8,128)(2,1)S(1)} collective-permute-done((bf16[64,768]{1,0:T(8,128)(2,1)S(1)}, bf16[64,768]{1,0:T(8,128)(2,1)S(1)}, u32[]{:S(2)}, u32[]{:S(2)}) %collective-permute-start.18) | collective-permute-done | bytes 98336 | tf_op jit(solution)/shard_map/ppermute | solution.py:57
  61.6 0.2 collective-permute-start.19
  61.7 2.4 %collective-permute-start.20 = (bf16[16,768]{1,0:T(8,128)(2,1)S(1)}, bf16[16,768]{1,0:T(8,128)(2,1)S(1)}, u32[]{:S(2)}, u32[]{:S(2)}) collective-permute-start(bf16[16,768]{1,0:T(8,128)(2,1)S(1)} %get-tuple-element.45.refs_2_), channel_id=1, source_target_pairs={{0,4},{1,5},{2,6},{3,7},{4,0},{5,1},{6,2},{7,3},{8,12},{9,13},{10,... | collective-permute-start | bytes 73736 | tf_op jit(solution)/shard_map/ppermute | solution.py:57
  64.1 2.2 %collective-permute-start.21 = (bf16[16,768]{1,0:T(8,128)(2,1)S(1)}, bf16[16,768]{1,0:T(8,128)(2,1)S(1)}, u32[]{:S(2)}, u32[]{:S(2)}) collective-permute-start(bf16[16,768]{1,0:T(8,128)(2,1)S(1)} %get-tuple-element.46.refs_3_), channel_id=1, source_target_pairs={{0,6},{1,7},{2,0},{3,1},{4,2},{5,3},{6,4},{7,5},{8,14},{9,15},{10,... | collective-permute-start | bytes 73736 | tf_op jit(solution)/shard_map/ppermute | solution.py:57
  66.4 1.2 %finish_rows.1 = (bf16[2048,768]{1,0:T(8,128)(2,1)}, f32[8,128]{1,0:T(8,128)S(1)}) custom-call(f32[1024,768]{1,0:T(8,128)S(1)} %weight_partial.5.refs_0_.mine_ref, bf16[1024,768]{1,0:T(8,128)(2,1)S(1)} %collective-permute-done.13.other_ref, bf16[2048,768]{1,0:T(8,128)(2,1)} %get-tuple-element.41.refs_0_, ...), custom_call_target="tpu_custom_call", output_to_operand_aliasing={{0}: (2, {})} | custom-call | flops 1610612736 | tf_op jit(solution)/shard_map/finish_rows/pallas_call | solution.py:277
  67.6 0.0 collective-permute-done.19.a_ref
  67.6 0.3 collective-permute-done.21.c_ref
  67.9 0.6 add.25
  (13 shorter events, 0.1 us)
Async XLA Ops:
  0.6 23.0 %collective-permute-start.7 = (bf16[2048,768]{1,0:T(8,128)(2,1)}, bf16[2048,768]{1,0:T(8,128)(2,1)S(1)}, u32[]{:S(2)}, u32[]{:S(2)}) collective-permute-start(bf16[2048,768]{1,0:T(8,128)(2,1)} %w_ref.1), channel_id=1, source_target_pairs={{0,1},{1,0},{2,3},{3,2},{4,5},{5,4},{6,7},{7,6},{8,9},{9,8},{10,11... | collective-permute-start | bytes 9437192 | tf_op jit(solution)/shard_map/ppermute | solution.py:61
  0.7 7.6 %collective-permute-start.1 = (bf16[16,768]{1,0:T(8,128)(2,1)}, bf16[16,768]{1,0:T(8,128)(2,1)S(1)}, u32[]{:S(2)}, u32[]{:S(2)}) collective-permute-start(bf16[16,768]{1,0:T(8,128)(2,1)} %x_ref.1), channel_id=1, source_target_pairs={{0,6},{1,7},{2,0},{3,1},{4,2},{5,3},{6,4},{7,5},{8,14},{9,15},{10,... | collective-permute-start | bytes 73736 | tf_op jit(solution)/shard_map/ppermute | solution.py:53
  4.9 5.5 %collective-permute-start.2 = (bf16[16,768]{1,0:T(8,128)(2,1)}, bf16[16,768]{1,0:T(8,128)(2,1)S(1)}, u32[]{:S(2)}, u32[]{:S(2)}) collective-permute-start(bf16[16,768]{1,0:T(8,128)(2,1)} %x_ref.1), channel_id=1, source_target_pairs={{0,4},{1,5},{2,6},{3,7},{4,0},{5,1},{6,2},{7,3},{8,12},{9,13},{10,... | collective-permute-start | bytes 73736 | tf_op jit(solution)/shard_map/ppermute | solution.py:53
  4.9 5.5 %collective-permute-start.3 = (bf16[16,768]{1,0:T(8,128)(2,1)}, bf16[16,768]{1,0:T(8,128)(2,1)S(1)}, u32[]{:S(2)}, u32[]{:S(2)}) collective-permute-start(bf16[16,768]{1,0:T(8,128)(2,1)} %x_ref.1), channel_id=1, source_target_pairs={{0,2},{1,3},{2,4},{3,5},{4,6},{5,7},{6,0},{7,1},{8,10},{9,11},{10,... | collective-permute-start | bytes 73736 | tf_op jit(solution)/shard_map/ppermute | solution.py:53
  6.2 1.4 %collective-permute-start = (f32[1,2048]{1,0:T(1,128)}, f32[1,2048]{1,0:T(1,128)S(1)}, u32[]{:S(2)}, u32[]{:S(2)}) collective-permute-start(f32[1,2048]{1,0:T(1,128)} %bitcast.9), channel_id=1, source_target_pairs={{0,1},{1,0},{2,3},{3,2},{4,5},{5,4},{6,7},{7,6},{8,9},{9,8},{10,11... | collective-permute-start | bytes 24584 | tf_op jit(solution)/shard_map/ppermute | solution.py:61
  10.5 8.0 %collective-permute-start.4 = (bf16[64,768]{1,0:T(8,128)(2,1)S(1)}, bf16[64,768]{1,0:T(8,128)(2,1)S(1)}, u32[]{:S(2)}, u32[]{:S(2)}) collective-permute-start(bf16[64,768]{1,0:T(8,128)(2,1)S(1)} %join.2.refs_0_), channel_id=1, source_target_pairs={{0,96},{1,25},{2,98},{3,27},{4,100},{5,29},{6,102},{7,31},{8,104},... | collective-permute-start | bytes 294920 | tf_op jit(solution)/shard_map/ppermute | solution.py:53
  13.6 6.2 %collective-permute-start.5 = (bf16[64,768]{1,0:T(8,128)(2,1)S(1)}, bf16[64,768]{1,0:T(8,128)(2,1)S(1)}, u32[]{:S(2)}, u32[]{:S(2)}) collective-permute-start(bf16[64,768]{1,0:T(8,128)(2,1)S(1)} %join.2.refs_0_), channel_id=1, source_target_pairs={{0,64},{1,17},{2,66},{3,19},{4,68},{5,21},{6,70},{7,23},{8,72},{9,... | collective-permute-start | bytes 294920 | tf_op jit(solution)/shard_map/ppermute | solution.py:53
  14.2 6.5 %collective-permute-start.6 = (bf16[64,768]{1,0:T(8,128)(2,1)S(1)}, bf16[64,768]{1,0:T(8,128)(2,1)S(1)}, u32[]{:S(2)}, u32[]{:S(2)}) collective-permute-start(bf16[64,768]{1,0:T(8,128)(2,1)S(1)} %join.2.refs_0_), channel_id=1, source_target_pairs={{0,32},{1,9},{2,34},{3,11},{4,36},{5,13},{6,38},{7,15},{8,40},{9,1... | collective-permute-start | bytes 294920 | tf_op jit(solution)/shard_map/ppermute | solution.py:53
  20.8 8.9 %collective-permute-start.8 = (bf16[256,768]{1,0:T(8,128)(2,1)S(1)}, bf16[256,768]{1,0:T(8,128)(2,1)S(1)}, u32[]{:S(2)}, u32[]{:S(2)}) collective-permute-start(bf16[256,768]{1,0:T(8,128)(2,1)S(1)} %join.3.f_ref.refs_4_), channel_id=1, source_target_pairs={{0,24},{1,97},{2,26},{3,99},{4,28},{5,101},{6,30},{7,103},{8,0},{9... | collective-permute-start | bytes 1179656 | tf_op jit(solution)/shard_map/ppermute | solution.py:53
  23.6 13.2 %collective-permute-start.10 = (bf16[256,768]{1,0:T(8,128)(2,1)S(1)}, bf16[256,768]{1,0:T(8,128)(2,1)S(1)}, u32[]{:S(2)}, u32[]{:S(2)}) collective-permute-start(bf16[256,768]{1,0:T(8,128)(2,1)S(1)} %join.3.f_ref.refs_4_), channel_id=1, source_target_pairs={{0,8},{1,33},{2,10},{3,35},{4,12},{5,37},{6,14},{7,39},{8,16},{9,4... | collective-permute-start | bytes 1179656 | tf_op jit(solution)/shard_map/ppermute | solution.py:53
  27.2 13.3 %collective-permute-start.9 = (bf16[256,768]{1,0:T(8,128)(2,1)S(1)}, bf16[256,768]{1,0:T(8,128)(2,1)S(1)}, u32[]{:S(2)}, u32[]{:S(2)}) collective-permute-start(bf16[256,768]{1,0:T(8,128)(2,1)S(1)} %get-tuple-element.32), channel_id=1, source_target_pairs={{0,16},{1,65},{2,18},{3,67},{4,20},{5,69},{6,22},{7,71},{8,24},{9,... | collective-permute-start | bytes 1179656 | tf_op jit(solution)/shard_map/ppermute | solution.py:53
  33.3 12.2 %collective-permute-start.11 = (bf16[256,768]{1,0:T(8,128)(2,1)S(1)}, bf16[256,768]{1,0:T(8,128)(2,1)S(1)}, u32[]{:S(2)}, u32[]{:S(2)}) collective-permute-start(bf16[256,768]{1,0:T(8,128)(2,1)S(1)} %get-tuple-element.33.refs_0_), channel_id=1, source_target_pairs={{0,8},{1,33},{2,10},{3,35},{4,12},{5,37},{6,14},{7,39},{8,16},{9,4... | collective-permute-start | bytes 1179656 | tf_op jit(solution)/shard_map/ppermute | solution.py:57
  40.4 7.8 %collective-permute-start.12 = (bf16[256,768]{1,0:T(8,128)(2,1)S(1)}, bf16[256,768]{1,0:T(8,128)(2,1)S(1)}, u32[]{:S(2)}, u32[]{:S(2)}) collective-permute-start(bf16[256,768]{1,0:T(8,128)(2,1)S(1)} %get-tuple-element.34.refs_0_), channel_id=1, source_target_pairs={{0,24},{1,97},{2,26},{3,99},{4,28},{5,101},{6,30},{7,103},{8,0},{9... | collective-permute-start | bytes 1179656 | tf_op jit(solution)/shard_map/ppermute | solution.py:57
  44.2 9.4 %collective-permute-start.15 = (bf16[256,768]{1,0:T(8,128)(2,1)S(1)}, bf16[256,768]{1,0:T(8,128)(2,1)S(1)}, u32[]{:S(2)}, u32[]{:S(2)}) collective-permute-start(bf16[256,768]{1,0:T(8,128)(2,1)S(1)} %get-tuple-element.37), channel_id=1, source_target_pairs={{0,16},{1,65},{2,18},{3,67},{4,20},{5,69},{6,22},{7,71},{8,24},{9,... | collective-permute-start | bytes 1179656 | tf_op jit(solution)/shard_map/ppermute | solution.py:57
  47.2 10.1 %collective-permute-start.14 = (bf16[1024,768]{1,0:T(8,128)(2,1)S(1)}, bf16[1024,768]{1,0:T(8,128)(2,1)S(1)}, u32[]{:S(2)}, u32[]{:S(2)}) collective-permute-start(bf16[1024,768]{1,0:T(8,128)(2,1)S(1)} %weight_partial.3.refs_8_), channel_id=1, source_target_pairs={{0,1},{1,0},{2,3},{3,2},{4,5},{5,4},{6,7},{7,6},{8,9},{9,8},{10,11... | collective-permute-start | bytes 4718600 | tf_op jit(solution)/shard_map/ppermute | solution.py:61
  50.1 16.2 %collective-permute-start.13 = (bf16[1024,768]{1,0:T(8,128)(2,1)S(1)}, bf16[1024,768]{1,0:T(8,128)(2,1)S(1)}, u32[]{:S(2)}, u32[]{:S(2)}) collective-permute-start(bf16[1024,768]{1,0:T(8,128)(2,1)S(1)} %weight_partial.4.refs_9_), channel_id=1, source_target_pairs={{0,1},{1,0},{2,3},{3,2},{4,5},{5,4},{6,7},{7,6},{8,9},{9,8},{10,11... | collective-permute-start | bytes 4718600 | tf_op jit(solution)/shard_map/ppermute | solution.py:61
  53.7 6.9 %collective-permute-start.16 = (bf16[64,768]{1,0:T(8,128)(2,1)S(1)}, bf16[64,768]{1,0:T(8,128)(2,1)S(1)}, u32[]{:S(2)}, u32[]{:S(2)}) collective-permute-start(bf16[64,768]{1,0:T(8,128)(2,1)S(1)} %get-tuple-element.38.refs_9_), channel_id=1, source_target_pairs={{0,32},{1,9},{2,34},{3,11},{4,36},{5,13},{6,38},{7,15},{8,40},{9,1... | collective-permute-start | bytes 294920 | tf_op jit(solution)/shard_map/ppermute | solution.py:57
  53.8 6.9 %collective-permute-start.17 = (bf16[64,768]{1,0:T(8,128)(2,1)S(1)}, bf16[64,768]{1,0:T(8,128)(2,1)S(1)}, u32[]{:S(2)}, u32[]{:S(2)}) collective-permute-start(bf16[64,768]{1,0:T(8,128)(2,1)S(1)} %get-tuple-element.39.refs_10_), channel_id=1, source_target_pairs={{0,64},{1,17},{2,66},{3,19},{4,68},{5,21},{6,70},{7,23},{8,72},{9,... | collective-permute-start | bytes 294920 | tf_op jit(solution)/shard_map/ppermute | solution.py:57
  55.8 5.7 %collective-permute-start.18 = (bf16[64,768]{1,0:T(8,128)(2,1)S(1)}, bf16[64,768]{1,0:T(8,128)(2,1)S(1)}, u32[]{:S(2)}, u32[]{:S(2)}) collective-permute-start(bf16[64,768]{1,0:T(8,128)(2,1)S(1)} %get-tuple-element.40.refs_11_), channel_id=1, source_target_pairs={{0,96},{1,25},{2,98},{3,27},{4,100},{5,29},{6,102},{7,31},{8,104},... | collective-permute-start | bytes 294920 | tf_op jit(solution)/shard_map/ppermute | solution.py:57
  61.6 6.0 %collective-permute-start.19 = (bf16[16,768]{1,0:T(8,128)(2,1)S(1)}, bf16[16,768]{1,0:T(8,128)(2,1)S(1)}, u32[]{:S(2)}, u32[]{:S(2)}) collective-permute-start(bf16[16,768]{1,0:T(8,128)(2,1)S(1)} %get-tuple-element.44.refs_1_), channel_id=1, source_target_pairs={{0,2},{1,3},{2,4},{3,5},{4,6},{5,7},{6,0},{7,1},{8,10},{9,11},{10,... | collective-permute-start | bytes 73736 | tf_op jit(solution)/shard_map/ppermute | solution.py:57
  61.7 5.9 %collective-permute-start.20 = (bf16[16,768]{1,0:T(8,128)(2,1)S(1)}, bf16[16,768]{1,0:T(8,128)(2,1)S(1)}, u32[]{:S(2)}, u32[]{:S(2)}) collective-permute-start(bf16[16,768]{1,0:T(8,128)(2,1)S(1)} %get-tuple-element.45.refs_2_), channel_id=1, source_target_pairs={{0,4},{1,5},{2,6},{3,7},{4,0},{5,1},{6,2},{7,3},{8,12},{9,13},{10,... | collective-permute-start | bytes 73736 | tf_op jit(solution)/shard_map/ppermute | solution.py:57
  64.1 3.8 %collective-permute-start.21 = (bf16[16,768]{1,0:T(8,128)(2,1)S(1)}, bf16[16,768]{1,0:T(8,128)(2,1)S(1)}, u32[]{:S(2)}, u32[]{:S(2)}) collective-permute-start(bf16[16,768]{1,0:T(8,128)(2,1)S(1)} %get-tuple-element.46.refs_3_), channel_id=1, source_target_pairs={{0,6},{1,7},{2,0},{3,1},{4,2},{5,3},{6,4},{7,5},{8,14},{9,15},{10,... | collective-permute-start | bytes 73736 | tf_op jit(solution)/shard_map/ppermute | solution.py:57

commit v4 on v3

--- a/solution.py
+++ b/solution.py
@@ -40,6 +40,25 @@
 STAGES = {"first": ("z", "z"), "second": ("y", "x"), "third": ("x", "y")}
 
 
+def along(stage, core, chip):
+    place = {axis: chip // (step // 2) % N for axis, step in STRIDE.items()}
+    axes = STAGES[stage]
+    return jnp.where(core == 0, place[axes[0]], place[axes[1]])
+
+
+def partners(stage, k):
+    pairs = []
+    for d in range(2 * N * N * N):
+        step = STRIDE[STAGES[stage][d % 2]]
+        at = d // step % N
+        pairs.append((d, d + ((at ^ k) - at) * step))
+    return pairs
+
+
+def exchange(x, stage, k):
+    return lax.ppermute(x, AXES, partners(stage, k))
+
+
 def shifted(stage, k):
     pairs = []
     for d in range(2 * N * N * N):
@@ -73,7 +92,7 @@
     slots, queries = ids_ref.shape
     row = lax.broadcasted_iota(jnp.int32, (8, LANES), 0)
     slot = lax.broadcasted_iota(jnp.int32, (slots, LANES), 0)
-    third, second, first = pos_ref[3], pos_ref[4], pos_ref[5]
+    first, second, third = pos_ref[3], pos_ref[4], pos_ref[5]
     lane = lax.broadcasted_iota(jnp.int32, (slots, LANES), 1)
     kept = (lane // piece) % 2 == core
     shift = jnp.where(core == 0, piece, LANES - piece)
@@ -99,10 +118,9 @@
         for place in range(LANES // piece):
             near = place % 2 == core
             chip = q // (2 * piece) + place // 2 + jnp.where(near, 0, N)
-            y, x, z = chip // (N * N), chip // N % N, chip % N
-            at3 = (jnp.where(core == 0, x, y) - third + N) % N
-            at2 = (jnp.where(core == 0, y, x) - second + N) % N
-            row_at = ((at3 * N + at2) * N + (z - first + N) % N) * piece
+            at1, at2, at3 = (along(stage, core, chip) for stage in STAGES)
+            at1, at2, at3 = (at1 - first + N) % N, (at2 - second + N) % N, at3 ^ third
+            row_at = ((at3 * N + at2) * N + at1) * piece
             words_out[pl.ds(pl.multiple_of(row_at, piece), piece), :] = words[place * piece : (place + 1) * piece, :]
     copies[2].wait()
     half_out[...] = 0.5 * jnp.concatenate([b0_ref[...], b1_ref[...]], axis=1)
@@ -316,24 +334,27 @@
     own, width = label_weight.shape
     piece = features.shape[0]
     me = lax.axis_index(AXES)
-    core, z, x, y = me % 2, me // 2 % N, me // 8 % N, me // 32
-    pos = jnp.stack([core, me // 2 * 2 * own, own, jnp.where(core == 0, x, y), jnp.where(core == 0, y, x), z])
+    core, chip = me % 2, me // 2
+    pos = jnp.stack([core, chip * 2 * own, own] + [along(stage, core, chip) for stage in STAGES])
 
     b0 = label_bias.reshape(1, own)
-    w1, b1 = swap(label_weight), swap(b0)
-    f64 = join([load(features, (b1,))] + [fetch(features, "first", k) for k in (1, 2, 3)], factor=0.5)
+    b1 = swap(b0)
+    near = [fetch(features, "first", k) for k in (1, 2, 3)]
+    f64 = join([load(features, (b1,))] + near, factor=0.5)
+    late, f64 = lax.optimization_barrier((label_weight, f64))
+    w1 = swap(late)
     w0, words, b = prepare(piece, pos, label_weight, positive_ids.T, positive_counts.reshape(1, -1), b0, b1, after=(f64,))
     f256 = join([f64] + [fetch(f64, "second", k) for k in (1, 2, 3)], after=(words,))
-    fs = [f256, fetch(f256, "third", 1), None, fetch(f256, "third", 3)]
+    fs = [f256, exchange(f256, "third", 1), None, exchange(f256, "third", 3)]
 
     rs = [None] * N
     rs[0], sums, again = residual(0, f256, w0, w1, b, words, jnp.float32, again=True)
-    fs[2] = fetch(again, "third", 2)
+    fs[2] = exchange(again, "third", 2)
     arrived, after = [], (sums,)
     for k in (1, 3, 2):
         rs[k], part = residual(k, fs[k], w0, w1, b, words, jnp.bfloat16, after)
         after = (part,)
-        arrived.append(push(part, "third", k))
+        arrived.append(exchange(part, "third", k))
 
     half = own // 2
     partial = functools.partial(weight_partial, rs, fs)

time: 69.2 us -> 68 us (0.983)
  waiting for transfers between devices: 11.4 us -> 10.4 us
    ppermute x0 -> x6, starting transfers between devices: none -> 8.92 us  [exchange(): return lax.ppermute(x, AXES, partners(stage, k))]
    ppermute x9 -> x6, starting transfers between devices: 15.3 us -> 10.1 us  [fetch(): return lax.ppermute(x, AXES, shifted(stage, -k))]
    ppermute x9 -> x6, starting transfers between devices: 11.8 us -> 8.39 us  [push(): return lax.ppermute(x, AXES, shifted(stage, k))]
    ppermute x0 -> x6, waiting for transfers between devices: none -> 2.95 us  [exchange(): return lax.ppermute(x, AXES, partners(stage, k))]
    ppermute x9 -> x6, waiting for transfers between devices: 4.15 us -> 1.62 us  [push(): return lax.ppermute(x, AXES, shifted(stage, k))]
    ppermute x9 -> x6, waiting for transfers between devices: 5.88 us -> 4.46 us  [fetch(): return lax.ppermute(x, AXES, shifted(stage, -k))]
  transfers between devices with their start and end apart: 22 -> 22, of which waited for: 10 -> 9; matrix products, arithmetic and copies ran while one was open for 0% -> 0% of each run, Pallas kernels for 41% -> 42%
where the time goes in v4:
time: 68 us; the launch traced here: 67.8 us
  Pallas kernels  28.8 us (42%)
  starting transfers between devices  27.7 us (41%)
  waiting for transfers between devices  10.4 us (15%)
  between operations  0.79 us (1%)
    pallas_call x4, Pallas kernels, residual(): pl.pallas_call(functools.partial(residual_kernel, chunk, again), in_specs...  14.6 us
    ppermute x6, starting transfers between devices, fetch(): return lax.ppermute(x, AXES, shifted(stage, -k))  10.1 us
    ppermute x6, starting transfers between devices, exchange(): return lax.ppermute(x, AXES, partners(stage, k))  8.92 us
    ppermute x6, starting transfers between devices, push(): return lax.ppermute(x, AXES, shifted(stage, k))  8.39 us
    pallas_call x3, Pallas kernels, weight_partial(): pl.pallas_call(functools.partial(weight_partial_kernel, start), in_specs=...  5.47 us
    ppermute x6, waiting for transfers between devices, fetch(): return lax.ppermute(x, AXES, shifted(stage, -k))  4.46 us
    pallas_call x1, Pallas kernels, prepare(): pl.pallas_call(functools.partial(prepare_kernel, piece), in_specs=[SCALAR...  3.18 us
    ppermute x6, waiting for transfers between devices, exchange(): return lax.ppermute(x, AXES, partners(stage, k))  2.95 us
  transfers between devices with their start and end apart: 22, of which 9 were waited for; matrix products, arithmetic and copies ran while one was open for 0% of the time, Pallas kernels for 42%

profile of v4, /device:TPU:0, one launch (start us, length us, event | category | flops | bytes accessed | tf_op | source)
XLA Modules:
  0.0 67.8 jit_solution(14382804830711875202)
XLA Ops:
  0.6 4.2 %collective-permute-start.1 = (bf16[16,768]{1,0:T(8,128)(2,1)}, bf16[16,768]{1,0:T(8,128)(2,1)S(1)}, u32[]{:S(2)}, u32[]{:S(2)}) collective-permute-start(bf16[16,768]{1,0:T(8,128)(2,1)} %x_ref.1), channel_id=1, source_target_pairs={{0,6},{1,7},{2,0},{3,1},{4,2},{5,3},{6,4},{7,5},{8,14},{9,15},{10,... | collective-permute-start | bytes 73736 | tf_op jit(solution)/shard_map/ppermute | solution.py:72
  4.8 1.3 %collective-permute-start.3 = (bf16[16,768]{1,0:T(8,128)(2,1)}, bf16[16,768]{1,0:T(8,128)(2,1)S(1)}, u32[]{:S(2)}, u32[]{:S(2)}) collective-permute-start(bf16[16,768]{1,0:T(8,128)(2,1)} %x_ref.1), channel_id=1, source_target_pairs={{0,2},{1,3},{2,4},{3,5},{4,6},{5,7},{6,0},{7,1},{8,10},{9,11},{10,... | collective-permute-start | bytes 73736 | tf_op jit(solution)/shard_map/ppermute | solution.py:72
  6.1 1.4 %collective-permute-done.refs_0_.b1_ref = f32[1,2048]{1,0:T(1,128)S(1)} collective-permute-done((f32[1,2048]{1,0:T(1,128)}, f32[1,2048]{1,0:T(1,128)S(1)}, u32[]{:S(2)}, u32[]{:S(2)}) %collective-permute-start) | collective-permute-done | bytes 8224 | tf_op jit(solution)/shard_map/ppermute | solution.py:80
  7.5 0.7 %load.1.refs_0_ = bf16[16,768]{1,0:T(8,128)(2,1)S(1)} custom-call(bf16[16,768]{1,0:T(8,128)(2,1)} %x_ref.1, f32[1,2048]{1,0:T(1,128)S(1)} %collective-permute-done.refs_0_.b1_ref), custom_call_target="tpu_custom_call" | custom-call | tf_op jit(solution)/shard_map/load/pallas_call | solution.py:157
  8.2 0.0 collective-permute-done.1.refs_1_
  8.2 2.2 %collective-permute-done.2.refs_2_ = bf16[16,768]{1,0:T(8,128)(2,1)S(1)} collective-permute-done((bf16[16,768]{1,0:T(8,128)(2,1)}, bf16[16,768]{1,0:T(8,128)(2,1)S(1)}, u32[]{:S(2)}, u32[]{:S(2)}) %collective-permute-start.2) | collective-permute-done | bytes 24608 | tf_op jit(solution)/shard_map/ppermute | solution.py:72
  10.4 0.0 collective-permute-done.3.refs_3_
  10.4 0.1 collective-permute-start.7
  10.5 3.1 %collective-permute-start.4 = (bf16[64,768]{1,0:T(8,128)(2,1)S(1)}, bf16[64,768]{1,0:T(8,128)(2,1)S(1)}, u32[]{:S(2)}, u32[]{:S(2)}) collective-permute-start(bf16[64,768]{1,0:T(8,128)(2,1)S(1)} %join.2.refs_0_), channel_id=1, source_target_pairs={{0,96},{1,25},{2,98},{3,27},{4,100},{5,29},{6,102},{7,31},{8,104},... | collective-permute-start | bytes 294920 | tf_op jit(solution)/shard_map/ppermute | solution.py:72
  13.6 0.6 collective-permute-start.5
  14.2 1.0 %collective-permute-start.6 = (bf16[64,768]{1,0:T(8,128)(2,1)S(1)}, bf16[64,768]{1,0:T(8,128)(2,1)S(1)}, u32[]{:S(2)}, u32[]{:S(2)}) collective-permute-start(bf16[64,768]{1,0:T(8,128)(2,1)S(1)} %join.2.refs_0_), channel_id=1, source_target_pairs={{0,32},{1,9},{2,34},{3,11},{4,36},{5,13},{6,38},{7,15},{8,40},{9,1... | collective-permute-start | bytes 294920 | tf_op jit(solution)/shard_map/ppermute | solution.py:72
  15.2 0.1 stack.23.pos_ref
  15.2 3.2 %prepare.1 = (bf16[2048,768]{1,0:T(8,128)(2,1)S(1)}, s32[1024,128]{1,0:T(8,128)S(1)}, f32[1,4096]{1,0:T(1,128)S(1)}) custom-call(s32[6]{0:T(128)S(1)} %stack.23.pos_ref, f32[1,2048]{1,0:T(1,128)S(1)} %collective-permute-done.refs_0_.b1_ref, bf16[2048,768]{1,0:T(8,128)(2,1)} %w_ref.1, s32[16,2048]{1,0:T(8,128)} %bitcast.8, s32[1,2048]{1,0:T(1,128)} %bitcast.11, ...), custom_call_target="tpu_custom_call" | custom-call | tf_op jit(solution)/shard_map/prepare/pallas_call | solution.py:131
  18.4 0.0 collective-permute-done.4.refs_1_
  18.4 1.3 %collective-permute-done.5.refs_2_ = bf16[64,768]{1,0:T(8,128)(2,1)S(1)} collective-permute-done((bf16[64,768]{1,0:T(8,128)(2,1)S(1)}, bf16[64,768]{1,0:T(8,128)(2,1)S(1)}, u32[]{:S(2)}, u32[]{:S(2)}) %collective-permute-start.5) | collective-permute-done | bytes 98336 | tf_op jit(solution)/shard_map/ppermute | solution.py:72
  19.8 1.0 %collective-permute-done.6.refs_3_ = bf16[64,768]{1,0:T(8,128)(2,1)S(1)} collective-permute-done((bf16[64,768]{1,0:T(8,128)(2,1)S(1)}, bf16[64,768]{1,0:T(8,128)(2,1)S(1)}, u32[]{:S(2)}, u32[]{:S(2)}) %collective-permute-start.6) | collective-permute-done | bytes 98336 | tf_op jit(solution)/shard_map/ppermute | solution.py:72
  20.8 1.6 %collective-permute-start.8 = (bf16[256,768]{1,0:T(8,128)(2,1)S(1)}, bf16[256,768]{1,0:T(8,128)(2,1)S(1)}, u32[]{:S(2)}, u32[]{:S(2)}) collective-permute-start(bf16[256,768]{1,0:T(8,128)(2,1)S(1)} %join.3.f_ref.refs_4_), channel_id=1, source_target_pairs={{0,8},{1,33},{2,10},{3,35},{4,12},{5,37},{6,14},{7,39},{8,0},{9,41... | collective-permute-start | bytes 1179656 | tf_op jit(solution)/shard_map/ppermute | solution.py:59
  22.3 2.1 %collective-permute-start.10 = (bf16[256,768]{1,0:T(8,128)(2,1)S(1)}, bf16[256,768]{1,0:T(8,128)(2,1)S(1)}, u32[]{:S(2)}, u32[]{:S(2)}) collective-permute-start(bf16[256,768]{1,0:T(8,128)(2,1)S(1)} %join.3.f_ref.refs_4_), channel_id=1, source_target_pairs={{0,24},{1,97},{2,26},{3,99},{4,28},{5,101},{6,30},{7,103},{8,16},{... | collective-permute-start | bytes 1179656 | tf_op jit(solution)/shard_map/ppermute | solution.py:59
  24.4 0.0 collective-permute-done.7.w1_ref
  24.4 3.6 %residual.4 = (bf16[256,4096]{1,0:T(8,128)(2,1)S(1)}, f32[256,768]{1,0:T(8,128)S(1)}, bf16[256,768]{1,0:T(8,128)(2,1)S(1)}) custom-call(bf16[256,768]{1,0:T(8,128)(2,1)S(1)} %join.3.f_ref.refs_4_, bf16[2048,768]{1,0:T(8,128)(2,1)S(1)} %get-tuple-element.30.w0_ref, bf16[2048,768]{1,0:T(8,128)(2,1)S(1)} %collective-permute-done.7.w1_ref, ...), custom_call_target="tpu_custom_call" | custom-call | flops 524288 | tf_op jit(solution)/shard_map/residual/pallas_call | solution.py:211
  28.1 0.7 %collective-permute-start.9 = (bf16[256,768]{1,0:T(8,128)(2,1)S(1)}, bf16[256,768]{1,0:T(8,128)(2,1)S(1)}, u32[]{:S(2)}, u32[]{:S(2)}) collective-permute-start(bf16[256,768]{1,0:T(8,128)(2,1)S(1)} %get-tuple-element.36), channel_id=1, source_target_pairs={{0,16},{1,65},{2,18},{3,67},{4,20},{5,69},{6,22},{7,71},{8,24},{9,... | collective-permute-start | bytes 1179656 | tf_op jit(solution)/shard_map/ppermute | solution.py:59
  28.8 0.0 collective-permute-done.8.f_ref.refs_5_
  28.8 3.6 %residual.5 = (bf16[256,4096]{1,0:T(8,128)(2,1)S(1)}, bf16[256,768]{1,0:T(8,128)(2,1)S(1)}) custom-call(bf16[256,768]{1,0:T(8,128)(2,1)S(1)} %collective-permute-done.8.f_ref.refs_5_, bf16[2048,768]{1,0:T(8,128)(2,1)S(1)} %get-tuple-element.30.w0_ref, bf16[2048,768]{1,0:T(8,128)(2,1)S(1)} %collective-permute-done.7.w1_ref, ...), custom_call_target="tpu_custom_call" | custom-call | flops 524288 | tf_op jit(solution)/shard_map/residual/pallas_call | solution.py:211
  32.5 1.6 %collective-permute-start.11 = (bf16[256,768]{1,0:T(8,128)(2,1)S(1)}, bf16[256,768]{1,0:T(8,128)(2,1)S(1)}, u32[]{:S(2)}, u32[]{:S(2)}) collective-permute-start(bf16[256,768]{1,0:T(8,128)(2,1)S(1)} %get-tuple-element.37.refs_0_), channel_id=1, source_target_pairs={{0,8},{1,33},{2,10},{3,35},{4,12},{5,37},{6,14},{7,39},{8,0},{9,41... | collective-permute-start | bytes 1179656 | tf_op jit(solution)/shard_map/ppermute | solution.py:59
  34.1 3.6 %residual.6 = (bf16[256,4096]{1,0:T(8,128)(2,1)S(1)}, bf16[256,768]{1,0:T(8,128)(2,1)S(1)}) custom-call(bf16[256,768]{1,0:T(8,128)(2,1)S(1)} %collective-permute-done.10.f_ref.refs_7_, bf16[2048,768]{1,0:T(8,128)(2,1)S(1)} %get-tuple-element.30.w0_ref, bf16[2048,768]{1,0:T(8,128)(2,1)S(1)} %collective-permute-done.7.w1_ref, ...), custom_call_target="tpu_custom_call" | custom-call | flops 524288 | tf_op jit(solution)/shard_map/residual/pallas_call | solution.py:211
  37.7 2.2 %collective-permute-start.12 = (bf16[256,768]{1,0:T(8,128)(2,1)S(1)}, bf16[256,768]{1,0:T(8,128)(2,1)S(1)}, u32[]{:S(2)}, u32[]{:S(2)}) collective-permute-start(bf16[256,768]{1,0:T(8,128)(2,1)S(1)} %get-tuple-element.38.refs_0_), channel_id=1, source_target_pairs={{0,24},{1,97},{2,26},{3,99},{4,28},{5,101},{6,30},{7,103},{8,16},{... | collective-permute-start | bytes 1179656 | tf_op jit(solution)/shard_map/ppermute | solution.py:59
  39.9 3.6 %residual.7 = (bf16[256,4096]{1,0:T(8,128)(2,1)S(1)}, bf16[256,768]{1,0:T(8,128)(2,1)S(1)}) custom-call(bf16[256,768]{1,0:T(8,128)(2,1)S(1)} %collective-permute-done.9.f_ref.refs_6_, bf16[2048,768]{1,0:T(8,128)(2,1)S(1)} %get-tuple-element.30.w0_ref, bf16[2048,768]{1,0:T(8,128)(2,1)S(1)} %collective-permute-done.7.w1_ref, ...), custom_call_target="tpu_custom_call" | custom-call | flops 524288 | tf_op jit(solution)/shard_map/residual/pallas_call | solution.py:211
  43.5 0.7 %collective-permute-start.15 = (bf16[256,768]{1,0:T(8,128)(2,1)S(1)}, bf16[256,768]{1,0:T(8,128)(2,1)S(1)}, u32[]{:S(2)}, u32[]{:S(2)}) collective-permute-start(bf16[256,768]{1,0:T(8,128)(2,1)S(1)} %get-tuple-element.41), channel_id=1, source_target_pairs={{0,16},{1,65},{2,18},{3,67},{4,20},{5,69},{6,22},{7,71},{8,24},{9,... | collective-permute-start | bytes 1179656 | tf_op jit(solution)/shard_map/ppermute | solution.py:59
  44.3 1.8 %weight_partial.3.refs_8_ = bf16[1024,768]{1,0:T(8,128)(2,1)S(1)} custom-call(bf16[256,4096]{1,0:T(8,128)(2,1)S(1)} %get-tuple-element.33.refs_0_, bf16[256,4096]{1,0:T(8,128)(2,1)S(1)} %get-tuple-element.35.refs_1_, bf16[256,4096]{1,0:T(8,128)(2,1)S(1)} %get-tuple-element.39.refs_2_, bf16[256,4096]{1,0:T(8,128)(2,1)S(1)} %get-tuple-element.40.refs_3_, ...), custom_call_target="tpu_custom_call" | custom-call | flops 65536 | tf_op jit(solution)/shard_map/weight_partial/pallas_call | solution.py:233
  46.1 0.1 collective-permute-start.14
  46.2 0.6 collective-permute-done.12.refs_8_.b_ref
  46.8 1.8 %weight_partial.4.refs_9_ = bf16[1024,768]{1,0:T(8,128)(2,1)S(1)} custom-call(bf16[256,4096]{1,0:T(8,128)(2,1)S(1)} %get-tuple-element.33.refs_0_, bf16[256,4096]{1,0:T(8,128)(2,1)S(1)} %get-tuple-element.35.refs_1_, bf16[256,4096]{1,0:T(8,128)(2,1)S(1)} %get-tuple-element.39.refs_2_, bf16[256,4096]{1,0:T(8,128)(2,1)S(1)} %get-tuple-element.40.refs_3_, ...), custom_call_target="tpu_custom_call" | custom-call | flops 65536 | tf_op jit(solution)/shard_map/weight_partial/pallas_call | solution.py:233
  48.6 0.1 collective-permute-start.13
  48.7 1.8 %weight_partial.5.refs_0_.mine_ref = f32[1024,768]{1,0:T(8,128)S(1)} custom-call(bf16[256,4096]{1,0:T(8,128)(2,1)S(1)} %get-tuple-element.33.refs_0_, bf16[256,4096]{1,0:T(8,128)(2,1)S(1)} %get-tuple-element.35.refs_1_, bf16[256,4096]{1,0:T(8,128)(2,1)S(1)} %get-tuple-element.39.refs_2_, bf16[256,4096]{1,0:T(8,128)(2,1)S(1)} %get-tuple-element.40.refs_3_, ...), custom_call_target="tpu_custom_call" | custom-call | flops 65536 | tf_op jit(solution)/shard_map/weight_partial/pallas_call | solution.py:233
  50.5 2.4 %collective-permute-done.15.c_ref = bf16[256,768]{1,0:T(8,128)(2,1)S(1)} collective-permute-done((bf16[256,768]{1,0:T(8,128)(2,1)S(1)}, bf16[256,768]{1,0:T(8,128)(2,1)S(1)}, u32[]{:S(2)}, u32[]{:S(2)}) %collective-permute-start.15) | collective-permute-done | bytes 393248 | tf_op jit(solution)/shard_map/ppermute | solution.py:59
  52.9 0.2 add.30
  53.1 0.1 collective-permute-start.16
  53.2 2.0 %collective-permute-start.17 = (bf16[64,768]{1,0:T(8,128)(2,1)S(1)}, bf16[64,768]{1,0:T(8,128)(2,1)S(1)}, u32[]{:S(2)}, u32[]{:S(2)}) collective-permute-start(bf16[64,768]{1,0:T(8,128)(2,1)S(1)} %get-tuple-element.43.refs_10_), channel_id=1, source_target_pairs={{0,64},{1,17},{2,66},{3,19},{4,68},{5,21},{6,70},{7,23},{8,72},{9,... | collective-permute-start | bytes 294920 | tf_op jit(solution)/shard_map/ppermute | solution.py:76
  55.2 1.6 %collective-permute-start.18 = (bf16[64,768]{1,0:T(8,128)(2,1)S(1)}, bf16[64,768]{1,0:T(8,128)(2,1)S(1)}, u32[]{:S(2)}, u32[]{:S(2)}) collective-permute-start(bf16[64,768]{1,0:T(8,128)(2,1)S(1)} %get-tuple-element.44.refs_11_), channel_id=1, source_target_pairs={{0,96},{1,25},{2,98},{3,27},{4,100},{5,29},{6,102},{7,31},{8,104},... | collective-permute-start | bytes 294920 | tf_op jit(solution)/shard_map/ppermute | solution.py:76
  56.8 2.8 %weight_rows.1 = (bf16[2048,768]{1,0:T(8,128)(2,1)}, f32[8,128]{1,0:T(8,128)S(1)}) custom-call(bf16[256,4096]{1,0:T(8,128)(2,1)S(1)} %get-tuple-element.33.refs_0_, bf16[256,4096]{1,0:T(8,128)(2,1)S(1)} %get-tuple-element.35.refs_1_, bf16[256,4096]{1,0:T(8,128)(2,1)S(1)} %get-tuple-element.39.refs_2_, bf16[256,4096]{1,0:T(8,128)(2,1)S(1)} %get-tuple-element.40.refs_3_, ...), custom_call_target="tpu_custom_call" | custom-call | flops 1610612736 | tf_op jit(solution)/shard_map/weight_rows/pallas_call | solution.py:266
  59.5 0.5 collective-permute-done.16.a_ref
  60.0 0.9 %collective-permute-done.18.c_ref = bf16[64,768]{1,0:T(8,128)(2,1)S(1)} collective-permute-done((bf16[64,768]{1,0:T(8,128)(2,1)S(1)}, bf16[64,768]{1,0:T(8,128)(2,1)S(1)}, u32[]{:S(2)}, u32[]{:S(2)}) %collective-permute-start.18) | collective-permute-done | bytes 98336 | tf_op jit(solution)/shard_map/ppermute | solution.py:76
  60.9 0.2 collective-permute-start.19
  61.2 2.1 %collective-permute-start.20 = (bf16[16,768]{1,0:T(8,128)(2,1)S(1)}, bf16[16,768]{1,0:T(8,128)(2,1)S(1)}, u32[]{:S(2)}, u32[]{:S(2)}) collective-permute-start(bf16[16,768]{1,0:T(8,128)(2,1)S(1)} %get-tuple-element.49.refs_2_), channel_id=1, source_target_pairs={{0,4},{1,5},{2,6},{3,7},{4,0},{5,1},{6,2},{7,3},{8,12},{9,13},{10,... | collective-permute-start | bytes 73736 | tf_op jit(solution)/shard_map/ppermute | solution.py:76
  63.3 2.4 %collective-permute-start.21 = (bf16[16,768]{1,0:T(8,128)(2,1)S(1)}, bf16[16,768]{1,0:T(8,128)(2,1)S(1)}, u32[]{:S(2)}, u32[]{:S(2)}) collective-permute-start(bf16[16,768]{1,0:T(8,128)(2,1)S(1)} %get-tuple-element.50.refs_3_), channel_id=1, source_target_pairs={{0,6},{1,7},{2,0},{3,1},{4,2},{5,3},{6,4},{7,5},{8,14},{9,15},{10,... | collective-permute-start | bytes 73736 | tf_op jit(solution)/shard_map/ppermute | solution.py:76
  65.7 1.2 %finish_rows.1 = (bf16[2048,768]{1,0:T(8,128)(2,1)}, f32[8,128]{1,0:T(8,128)S(1)}) custom-call(f32[1024,768]{1,0:T(8,128)S(1)} %weight_partial.5.refs_0_.mine_ref, bf16[1024,768]{1,0:T(8,128)(2,1)S(1)} %collective-permute-done.13.other_ref, bf16[2048,768]{1,0:T(8,128)(2,1)} %get-tuple-element.45.refs_0_, ...), custom_call_target="tpu_custom_call", output_to_operand_aliasing={{0}: (2, {})} | custom-call | flops 1610612736 | tf_op jit(solution)/shard_map/finish_rows/pallas_call | solution.py:295
  66.9 0.3 collective-permute-done.21.c_ref
  67.2 0.6 add.32
  (13 shorter events, 0.1 us)
Async XLA Ops:
  0.6 7.6 %collective-permute-start.1 = (bf16[16,768]{1,0:T(8,128)(2,1)}, bf16[16,768]{1,0:T(8,128)(2,1)S(1)}, u32[]{:S(2)}, u32[]{:S(2)}) collective-permute-start(bf16[16,768]{1,0:T(8,128)(2,1)} %x_ref.1), channel_id=1, source_target_pairs={{0,6},{1,7},{2,0},{3,1},{4,2},{5,3},{6,4},{7,5},{8,14},{9,15},{10,... | collective-permute-start | bytes 73736 | tf_op jit(solution)/shard_map/ppermute | solution.py:72
  4.8 5.5 %collective-permute-start.2 = (bf16[16,768]{1,0:T(8,128)(2,1)}, bf16[16,768]{1,0:T(8,128)(2,1)S(1)}, u32[]{:S(2)}, u32[]{:S(2)}) collective-permute-start(bf16[16,768]{1,0:T(8,128)(2,1)} %x_ref.1), channel_id=1, source_target_pairs={{0,4},{1,5},{2,6},{3,7},{4,0},{5,1},{6,2},{7,3},{8,12},{9,13},{10,... | collective-permute-start | bytes 73736 | tf_op jit(solution)/shard_map/ppermute | solution.py:72
  4.8 5.5 %collective-permute-start.3 = (bf16[16,768]{1,0:T(8,128)(2,1)}, bf16[16,768]{1,0:T(8,128)(2,1)S(1)}, u32[]{:S(2)}, u32[]{:S(2)}) collective-permute-start(bf16[16,768]{1,0:T(8,128)(2,1)} %x_ref.1), channel_id=1, source_target_pairs={{0,2},{1,3},{2,4},{3,5},{4,6},{5,7},{6,0},{7,1},{8,10},{9,11},{10,... | collective-permute-start | bytes 73736 | tf_op jit(solution)/shard_map/ppermute | solution.py:72
  6.1 1.4 %collective-permute-start = (f32[1,2048]{1,0:T(1,128)}, f32[1,2048]{1,0:T(1,128)S(1)}, u32[]{:S(2)}, u32[]{:S(2)}) collective-permute-start(f32[1,2048]{1,0:T(1,128)} %bitcast.9), channel_id=1, source_target_pairs={{0,1},{1,0},{2,3},{3,2},{4,5},{5,4},{6,7},{7,6},{8,9},{9,8},{10,11... | collective-permute-start | bytes 24584 | tf_op jit(solution)/shard_map/ppermute | solution.py:80
  10.4 14.1 %collective-permute-start.7 = (bf16[2048,768]{1,0:T(8,128)(2,1)}, bf16[2048,768]{1,0:T(8,128)(2,1)S(1)}, u32[]{:S(2)}, u32[]{:S(2)}) collective-permute-start(bf16[2048,768]{1,0:T(8,128)(2,1)} %w_ref.1), channel_id=1, source_target_pairs={{0,1},{1,0},{2,3},{3,2},{4,5},{5,4},{6,7},{7,6},{8,9},{9,8},{10,11... | collective-permute-start | bytes 9437192 | tf_op jit(solution)/shard_map/ppermute | solution.py:80
  10.5 8.0 %collective-permute-start.4 = (bf16[64,768]{1,0:T(8,128)(2,1)S(1)}, bf16[64,768]{1,0:T(8,128)(2,1)S(1)}, u32[]{:S(2)}, u32[]{:S(2)}) collective-permute-start(bf16[64,768]{1,0:T(8,128)(2,1)S(1)} %join.2.refs_0_), channel_id=1, source_target_pairs={{0,96},{1,25},{2,98},{3,27},{4,100},{5,29},{6,102},{7,31},{8,104},... | collective-permute-start | bytes 294920 | tf_op jit(solution)/shard_map/ppermute | solution.py:72
  13.6 6.2 %collective-permute-start.5 = (bf16[64,768]{1,0:T(8,128)(2,1)S(1)}, bf16[64,768]{1,0:T(8,128)(2,1)S(1)}, u32[]{:S(2)}, u32[]{:S(2)}) collective-permute-start(bf16[64,768]{1,0:T(8,128)(2,1)S(1)} %join.2.refs_0_), channel_id=1, source_target_pairs={{0,64},{1,17},{2,66},{3,19},{4,68},{5,21},{6,70},{7,23},{8,72},{9,... | collective-permute-start | bytes 294920 | tf_op jit(solution)/shard_map/ppermute | solution.py:72
  14.2 6.5 %collective-permute-start.6 = (bf16[64,768]{1,0:T(8,128)(2,1)S(1)}, bf16[64,768]{1,0:T(8,128)(2,1)S(1)}, u32[]{:S(2)}, u32[]{:S(2)}) collective-permute-start(bf16[64,768]{1,0:T(8,128)(2,1)S(1)} %join.2.refs_0_), channel_id=1, source_target_pairs={{0,32},{1,9},{2,34},{3,11},{4,36},{5,13},{6,38},{7,15},{8,40},{9,1... | collective-permute-start | bytes 294920 | tf_op jit(solution)/shard_map/ppermute | solution.py:72
  20.8 8.0 %collective-permute-start.8 = (bf16[256,768]{1,0:T(8,128)(2,1)S(1)}, bf16[256,768]{1,0:T(8,128)(2,1)S(1)}, u32[]{:S(2)}, u32[]{:S(2)}) collective-permute-start(bf16[256,768]{1,0:T(8,128)(2,1)S(1)} %join.3.f_ref.refs_4_), channel_id=1, source_target_pairs={{0,8},{1,33},{2,10},{3,35},{4,12},{5,37},{6,14},{7,39},{8,0},{9,41... | collective-permute-start | bytes 1179656 | tf_op jit(solution)/shard_map/ppermute | solution.py:59
  22.3 11.7 %collective-permute-start.10 = (bf16[256,768]{1,0:T(8,128)(2,1)S(1)}, bf16[256,768]{1,0:T(8,128)(2,1)S(1)}, u32[]{:S(2)}, u32[]{:S(2)}) collective-permute-start(bf16[256,768]{1,0:T(8,128)(2,1)S(1)} %join.3.f_ref.refs_4_), channel_id=1, source_target_pairs={{0,24},{1,97},{2,26},{3,99},{4,28},{5,101},{6,30},{7,103},{8,16},{... | collective-permute-start | bytes 1179656 | tf_op jit(solution)/shard_map/ppermute | solution.py:59
  28.1 11.8 %collective-permute-start.9 = (bf16[256,768]{1,0:T(8,128)(2,1)S(1)}, bf16[256,768]{1,0:T(8,128)(2,1)S(1)}, u32[]{:S(2)}, u32[]{:S(2)}) collective-permute-start(bf16[256,768]{1,0:T(8,128)(2,1)S(1)} %get-tuple-element.36), channel_id=1, source_target_pairs={{0,16},{1,65},{2,18},{3,67},{4,20},{5,69},{6,22},{7,71},{8,24},{9,... | collective-permute-start | bytes 1179656 | tf_op jit(solution)/shard_map/ppermute | solution.py:59
  32.5 11.8 %collective-permute-start.11 = (bf16[256,768]{1,0:T(8,128)(2,1)S(1)}, bf16[256,768]{1,0:T(8,128)(2,1)S(1)}, u32[]{:S(2)}, u32[]{:S(2)}) collective-permute-start(bf16[256,768]{1,0:T(8,128)(2,1)S(1)} %get-tuple-element.37.refs_0_), channel_id=1, source_target_pairs={{0,8},{1,33},{2,10},{3,35},{4,12},{5,37},{6,14},{7,39},{8,0},{9,41... | collective-permute-start | bytes 1179656 | tf_op jit(solution)/shard_map/ppermute | solution.py:59
  37.7 9.1 %collective-permute-start.12 = (bf16[256,768]{1,0:T(8,128)(2,1)S(1)}, bf16[256,768]{1,0:T(8,128)(2,1)S(1)}, u32[]{:S(2)}, u32[]{:S(2)}) collective-permute-start(bf16[256,768]{1,0:T(8,128)(2,1)S(1)} %get-tuple-element.38.refs_0_), channel_id=1, source_target_pairs={{0,24},{1,97},{2,26},{3,99},{4,28},{5,101},{6,30},{7,103},{8,16},{... | collective-permute-start | bytes 1179656 | tf_op jit(solution)/shard_map/ppermute | solution.py:59
  43.5 9.4 %collective-permute-start.15 = (bf16[256,768]{1,0:T(8,128)(2,1)S(1)}, bf16[256,768]{1,0:T(8,128)(2,1)S(1)}, u32[]{:S(2)}, u32[]{:S(2)}) collective-permute-start(bf16[256,768]{1,0:T(8,128)(2,1)S(1)} %get-tuple-element.41), channel_id=1, source_target_pairs={{0,16},{1,65},{2,18},{3,67},{4,20},{5,69},{6,22},{7,71},{8,24},{9,... | collective-permute-start | bytes 1179656 | tf_op jit(solution)/shard_map/ppermute | solution.py:59
  46.1 10.6 %collective-permute-start.14 = (bf16[1024,768]{1,0:T(8,128)(2,1)S(1)}, bf16[1024,768]{1,0:T(8,128)(2,1)S(1)}, u32[]{:S(2)}, u32[]{:S(2)}) collective-permute-start(bf16[1024,768]{1,0:T(8,128)(2,1)S(1)} %weight_partial.3.refs_8_), channel_id=1, source_target_pairs={{0,1},{1,0},{2,3},{3,2},{4,5},{5,4},{6,7},{7,6},{8,9},{9,8},{10,11... | collective-permute-start | bytes 4718600 | tf_op jit(solution)/shard_map/ppermute | solution.py:80
  48.6 17.1 %collective-permute-start.13 = (bf16[1024,768]{1,0:T(8,128)(2,1)S(1)}, bf16[1024,768]{1,0:T(8,128)(2,1)S(1)}, u32[]{:S(2)}, u32[]{:S(2)}) collective-permute-start(bf16[1024,768]{1,0:T(8,128)(2,1)S(1)} %weight_partial.4.refs_9_), channel_id=1, source_target_pairs={{0,1},{1,0},{2,3},{3,2},{4,5},{5,4},{6,7},{7,6},{8,9},{9,8},{10,11... | collective-permute-start | bytes 4718600 | tf_op jit(solution)/shard_map/ppermute | solution.py:80
  53.1 6.9 %collective-permute-start.16 = (bf16[64,768]{1,0:T(8,128)(2,1)S(1)}, bf16[64,768]{1,0:T(8,128)(2,1)S(1)}, u32[]{:S(2)}, u32[]{:S(2)}) collective-permute-start(bf16[64,768]{1,0:T(8,128)(2,1)S(1)} %get-tuple-element.42.refs_9_), channel_id=1, source_target_pairs={{0,32},{1,9},{2,34},{3,11},{4,36},{5,13},{6,38},{7,15},{8,40},{9,1... | collective-permute-start | bytes 294920 | tf_op jit(solution)/shard_map/ppermute | solution.py:76
  53.2 6.9 %collective-permute-start.17 = (bf16[64,768]{1,0:T(8,128)(2,1)S(1)}, bf16[64,768]{1,0:T(8,128)(2,1)S(1)}, u32[]{:S(2)}, u32[]{:S(2)}) collective-permute-start(bf16[64,768]{1,0:T(8,128)(2,1)S(1)} %get-tuple-element.43.refs_10_), channel_id=1, source_target_pairs={{0,64},{1,17},{2,66},{3,19},{4,68},{5,21},{6,70},{7,23},{8,72},{9,... | collective-permute-start | bytes 294920 | tf_op jit(solution)/shard_map/ppermute | solution.py:76
  55.2 5.7 %collective-permute-start.18 = (bf16[64,768]{1,0:T(8,128)(2,1)S(1)}, bf16[64,768]{1,0:T(8,128)(2,1)S(1)}, u32[]{:S(2)}, u32[]{:S(2)}) collective-permute-start(bf16[64,768]{1,0:T(8,128)(2,1)S(1)} %get-tuple-element.44.refs_11_), channel_id=1, source_target_pairs={{0,96},{1,25},{2,98},{3,27},{4,100},{5,29},{6,102},{7,31},{8,104},... | collective-permute-start | bytes 294920 | tf_op jit(solution)/shard_map/ppermute | solution.py:76
  60.9 6.0 %collective-permute-start.19 = (bf16[16,768]{1,0:T(8,128)(2,1)S(1)}, bf16[16,768]{1,0:T(8,128)(2,1)S(1)}, u32[]{:S(2)}, u32[]{:S(2)}) collective-permute-start(bf16[16,768]{1,0:T(8,128)(2,1)S(1)} %get-tuple-element.48.refs_1_), channel_id=1, source_target_pairs={{0,2},{1,3},{2,4},{3,5},{4,6},{5,7},{6,0},{7,1},{8,10},{9,11},{10,... | collective-permute-start | bytes 73736 | tf_op jit(solution)/shard_map/ppermute | solution.py:76
  61.2 5.7 %collective-permute-start.20 = (bf16[16,768]{1,0:T(8,128)(2,1)S(1)}, bf16[16,768]{1,0:T(8,128)(2,1)S(1)}, u32[]{:S(2)}, u32[]{:S(2)}) collective-permute-start(bf16[16,768]{1,0:T(8,128)(2,1)S(1)} %get-tuple-element.49.refs_2_), channel_id=1, source_target_pairs={{0,4},{1,5},{2,6},{3,7},{4,0},{5,1},{6,2},{7,3},{8,12},{9,13},{10,... | collective-permute-start | bytes 73736 | tf_op jit(solution)/shard_map/ppermute | solution.py:76
  63.3 3.9 %collective-permute-start.21 = (bf16[16,768]{1,0:T(8,128)(2,1)S(1)}, bf16[16,768]{1,0:T(8,128)(2,1)S(1)}, u32[]{:S(2)}, u32[]{:S(2)}) collective-permute-start(bf16[16,768]{1,0:T(8,128)(2,1)S(1)} %get-tuple-element.50.refs_3_), channel_id=1, source_target_pairs={{0,6},{1,7},{2,0},{3,1},{4,2},{5,3},{6,4},{7,5},{8,14},{9,15},{10,... | collective-permute-start | bytes 73736 | tf_op jit(solution)/shard_map/ppermute | solution.py:76

commit v5 on v4

--- a/solution.py
+++ b/solution.py
@@ -74,6 +74,9 @@
 
 def push(x, stage, k):
     return lax.ppermute(x, AXES, shifted(stage, k))
+
+
+ORDERED = (0, 2, 1, 3)
 
 
 def swap(x):
@@ -166,6 +169,7 @@
 
 
 def join_kernel(count, factor, *refs):
+    refs = [refs[ORDERED.index(k)] for k in range(count)] + [refs[-1]]
     refs[-1][...] = jnp.concatenate([ref[...] for ref in refs[:count]], axis=0) * jnp.bfloat16(factor)
 
 
@@ -339,12 +343,12 @@
 
     b0 = label_bias.reshape(1, own)
     b1 = swap(b0)
-    near = [fetch(features, "first", k) for k in (1, 2, 3)]
+    near = [fetch(features, "first", k) for k in ORDERED[1:]]
     f64 = join([load(features, (b1,))] + near, factor=0.5)
     late, f64 = lax.optimization_barrier((label_weight, f64))
     w1 = swap(late)
     w0, words, b = prepare(piece, pos, label_weight, positive_ids.T, positive_counts.reshape(1, -1), b0, b1, after=(f64,))
-    f256 = join([f64] + [fetch(f64, "second", k) for k in (1, 2, 3)], after=(words,))
+    f256 = join([f64] + [fetch(f64, "second", k) for k in ORDERED[1:]], after=(words,))
     fs = [f256, exchange(f256, "third", 1), None, exchange(f256, "third", 3)]
 
     rs = [None] * N
@@ -362,10 +366,10 @@
     mine = partial(half, half, jnp.float32, theirs)
     theirs = [swap(x) for x in theirs]
     sums, *sent = add(sums, arrived, N, after=(mine,))
-    arrived = [push(x, "second", k) for k, x in zip((1, 2, 3), sent)]
+    arrived = [push(sent[k - 1], "second", k) for k in ORDERED[1:]]
     weight_grad, done = weight_rows(rs, fs, 0, half, own, theirs[0], sent)
     sums, *sent = add(sums, arrived, N, after=(done,))
-    arrived = [push(x, "first", k) for k, x in zip((1, 2, 3), sent)]
+    arrived = [push(sent[k - 1], "first", k) for k in ORDERED[1:]]
     weight_grad, done = finish_rows(mine, theirs[1], weight_grad, half, sent)
     (sums,) = add(sums, arrived, 1, after=(done,))
     return weight_grad, sums

time: 68 us -> 67.6 us (level)
  waiting for transfers between devices: 10.4 us -> 8.92 us
  starting transfers between devices: 27.7 us -> 28.8 us
    ppermute x6, starting transfers between devices: 10.1 us -> 11.4 us  [fetch(): return lax.ppermute(x, AXES, shifted(stage, -k))]
    ppermute x6, waiting for transfers between devices: 4.46 us -> 3.38 us  [fetch(): return lax.ppermute(x, AXES, shifted(stage, -k))]
  transfers between devices with their start and end apart: 22 -> 22, of which waited for: 9 -> 7; matrix products, arithmetic and copies ran while one was open for 0% -> 0% of each run, Pallas kernels for 42% -> 42%
where the time goes in v5:
time: 67.6 us; the launch traced here: 67.5 us
  Pallas kernels  28.9 us (43%)
  starting transfers between devices  28.8 us (43%)
  waiting for transfers between devices  8.92 us (13%)
  between operations  0.79 us (1%)
    pallas_call x4, Pallas kernels, residual(): pl.pallas_call(functools.partial(residual_kernel, chunk, again), in_specs...  14.6 us
    ppermute x6, starting transfers between devices, fetch(): return lax.ppermute(x, AXES, shifted(stage, -k))  11.4 us
    ppermute x6, starting transfers between devices, exchange(): return lax.ppermute(x, AXES, partners(stage, k))  8.89 us
    ppermute x6, starting transfers between devices, push(): return lax.ppermute(x, AXES, shifted(stage, k))  8.27 us
    pallas_call x3, Pallas kernels, weight_partial(): pl.pallas_call(functools.partial(weight_partial_kernel, start), in_specs=...  5.47 us
    ppermute x6, waiting for transfers between devices, fetch(): return lax.ppermute(x, AXES, shifted(stage, -k))  3.38 us
    pallas_call x1, Pallas kernels, prepare(): pl.pallas_call(functools.partial(prepare_kernel, piece), in_specs=[SCALAR...  3.18 us
    ppermute x6, waiting for transfers between devices, exchange(): return lax.ppermute(x, AXES, partners(stage, k))  2.91 us
  transfers between devices with their start and end apart: 22, of which 7 were waited for; matrix products, arithmetic and copies ran while one was open for 0% of the time, Pallas kernels for 42%

profile of v5, /device:TPU:0, one launch (start us, length us, event | category | flops | bytes accessed | tf_op | source)
XLA Modules:
  0.0 67.5 jit_solution(27341775184967919)
XLA Ops:
  0.6 4.0 %collective-permute-start.1 = (bf16[16,768]{1,0:T(8,128)(2,1)}, bf16[16,768]{1,0:T(8,128)(2,1)S(1)}, u32[]{:S(2)}, u32[]{:S(2)}) collective-permute-start(bf16[16,768]{1,0:T(8,128)(2,1)} %x_ref.1), channel_id=1, source_target_pairs={{0,4},{1,5},{2,6},{3,7},{4,0},{5,1},{6,2},{7,3},{8,12},{9,13},{10,... | collective-permute-start | bytes 73736 | tf_op jit(solution)/shard_map/ppermute | solution.py:72
  4.7 0.7 %collective-permute-start.2 = (bf16[16,768]{1,0:T(8,128)(2,1)}, bf16[16,768]{1,0:T(8,128)(2,1)S(1)}, u32[]{:S(2)}, u32[]{:S(2)}) collective-permute-start(bf16[16,768]{1,0:T(8,128)(2,1)} %x_ref.1), channel_id=1, source_target_pairs={{0,6},{1,7},{2,0},{3,1},{4,2},{5,3},{6,4},{7,5},{8,14},{9,15},{10,... | collective-permute-start | bytes 73736 | tf_op jit(solution)/shard_map/ppermute | solution.py:72
  5.4 1.3 %collective-permute-start.3 = (bf16[16,768]{1,0:T(8,128)(2,1)}, bf16[16,768]{1,0:T(8,128)(2,1)S(1)}, u32[]{:S(2)}, u32[]{:S(2)}) collective-permute-start(bf16[16,768]{1,0:T(8,128)(2,1)} %x_ref.1), channel_id=1, source_target_pairs={{0,2},{1,3},{2,4},{3,5},{4,6},{5,7},{6,0},{7,1},{8,10},{9,11},{10,... | collective-permute-start | bytes 73736 | tf_op jit(solution)/shard_map/ppermute | solution.py:72
  6.7 0.0 collective-permute-start
  6.7 1.4 %collective-permute-done.refs_0_.b1_ref = f32[1,2048]{1,0:T(1,128)S(1)} collective-permute-done((f32[1,2048]{1,0:T(1,128)}, f32[1,2048]{1,0:T(1,128)S(1)}, u32[]{:S(2)}, u32[]{:S(2)}) %collective-permute-start) | collective-permute-done | bytes 8224 | tf_op jit(solution)/shard_map/ppermute | solution.py:83
  8.1 0.7 %load.1.refs_0_ = bf16[16,768]{1,0:T(8,128)(2,1)S(1)} custom-call(bf16[16,768]{1,0:T(8,128)(2,1)} %x_ref.1, f32[1,2048]{1,0:T(1,128)S(1)} %collective-permute-done.refs_0_.b1_ref), custom_call_target="tpu_custom_call" | custom-call | tf_op jit(solution)/shard_map/load/pallas_call | solution.py:160
  8.8 0.0 collective-permute-done.1.refs_1_
  8.8 0.0 collective-permute-done.2.refs_2_
  8.8 1.8 %collective-permute-done.3.refs_3_ = bf16[16,768]{1,0:T(8,128)(2,1)S(1)} collective-permute-done((bf16[16,768]{1,0:T(8,128)(2,1)}, bf16[16,768]{1,0:T(8,128)(2,1)S(1)}, u32[]{:S(2)}, u32[]{:S(2)}) %collective-permute-start.3) | collective-permute-done | bytes 24608 | tf_op jit(solution)/shard_map/ppermute | solution.py:72
  10.6 0.1 collective-permute-start.7
  10.7 3.3 %collective-permute-start.4 = (bf16[64,768]{1,0:T(8,128)(2,1)S(1)}, bf16[64,768]{1,0:T(8,128)(2,1)S(1)}, u32[]{:S(2)}, u32[]{:S(2)}) collective-permute-start(bf16[64,768]{1,0:T(8,128)(2,1)S(1)} %join.2.refs_0_), channel_id=1, source_target_pairs={{0,64},{1,17},{2,66},{3,19},{4,68},{5,21},{6,70},{7,23},{8,72},{9,... | collective-permute-start | bytes 294920 | tf_op jit(solution)/shard_map/ppermute | solution.py:72
  14.0 1.1 %collective-permute-start.5 = (bf16[64,768]{1,0:T(8,128)(2,1)S(1)}, bf16[64,768]{1,0:T(8,128)(2,1)S(1)}, u32[]{:S(2)}, u32[]{:S(2)}) collective-permute-start(bf16[64,768]{1,0:T(8,128)(2,1)S(1)} %join.2.refs_0_), channel_id=1, source_target_pairs={{0,96},{1,25},{2,98},{3,27},{4,100},{5,29},{6,102},{7,31},{8,104},... | collective-permute-start | bytes 294920 | tf_op jit(solution)/shard_map/ppermute | solution.py:72
  15.1 1.0 %collective-permute-start.6 = (bf16[64,768]{1,0:T(8,128)(2,1)S(1)}, bf16[64,768]{1,0:T(8,128)(2,1)S(1)}, u32[]{:S(2)}, u32[]{:S(2)}) collective-permute-start(bf16[64,768]{1,0:T(8,128)(2,1)S(1)} %join.2.refs_0_), channel_id=1, source_target_pairs={{0,32},{1,9},{2,34},{3,11},{4,36},{5,13},{6,38},{7,15},{8,40},{9,1... | collective-permute-start | bytes 294920 | tf_op jit(solution)/shard_map/ppermute | solution.py:72
  16.0 0.1 stack.23.pos_ref
  16.1 3.2 %prepare.1 = (bf16[2048,768]{1,0:T(8,128)(2,1)S(1)}, s32[1024,128]{1,0:T(8,128)S(1)}, f32[1,4096]{1,0:T(1,128)S(1)}) custom-call(s32[6]{0:T(128)S(1)} %stack.23.pos_ref, f32[1,2048]{1,0:T(1,128)S(1)} %collective-permute-done.refs_0_.b1_ref, bf16[2048,768]{1,0:T(8,128)(2,1)} %w_ref.1, s32[16,2048]{1,0:T(8,128)} %bitcast.8, s32[1,2048]{1,0:T(1,128)} %bitcast.11, ...), custom_call_target="tpu_custom_call" | custom-call | tf_op jit(solution)/shard_map/prepare/pallas_call | solution.py:134
  19.3 0.0 collective-permute-done.5.refs_2_
  19.3 1.6 %collective-permute-done.6.refs_3_ = bf16[64,768]{1,0:T(8,128)(2,1)S(1)} collective-permute-done((bf16[64,768]{1,0:T(8,128)(2,1)S(1)}, bf16[64,768]{1,0:T(8,128)(2,1)S(1)}, u32[]{:S(2)}, u32[]{:S(2)}) %collective-permute-start.6) | collective-permute-done | bytes 98336 | tf_op jit(solution)/shard_map/ppermute | solution.py:72
  20.9 1.6 %collective-permute-start.8 = (bf16[256,768]{1,0:T(8,128)(2,1)S(1)}, bf16[256,768]{1,0:T(8,128)(2,1)S(1)}, u32[]{:S(2)}, u32[]{:S(2)}) collective-permute-start(bf16[256,768]{1,0:T(8,128)(2,1)S(1)} %join.3.f_ref.refs_4_), channel_id=1, source_target_pairs={{0,8},{1,33},{2,10},{3,35},{4,12},{5,37},{6,14},{7,39},{8,0},{9,41... | collective-permute-start | bytes 1179656 | tf_op jit(solution)/shard_map/ppermute | solution.py:59
  22.5 2.1 %collective-permute-start.10 = (bf16[256,768]{1,0:T(8,128)(2,1)S(1)}, bf16[256,768]{1,0:T(8,128)(2,1)S(1)}, u32[]{:S(2)}, u32[]{:S(2)}) collective-permute-start(bf16[256,768]{1,0:T(8,128)(2,1)S(1)} %join.3.f_ref.refs_4_), channel_id=1, source_target_pairs={{0,24},{1,97},{2,26},{3,99},{4,28},{5,101},{6,30},{7,103},{8,16},{... | collective-permute-start | bytes 1179656 | tf_op jit(solution)/shard_map/ppermute | solution.py:59
  24.6 0.0 collective-permute-done.7.w1_ref
  24.6 3.6 %residual.4 = (bf16[256,4096]{1,0:T(8,128)(2,1)S(1)}, f32[256,768]{1,0:T(8,128)S(1)}, bf16[256,768]{1,0:T(8,128)(2,1)S(1)}) custom-call(bf16[256,768]{1,0:T(8,128)(2,1)S(1)} %join.3.f_ref.refs_4_, bf16[2048,768]{1,0:T(8,128)(2,1)S(1)} %get-tuple-element.30.w0_ref, bf16[2048,768]{1,0:T(8,128)(2,1)S(1)} %collective-permute-done.7.w1_ref, ...), custom_call_target="tpu_custom_call" | custom-call | flops 524288 | tf_op jit(solution)/shard_map/residual/pallas_call | solution.py:215
  28.2 0.7 %collective-permute-start.9 = (bf16[256,768]{1,0:T(8,128)(2,1)S(1)}, bf16[256,768]{1,0:T(8,128)(2,1)S(1)}, u32[]{:S(2)}, u32[]{:S(2)}) collective-permute-start(bf16[256,768]{1,0:T(8,128)(2,1)S(1)} %get-tuple-element.36), channel_id=1, source_target_pairs={{0,16},{1,65},{2,18},{3,67},{4,20},{5,69},{6,22},{7,71},{8,24},{9,... | collective-permute-start | bytes 1179656 | tf_op jit(solution)/shard_map/ppermute | solution.py:59
  29.0 3.7 %residual.5 = (bf16[256,4096]{1,0:T(8,128)(2,1)S(1)}, bf16[256,768]{1,0:T(8,128)(2,1)S(1)}) custom-call(bf16[256,768]{1,0:T(8,128)(2,1)S(1)} %collective-permute-done.8.f_ref.refs_5_, bf16[2048,768]{1,0:T(8,128)(2,1)S(1)} %get-tuple-element.30.w0_ref, bf16[2048,768]{1,0:T(8,128)(2,1)S(1)} %collective-permute-done.7.w1_ref, ...), custom_call_target="tpu_custom_call" | custom-call | flops 524288 | tf_op jit(solution)/shard_map/residual/pallas_call | solution.py:215
  32.7 1.6 %collective-permute-start.11 = (bf16[256,768]{1,0:T(8,128)(2,1)S(1)}, bf16[256,768]{1,0:T(8,128)(2,1)S(1)}, u32[]{:S(2)}, u32[]{:S(2)}) collective-permute-start(bf16[256,768]{1,0:T(8,128)(2,1)S(1)} %get-tuple-element.37.refs_0_), channel_id=1, source_target_pairs={{0,8},{1,33},{2,10},{3,35},{4,12},{5,37},{6,14},{7,39},{8,0},{9,41... | collective-permute-start | bytes 1179656 | tf_op jit(solution)/shard_map/ppermute | solution.py:59
  34.2 0.0 collective-permute-done.10.f_ref.refs_7_
  34.2 3.6 %residual.6 = (bf16[256,4096]{1,0:T(8,128)(2,1)S(1)}, bf16[256,768]{1,0:T(8,128)(2,1)S(1)}) custom-call(bf16[256,768]{1,0:T(8,128)(2,1)S(1)} %collective-permute-done.10.f_ref.refs_7_, bf16[2048,768]{1,0:T(8,128)(2,1)S(1)} %get-tuple-element.30.w0_ref, bf16[2048,768]{1,0:T(8,128)(2,1)S(1)} %collective-permute-done.7.w1_ref, ...), custom_call_target="tpu_custom_call" | custom-call | flops 524288 | tf_op jit(solution)/shard_map/residual/pallas_call | solution.py:215
  37.9 2.2 %collective-permute-start.12 = (bf16[256,768]{1,0:T(8,128)(2,1)S(1)}, bf16[256,768]{1,0:T(8,128)(2,1)S(1)}, u32[]{:S(2)}, u32[]{:S(2)}) collective-permute-start(bf16[256,768]{1,0:T(8,128)(2,1)S(1)} %get-tuple-element.38.refs_0_), channel_id=1, source_target_pairs={{0,24},{1,97},{2,26},{3,99},{4,28},{5,101},{6,30},{7,103},{8,16},{... | collective-permute-start | bytes 1179656 | tf_op jit(solution)/shard_map/ppermute | solution.py:59
  40.1 3.6 %residual.7 = (bf16[256,4096]{1,0:T(8,128)(2,1)S(1)}, bf16[256,768]{1,0:T(8,128)(2,1)S(1)}) custom-call(bf16[256,768]{1,0:T(8,128)(2,1)S(1)} %collective-permute-done.9.f_ref.refs_6_, bf16[2048,768]{1,0:T(8,128)(2,1)S(1)} %get-tuple-element.30.w0_ref, bf16[2048,768]{1,0:T(8,128)(2,1)S(1)} %collective-permute-done.7.w1_ref, ...), custom_call_target="tpu_custom_call" | custom-call | flops 524288 | tf_op jit(solution)/shard_map/residual/pallas_call | solution.py:215
  43.7 0.8 %collective-permute-start.15 = (bf16[256,768]{1,0:T(8,128)(2,1)S(1)}, bf16[256,768]{1,0:T(8,128)(2,1)S(1)}, u32[]{:S(2)}, u32[]{:S(2)}) collective-permute-start(bf16[256,768]{1,0:T(8,128)(2,1)S(1)} %get-tuple-element.41), channel_id=1, source_target_pairs={{0,16},{1,65},{2,18},{3,67},{4,20},{5,69},{6,22},{7,71},{8,24},{9,... | collective-permute-start | bytes 1179656 | tf_op jit(solution)/shard_map/ppermute | solution.py:59
  44.5 1.8 %weight_partial.3.refs_8_ = bf16[1024,768]{1,0:T(8,128)(2,1)S(1)} custom-call(bf16[256,4096]{1,0:T(8,128)(2,1)S(1)} %get-tuple-element.33.refs_0_, bf16[256,4096]{1,0:T(8,128)(2,1)S(1)} %get-tuple-element.35.refs_1_, bf16[256,4096]{1,0:T(8,128)(2,1)S(1)} %get-tuple-element.39.refs_2_, bf16[256,4096]{1,0:T(8,128)(2,1)S(1)} %get-tuple-element.40.refs_3_, ...), custom_call_target="tpu_custom_call" | custom-call | flops 65536 | tf_op jit(solution)/shard_map/weight_partial/pallas_call | solution.py:237
  46.3 0.1 collective-permute-start.14
  46.4 0.5 collective-permute-done.12.refs_8_.b_ref
  47.0 1.8 %weight_partial.4.refs_9_ = bf16[1024,768]{1,0:T(8,128)(2,1)S(1)} custom-call(bf16[256,4096]{1,0:T(8,128)(2,1)S(1)} %get-tuple-element.33.refs_0_, bf16[256,4096]{1,0:T(8,128)(2,1)S(1)} %get-tuple-element.35.refs_1_, bf16[256,4096]{1,0:T(8,128)(2,1)S(1)} %get-tuple-element.39.refs_2_, bf16[256,4096]{1,0:T(8,128)(2,1)S(1)} %get-tuple-element.40.refs_3_, ...), custom_call_target="tpu_custom_call" | custom-call | flops 65536 | tf_op jit(solution)/shard_map/weight_partial/pallas_call | solution.py:237
  48.8 0.1 collective-permute-start.13
  48.9 1.8 %weight_partial.5.refs_0_.mine_ref = f32[1024,768]{1,0:T(8,128)S(1)} custom-call(bf16[256,4096]{1,0:T(8,128)(2,1)S(1)} %get-tuple-element.33.refs_0_, bf16[256,4096]{1,0:T(8,128)(2,1)S(1)} %get-tuple-element.35.refs_1_, bf16[256,4096]{1,0:T(8,128)(2,1)S(1)} %get-tuple-element.39.refs_2_, bf16[256,4096]{1,0:T(8,128)(2,1)S(1)} %get-tuple-element.40.refs_3_, ...), custom_call_target="tpu_custom_call" | custom-call | flops 65536 | tf_op jit(solution)/shard_map/weight_partial/pallas_call | solution.py:237
  50.7 2.4 %collective-permute-done.15.c_ref = bf16[256,768]{1,0:T(8,128)(2,1)S(1)} collective-permute-done((bf16[256,768]{1,0:T(8,128)(2,1)S(1)}, bf16[256,768]{1,0:T(8,128)(2,1)S(1)}, u32[]{:S(2)}, u32[]{:S(2)}) %collective-permute-start.15) | collective-permute-done | bytes 393248 | tf_op jit(solution)/shard_map/ppermute | solution.py:59
  53.1 0.2 add.30
  53.2 0.6 collective-permute-start.16
  53.8 1.1 %collective-permute-start.17 = (bf16[64,768]{1,0:T(8,128)(2,1)S(1)}, bf16[64,768]{1,0:T(8,128)(2,1)S(1)}, u32[]{:S(2)}, u32[]{:S(2)}) collective-permute-start(bf16[64,768]{1,0:T(8,128)(2,1)S(1)} %get-tuple-element.42.refs_9_), channel_id=1, source_target_pairs={{0,32},{1,9},{2,34},{3,11},{4,36},{5,13},{6,38},{7,15},{8,40},{9,1... | collective-permute-start | bytes 294920 | tf_op jit(solution)/shard_map/ppermute | solution.py:76
  54.9 2.2 %collective-permute-start.18 = (bf16[64,768]{1,0:T(8,128)(2,1)S(1)}, bf16[64,768]{1,0:T(8,128)(2,1)S(1)}, u32[]{:S(2)}, u32[]{:S(2)}) collective-permute-start(bf16[64,768]{1,0:T(8,128)(2,1)S(1)} %get-tuple-element.44.refs_11_), channel_id=1, source_target_pairs={{0,96},{1,25},{2,98},{3,27},{4,100},{5,29},{6,102},{7,31},{8,104},... | collective-permute-start | bytes 294920 | tf_op jit(solution)/shard_map/ppermute | solution.py:76
  57.0 0.0 collective-permute-done.14.refs_8_
  57.0 2.8 %weight_rows.1 = (bf16[2048,768]{1,0:T(8,128)(2,1)}, f32[8,128]{1,0:T(8,128)S(1)}) custom-call(bf16[256,4096]{1,0:T(8,128)(2,1)S(1)} %get-tuple-element.33.refs_0_, bf16[256,4096]{1,0:T(8,128)(2,1)S(1)} %get-tuple-element.35.refs_1_, bf16[256,4096]{1,0:T(8,128)(2,1)S(1)} %get-tuple-element.39.refs_2_, bf16[256,4096]{1,0:T(8,128)(2,1)S(1)} %get-tuple-element.40.refs_3_, ...), custom_call_target="tpu_custom_call" | custom-call | flops 1610612736 | tf_op jit(solution)/shard_map/weight_rows/pallas_call | solution.py:270
  59.8 0.7 %collective-permute-done.17.b_ref = bf16[64,768]{1,0:T(8,128)(2,1)S(1)} collective-permute-done((bf16[64,768]{1,0:T(8,128)(2,1)S(1)}, bf16[64,768]{1,0:T(8,128)(2,1)S(1)}, u32[]{:S(2)}, u32[]{:S(2)}) %collective-permute-start.17) | collective-permute-done | bytes 98336 | tf_op jit(solution)/shard_map/ppermute | solution.py:76
  60.6 1.2 %collective-permute-start.19 = (bf16[16,768]{1,0:T(8,128)(2,1)S(1)}, bf16[16,768]{1,0:T(8,128)(2,1)S(1)}, u32[]{:S(2)}, u32[]{:S(2)}) collective-permute-start(bf16[16,768]{1,0:T(8,128)(2,1)S(1)} %get-tuple-element.49.refs_2_), channel_id=1, source_target_pairs={{0,4},{1,5},{2,6},{3,7},{4,0},{5,1},{6,2},{7,3},{8,12},{9,13},{10,... | collective-permute-start | bytes 73736 | tf_op jit(solution)/shard_map/ppermute | solution.py:76
  61.8 3.2 %collective-permute-start.21 = (bf16[16,768]{1,0:T(8,128)(2,1)S(1)}, bf16[16,768]{1,0:T(8,128)(2,1)S(1)}, u32[]{:S(2)}, u32[]{:S(2)}) collective-permute-start(bf16[16,768]{1,0:T(8,128)(2,1)S(1)} %get-tuple-element.50.refs_3_), channel_id=1, source_target_pairs={{0,6},{1,7},{2,0},{3,1},{4,2},{5,3},{6,4},{7,5},{8,14},{9,15},{10,... | collective-permute-start | bytes 73736 | tf_op jit(solution)/shard_map/ppermute | solution.py:76
  65.0 1.2 %finish_rows.1 = (bf16[2048,768]{1,0:T(8,128)(2,1)}, f32[8,128]{1,0:T(8,128)S(1)}) custom-call(f32[1024,768]{1,0:T(8,128)S(1)} %weight_partial.5.refs_0_.mine_ref, bf16[1024,768]{1,0:T(8,128)(2,1)S(1)} %collective-permute-done.13.other_ref, bf16[2048,768]{1,0:T(8,128)(2,1)} %get-tuple-element.45.refs_0_, ...), custom_call_target="tpu_custom_call", output_to_operand_aliasing={{0}: (2, {})} | custom-call | flops 1610612736 | tf_op jit(solution)/shard_map/finish_rows/pallas_call | solution.py:299
  66.3 0.5 collective-permute-done.20.b_ref
  66.8 0.6 add.32
  (13 shorter events, 0.1 us)
Async XLA Ops:
  0.6 8.2 %collective-permute-start.1 = (bf16[16,768]{1,0:T(8,128)(2,1)}, bf16[16,768]{1,0:T(8,128)(2,1)S(1)}, u32[]{:S(2)}, u32[]{:S(2)}) collective-permute-start(bf16[16,768]{1,0:T(8,128)(2,1)} %x_ref.1), channel_id=1, source_target_pairs={{0,4},{1,5},{2,6},{3,7},{4,0},{5,1},{6,2},{7,3},{8,12},{9,13},{10,... | collective-permute-start | bytes 73736 | tf_op jit(solution)/shard_map/ppermute | solution.py:72
  4.7 4.2 %collective-permute-start.2 = (bf16[16,768]{1,0:T(8,128)(2,1)}, bf16[16,768]{1,0:T(8,128)(2,1)S(1)}, u32[]{:S(2)}, u32[]{:S(2)}) collective-permute-start(bf16[16,768]{1,0:T(8,128)(2,1)} %x_ref.1), channel_id=1, source_target_pairs={{0,6},{1,7},{2,0},{3,1},{4,2},{5,3},{6,4},{7,5},{8,14},{9,15},{10,... | collective-permute-start | bytes 73736 | tf_op jit(solution)/shard_map/ppermute | solution.py:72
  5.4 5.2 %collective-permute-start.3 = (bf16[16,768]{1,0:T(8,128)(2,1)}, bf16[16,768]{1,0:T(8,128)(2,1)S(1)}, u32[]{:S(2)}, u32[]{:S(2)}) collective-permute-start(bf16[16,768]{1,0:T(8,128)(2,1)} %x_ref.1), channel_id=1, source_target_pairs={{0,2},{1,3},{2,4},{3,5},{4,6},{5,7},{6,0},{7,1},{8,10},{9,11},{10,... | collective-permute-start | bytes 73736 | tf_op jit(solution)/shard_map/ppermute | solution.py:72
  6.7 1.4 %collective-permute-start = (f32[1,2048]{1,0:T(1,128)}, f32[1,2048]{1,0:T(1,128)S(1)}, u32[]{:S(2)}, u32[]{:S(2)}) collective-permute-start(f32[1,2048]{1,0:T(1,128)} %bitcast.9), channel_id=1, source_target_pairs={{0,1},{1,0},{2,3},{3,2},{4,5},{5,4},{6,7},{7,6},{8,9},{9,8},{10,11... | collective-permute-start | bytes 24584 | tf_op jit(solution)/shard_map/ppermute | solution.py:83
  10.6 14.0 %collective-permute-start.7 = (bf16[2048,768]{1,0:T(8,128)(2,1)}, bf16[2048,768]{1,0:T(8,128)(2,1)S(1)}, u32[]{:S(2)}, u32[]{:S(2)}) collective-permute-start(bf16[2048,768]{1,0:T(8,128)(2,1)} %w_ref.1), channel_id=1, source_target_pairs={{0,1},{1,0},{2,3},{3,2},{4,5},{5,4},{6,7},{7,6},{8,9},{9,8},{10,11... | collective-permute-start | bytes 9437192 | tf_op jit(solution)/shard_map/ppermute | solution.py:83
  10.7 8.6 %collective-permute-start.4 = (bf16[64,768]{1,0:T(8,128)(2,1)S(1)}, bf16[64,768]{1,0:T(8,128)(2,1)S(1)}, u32[]{:S(2)}, u32[]{:S(2)}) collective-permute-start(bf16[64,768]{1,0:T(8,128)(2,1)S(1)} %join.2.refs_0_), channel_id=1, source_target_pairs={{0,64},{1,17},{2,66},{3,19},{4,68},{5,21},{6,70},{7,23},{8,72},{9,... | collective-permute-start | bytes 294920 | tf_op jit(solution)/shard_map/ppermute | solution.py:72
  14.0 5.3 %collective-permute-start.5 = (bf16[64,768]{1,0:T(8,128)(2,1)S(1)}, bf16[64,768]{1,0:T(8,128)(2,1)S(1)}, u32[]{:S(2)}, u32[]{:S(2)}) collective-permute-start(bf16[64,768]{1,0:T(8,128)(2,1)S(1)} %join.2.refs_0_), channel_id=1, source_target_pairs={{0,96},{1,25},{2,98},{3,27},{4,100},{5,29},{6,102},{7,31},{8,104},... | collective-permute-start | bytes 294920 | tf_op jit(solution)/shard_map/ppermute | solution.py:72
  15.1 5.8 %collective-permute-start.6 = (bf16[64,768]{1,0:T(8,128)(2,1)S(1)}, bf16[64,768]{1,0:T(8,128)(2,1)S(1)}, u32[]{:S(2)}, u32[]{:S(2)}) collective-permute-start(bf16[64,768]{1,0:T(8,128)(2,1)S(1)} %join.2.refs_0_), channel_id=1, source_target_pairs={{0,32},{1,9},{2,34},{3,11},{4,36},{5,13},{6,38},{7,15},{8,40},{9,1... | collective-permute-start | bytes 294920 | tf_op jit(solution)/shard_map/ppermute | solution.py:72
  20.9 8.0 %collective-permute-start.8 = (bf16[256,768]{1,0:T(8,128)(2,1)S(1)}, bf16[256,768]{1,0:T(8,128)(2,1)S(1)}, u32[]{:S(2)}, u32[]{:S(2)}) collective-permute-start(bf16[256,768]{1,0:T(8,128)(2,1)S(1)} %join.3.f_ref.refs_4_), channel_id=1, source_target_pairs={{0,8},{1,33},{2,10},{3,35},{4,12},{5,37},{6,14},{7,39},{8,0},{9,41... | collective-permute-start | bytes 1179656 | tf_op jit(solution)/shard_map/ppermute | solution.py:59
  22.5 11.7 %collective-permute-start.10 = (bf16[256,768]{1,0:T(8,128)(2,1)S(1)}, bf16[256,768]{1,0:T(8,128)(2,1)S(1)}, u32[]{:S(2)}, u32[]{:S(2)}) collective-permute-start(bf16[256,768]{1,0:T(8,128)(2,1)S(1)} %join.3.f_ref.refs_4_), channel_id=1, source_target_pairs={{0,24},{1,97},{2,26},{3,99},{4,28},{5,101},{6,30},{7,103},{8,16},{... | collective-permute-start | bytes 1179656 | tf_op jit(solution)/shard_map/ppermute | solution.py:59
  28.2 11.8 %collective-permute-start.9 = (bf16[256,768]{1,0:T(8,128)(2,1)S(1)}, bf16[256,768]{1,0:T(8,128)(2,1)S(1)}, u32[]{:S(2)}, u32[]{:S(2)}) collective-permute-start(bf16[256,768]{1,0:T(8,128)(2,1)S(1)} %get-tuple-element.36), channel_id=1, source_target_pairs={{0,16},{1,65},{2,18},{3,67},{4,20},{5,69},{6,22},{7,71},{8,24},{9,... | collective-permute-start | bytes 1179656 | tf_op jit(solution)/shard_map/ppermute | solution.py:59
  32.7 11.8 %collective-permute-start.11 = (bf16[256,768]{1,0:T(8,128)(2,1)S(1)}, bf16[256,768]{1,0:T(8,128)(2,1)S(1)}, u32[]{:S(2)}, u32[]{:S(2)}) collective-permute-start(bf16[256,768]{1,0:T(8,128)(2,1)S(1)} %get-tuple-element.37.refs_0_), channel_id=1, source_target_pairs={{0,8},{1,33},{2,10},{3,35},{4,12},{5,37},{6,14},{7,39},{8,0},{9,41... | collective-permute-start | bytes 1179656 | tf_op jit(solution)/shard_map/ppermute | solution.py:59
  37.9 9.1 %collective-permute-start.12 = (bf16[256,768]{1,0:T(8,128)(2,1)S(1)}, bf16[256,768]{1,0:T(8,128)(2,1)S(1)}, u32[]{:S(2)}, u32[]{:S(2)}) collective-permute-start(bf16[256,768]{1,0:T(8,128)(2,1)S(1)} %get-tuple-element.38.refs_0_), channel_id=1, source_target_pairs={{0,24},{1,97},{2,26},{3,99},{4,28},{5,101},{6,30},{7,103},{8,16},{... | collective-permute-start | bytes 1179656 | tf_op jit(solution)/shard_map/ppermute | solution.py:59
  43.7 9.4 %collective-permute-start.15 = (bf16[256,768]{1,0:T(8,128)(2,1)S(1)}, bf16[256,768]{1,0:T(8,128)(2,1)S(1)}, u32[]{:S(2)}, u32[]{:S(2)}) collective-permute-start(bf16[256,768]{1,0:T(8,128)(2,1)S(1)} %get-tuple-element.41), channel_id=1, source_target_pairs={{0,16},{1,65},{2,18},{3,67},{4,20},{5,69},{6,22},{7,71},{8,24},{9,... | collective-permute-start | bytes 1179656 | tf_op jit(solution)/shard_map/ppermute | solution.py:59
  46.3 10.7 %collective-permute-start.14 = (bf16[1024,768]{1,0:T(8,128)(2,1)S(1)}, bf16[1024,768]{1,0:T(8,128)(2,1)S(1)}, u32[]{:S(2)}, u32[]{:S(2)}) collective-permute-start(bf16[1024,768]{1,0:T(8,128)(2,1)S(1)} %weight_partial.3.refs_8_), channel_id=1, source_target_pairs={{0,1},{1,0},{2,3},{3,2},{4,5},{5,4},{6,7},{7,6},{8,9},{9,8},{10,11... | collective-permute-start | bytes 4718600 | tf_op jit(solution)/shard_map/ppermute | solution.py:83
  48.8 16.2 %collective-permute-start.13 = (bf16[1024,768]{1,0:T(8,128)(2,1)S(1)}, bf16[1024,768]{1,0:T(8,128)(2,1)S(1)}, u32[]{:S(2)}, u32[]{:S(2)}) collective-permute-start(bf16[1024,768]{1,0:T(8,128)(2,1)S(1)} %weight_partial.4.refs_9_), channel_id=1, source_target_pairs={{0,1},{1,0},{2,3},{3,2},{4,5},{5,4},{6,7},{7,6},{8,9},{9,8},{10,11... | collective-permute-start | bytes 4718600 | tf_op jit(solution)/shard_map/ppermute | solution.py:83
  53.2 6.6 %collective-permute-start.16 = (bf16[64,768]{1,0:T(8,128)(2,1)S(1)}, bf16[64,768]{1,0:T(8,128)(2,1)S(1)}, u32[]{:S(2)}, u32[]{:S(2)}) collective-permute-start(bf16[64,768]{1,0:T(8,128)(2,1)S(1)} %get-tuple-element.43.refs_10_), channel_id=1, source_target_pairs={{0,64},{1,17},{2,66},{3,19},{4,68},{5,21},{6,70},{7,23},{8,72},{9,... | collective-permute-start | bytes 294920 | tf_op jit(solution)/shard_map/ppermute | solution.py:76
  53.8 6.7 %collective-permute-start.17 = (bf16[64,768]{1,0:T(8,128)(2,1)S(1)}, bf16[64,768]{1,0:T(8,128)(2,1)S(1)}, u32[]{:S(2)}, u32[]{:S(2)}) collective-permute-start(bf16[64,768]{1,0:T(8,128)(2,1)S(1)} %get-tuple-element.42.refs_9_), channel_id=1, source_target_pairs={{0,32},{1,9},{2,34},{3,11},{4,36},{5,13},{6,38},{7,15},{8,40},{9,1... | collective-permute-start | bytes 294920 | tf_op jit(solution)/shard_map/ppermute | solution.py:76
  54.9 5.6 %collective-permute-start.18 = (bf16[64,768]{1,0:T(8,128)(2,1)S(1)}, bf16[64,768]{1,0:T(8,128)(2,1)S(1)}, u32[]{:S(2)}, u32[]{:S(2)}) collective-permute-start(bf16[64,768]{1,0:T(8,128)(2,1)S(1)} %get-tuple-element.44.refs_11_), channel_id=1, source_target_pairs={{0,96},{1,25},{2,98},{3,27},{4,100},{5,29},{6,102},{7,31},{8,104},... | collective-permute-start | bytes 294920 | tf_op jit(solution)/shard_map/ppermute | solution.py:76
  60.6 5.7 %collective-permute-start.19 = (bf16[16,768]{1,0:T(8,128)(2,1)S(1)}, bf16[16,768]{1,0:T(8,128)(2,1)S(1)}, u32[]{:S(2)}, u32[]{:S(2)}) collective-permute-start(bf16[16,768]{1,0:T(8,128)(2,1)S(1)} %get-tuple-element.49.refs_2_), channel_id=1, source_target_pairs={{0,4},{1,5},{2,6},{3,7},{4,0},{5,1},{6,2},{7,3},{8,12},{9,13},{10,... | collective-permute-start | bytes 73736 | tf_op jit(solution)/shard_map/ppermute | solution.py:76
  61.8 5.0 %collective-permute-start.20 = (bf16[16,768]{1,0:T(8,128)(2,1)S(1)}, bf16[16,768]{1,0:T(8,128)(2,1)S(1)}, u32[]{:S(2)}, u32[]{:S(2)}) collective-permute-start(bf16[16,768]{1,0:T(8,128)(2,1)S(1)} %get-tuple-element.48.refs_1_), channel_id=1, source_target_pairs={{0,2},{1,3},{2,4},{3,5},{4,6},{5,7},{6,0},{7,1},{8,10},{9,11},{10,... | collective-permute-start | bytes 73736 | tf_op jit(solution)/shard_map/ppermute | solution.py:76
  61.8 5.0 %collective-permute-start.21 = (bf16[16,768]{1,0:T(8,128)(2,1)S(1)}, bf16[16,768]{1,0:T(8,128)(2,1)S(1)}, u32[]{:S(2)}, u32[]{:S(2)}) collective-permute-start(bf16[16,768]{1,0:T(8,128)(2,1)S(1)} %get-tuple-element.50.refs_3_), channel_id=1, source_target_pairs={{0,6},{1,7},{2,0},{3,1},{4,2},{5,3},{6,4},{7,5},{8,14},{9,15},{10,... | collective-permute-start | bytes 73736 | tf_op jit(solution)/shard_map/ppermute | solution.py:76

commit v6 on v5

--- a/solution.py
+++ b/solution.py
@@ -344,7 +344,7 @@
     b0 = label_bias.reshape(1, own)
     b1 = swap(b0)
     near = [fetch(features, "first", k) for k in ORDERED[1:]]
-    f64 = join([load(features, (b1,))] + near, factor=0.5)
+    f64 = join([load(features, ())] + near, factor=0.5, after=(b1,))
     late, f64 = lax.optimization_barrier((label_weight, f64))
     w1 = swap(late)
     w0, words, b = prepare(piece, pos, label_weight, positive_ids.T, positive_counts.reshape(1, -1), b0, b1, after=(f64,))

time: 67.6 us -> 67.6 us (level)
    ppermute x4, waiting for transfers between devices: 1.39 us -> 0.62 us  [swap(): return lax.ppermute(x, AXES, [(d, d ^ 1) for d in range(2 * N * N * N)])]
    ppermute x6, waiting for transfers between devices: 3.38 us -> 4.12 us  [fetch(): return lax.ppermute(x, AXES, shifted(stage, -k))]
  transfers between devices with their start and end apart: 22 -> 22, of which waited for: 7 -> 8; matrix products, arithmetic and copies ran while one was open for 0% -> 0% of each run, Pallas kernels for 42% -> 42%
where the time goes in v6:
time: 67.6 us; the launch traced here: 67.5 us
  Pallas kernels  28.9 us (43%)
  starting transfers between devices  28.8 us (43%)
  waiting for transfers between devices  8.89 us (13%)
  between operations  0.79 us (1%)
    pallas_call x4, Pallas kernels, residual(): pl.pallas_call(functools.partial(residual_kernel, chunk, again), in_specs...  14.6 us
    ppermute x6, starting transfers between devices, fetch(): return lax.ppermute(x, AXES, shifted(stage, -k))  11.4 us
    ppermute x6, starting transfers between devices, exchange(): return lax.ppermute(x, AXES, partners(stage, k))  8.89 us
    ppermute x6, starting transfers between devices, push(): return lax.ppermute(x, AXES, shifted(stage, k))  8.27 us
    pallas_call x3, Pallas kernels, weight_partial(): pl.pallas_call(functools.partial(weight_partial_kernel, start), in_specs=...  5.47 us
    ppermute x6, waiting for transfers between devices, fetch(): return lax.ppermute(x, AXES, shifted(stage, -k))  4.12 us
    pallas_call x1, Pallas kernels, prepare(): pl.pallas_call(functools.partial(prepare_kernel, piece), in_specs=[SCALAR...  3.18 us
    ppermute x6, waiting for transfers between devices, exchange(): return lax.ppermute(x, AXES, partners(stage, k))  2.91 us
  transfers between devices with their start and end apart: 22, of which 8 were waited for; matrix products, arithmetic and copies ran while one was open for 0% of the time, Pallas kernels for 42%

profile of v6, /device:TPU:0, one launch (start us, length us, event | category | flops | bytes accessed | tf_op | source)
XLA Modules:
  0.0 67.5 jit_solution(17705449189670713084)
XLA Ops:
  0.6 4.0 %collective-permute-start = (bf16[16,768]{1,0:T(8,128)(2,1)}, bf16[16,768]{1,0:T(8,128)(2,1)S(1)}, u32[]{:S(2)}, u32[]{:S(2)}) collective-permute-start(bf16[16,768]{1,0:T(8,128)(2,1)} %x_ref.1), channel_id=1, source_target_pairs={{0,4},{1,5},{2,6},{3,7},{4,0},{5,1},{6,2},{7,3},{8,12},{9,13},{10,... | collective-permute-start | bytes 73736 | tf_op jit(solution)/shard_map/ppermute | solution.py:72
  4.7 0.7 %collective-permute-start.1 = (bf16[16,768]{1,0:T(8,128)(2,1)}, bf16[16,768]{1,0:T(8,128)(2,1)S(1)}, u32[]{:S(2)}, u32[]{:S(2)}) collective-permute-start(bf16[16,768]{1,0:T(8,128)(2,1)} %x_ref.1), channel_id=1, source_target_pairs={{0,6},{1,7},{2,0},{3,1},{4,2},{5,3},{6,4},{7,5},{8,14},{9,15},{10,... | collective-permute-start | bytes 73736 | tf_op jit(solution)/shard_map/ppermute | solution.py:72
  5.4 1.3 %collective-permute-start.2 = (bf16[16,768]{1,0:T(8,128)(2,1)}, bf16[16,768]{1,0:T(8,128)(2,1)S(1)}, u32[]{:S(2)}, u32[]{:S(2)}) collective-permute-start(bf16[16,768]{1,0:T(8,128)(2,1)} %x_ref.1), channel_id=1, source_target_pairs={{0,2},{1,3},{2,4},{3,5},{4,6},{5,7},{6,0},{7,1},{8,10},{9,11},{10,... | collective-permute-start | bytes 73736 | tf_op jit(solution)/shard_map/ppermute | solution.py:72
  6.7 0.0 collective-permute-start.3
  6.7 0.8 %load.1.refs_0_ = bf16[16,768]{1,0:T(8,128)(2,1)S(1)} custom-call(bf16[16,768]{1,0:T(8,128)(2,1)} %x_ref.1), custom_call_target="tpu_custom_call" | custom-call | tf_op jit(solution)/shard_map/load/pallas_call | solution.py:160
  7.5 0.6 collective-permute-done.3.refs_4_.b1_ref
  8.1 0.0 collective-permute-done.refs_1_
  8.1 0.6 collective-permute-done.1.refs_2_
  8.7 1.9 %collective-permute-done.2.refs_3_ = bf16[16,768]{1,0:T(8,128)(2,1)S(1)} collective-permute-done((bf16[16,768]{1,0:T(8,128)(2,1)}, bf16[16,768]{1,0:T(8,128)(2,1)S(1)}, u32[]{:S(2)}, u32[]{:S(2)}) %collective-permute-start.2) | collective-permute-done | bytes 24608 | tf_op jit(solution)/shard_map/ppermute | solution.py:72
  10.6 0.1 collective-permute-start.7
  10.7 3.3 %collective-permute-start.4 = (bf16[64,768]{1,0:T(8,128)(2,1)S(1)}, bf16[64,768]{1,0:T(8,128)(2,1)S(1)}, u32[]{:S(2)}, u32[]{:S(2)}) collective-permute-start(bf16[64,768]{1,0:T(8,128)(2,1)S(1)} %join.2.refs_0_), channel_id=1, source_target_pairs={{0,64},{1,17},{2,66},{3,19},{4,68},{5,21},{6,70},{7,23},{8,72},{9,... | collective-permute-start | bytes 294920 | tf_op jit(solution)/shard_map/ppermute | solution.py:72
  14.0 1.1 %collective-permute-start.5 = (bf16[64,768]{1,0:T(8,128)(2,1)S(1)}, bf16[64,768]{1,0:T(8,128)(2,1)S(1)}, u32[]{:S(2)}, u32[]{:S(2)}) collective-permute-start(bf16[64,768]{1,0:T(8,128)(2,1)S(1)} %join.2.refs_0_), channel_id=1, source_target_pairs={{0,96},{1,25},{2,98},{3,27},{4,100},{5,29},{6,102},{7,31},{8,104},... | collective-permute-start | bytes 294920 | tf_op jit(solution)/shard_map/ppermute | solution.py:72
  15.1 1.0 %collective-permute-start.6 = (bf16[64,768]{1,0:T(8,128)(2,1)S(1)}, bf16[64,768]{1,0:T(8,128)(2,1)S(1)}, u32[]{:S(2)}, u32[]{:S(2)}) collective-permute-start(bf16[64,768]{1,0:T(8,128)(2,1)S(1)} %join.2.refs_0_), channel_id=1, source_target_pairs={{0,32},{1,9},{2,34},{3,11},{4,36},{5,13},{6,38},{7,15},{8,40},{9,1... | collective-permute-start | bytes 294920 | tf_op jit(solution)/shard_map/ppermute | solution.py:72
  16.0 0.1 stack.23.pos_ref
  16.1 3.2 %prepare.1 = (bf16[2048,768]{1,0:T(8,128)(2,1)S(1)}, s32[1024,128]{1,0:T(8,128)S(1)}, f32[1,4096]{1,0:T(1,128)S(1)}) custom-call(s32[6]{0:T(128)S(1)} %stack.23.pos_ref, f32[1,2048]{1,0:T(1,128)S(1)} %collective-permute-done.3.refs_4_.b1_ref, bf16[2048,768]{1,0:T(8,128)(2,1)} %w_ref.1, s32[16,2048]{1,0:T(8,128)} %bitcast.8, s32[1,2048]{1,0:T(1,128)} %bitcast.11, ...), custom_call_target="tpu_custom_call" | custom-call | tf_op jit(solution)/shard_map/prepare/pallas_call | solution.py:134
  19.3 0.0 collective-permute-done.5.refs_2_
  19.3 1.6 %collective-permute-done.6.refs_3_ = bf16[64,768]{1,0:T(8,128)(2,1)S(1)} collective-permute-done((bf16[64,768]{1,0:T(8,128)(2,1)S(1)}, bf16[64,768]{1,0:T(8,128)(2,1)S(1)}, u32[]{:S(2)}, u32[]{:S(2)}) %collective-permute-start.6) | collective-permute-done | bytes 98336 | tf_op jit(solution)/shard_map/ppermute | solution.py:72
  20.9 1.6 %collective-permute-start.8 = (bf16[256,768]{1,0:T(8,128)(2,1)S(1)}, bf16[256,768]{1,0:T(8,128)(2,1)S(1)}, u32[]{:S(2)}, u32[]{:S(2)}) collective-permute-start(bf16[256,768]{1,0:T(8,128)(2,1)S(1)} %join.3.f_ref.refs_4_), channel_id=1, source_target_pairs={{0,8},{1,33},{2,10},{3,35},{4,12},{5,37},{6,14},{7,39},{8,0},{9,41... | collective-permute-start | bytes 1179656 | tf_op jit(solution)/shard_map/ppermute | solution.py:59
  22.5 2.1 %collective-permute-start.10 = (bf16[256,768]{1,0:T(8,128)(2,1)S(1)}, bf16[256,768]{1,0:T(8,128)(2,1)S(1)}, u32[]{:S(2)}, u32[]{:S(2)}) collective-permute-start(bf16[256,768]{1,0:T(8,128)(2,1)S(1)} %join.3.f_ref.refs_4_), channel_id=1, source_target_pairs={{0,24},{1,97},{2,26},{3,99},{4,28},{5,101},{6,30},{7,103},{8,16},{... | collective-permute-start | bytes 1179656 | tf_op jit(solution)/shard_map/ppermute | solution.py:59
  24.6 0.0 collective-permute-done.7.w1_ref
  24.6 3.6 %residual.4 = (bf16[256,4096]{1,0:T(8,128)(2,1)S(1)}, f32[256,768]{1,0:T(8,128)S(1)}, bf16[256,768]{1,0:T(8,128)(2,1)S(1)}) custom-call(bf16[256,768]{1,0:T(8,128)(2,1)S(1)} %join.3.f_ref.refs_4_, bf16[2048,768]{1,0:T(8,128)(2,1)S(1)} %get-tuple-element.30.w0_ref, bf16[2048,768]{1,0:T(8,128)(2,1)S(1)} %collective-permute-done.7.w1_ref, ...), custom_call_target="tpu_custom_call" | custom-call | flops 524288 | tf_op jit(solution)/shard_map/residual/pallas_call | solution.py:215
  28.2 0.7 %collective-permute-start.9 = (bf16[256,768]{1,0:T(8,128)(2,1)S(1)}, bf16[256,768]{1,0:T(8,128)(2,1)S(1)}, u32[]{:S(2)}, u32[]{:S(2)}) collective-permute-start(bf16[256,768]{1,0:T(8,128)(2,1)S(1)} %get-tuple-element.36), channel_id=1, source_target_pairs={{0,16},{1,65},{2,18},{3,67},{4,20},{5,69},{6,22},{7,71},{8,24},{9,... | collective-permute-start | bytes 1179656 | tf_op jit(solution)/shard_map/ppermute | solution.py:59
  29.0 3.7 %residual.5 = (bf16[256,4096]{1,0:T(8,128)(2,1)S(1)}, bf16[256,768]{1,0:T(8,128)(2,1)S(1)}) custom-call(bf16[256,768]{1,0:T(8,128)(2,1)S(1)} %collective-permute-done.8.f_ref.refs_5_, bf16[2048,768]{1,0:T(8,128)(2,1)S(1)} %get-tuple-element.30.w0_ref, bf16[2048,768]{1,0:T(8,128)(2,1)S(1)} %collective-permute-done.7.w1_ref, ...), custom_call_target="tpu_custom_call" | custom-call | flops 524288 | tf_op jit(solution)/shard_map/residual/pallas_call | solution.py:215
  32.7 1.6 %collective-permute-start.11 = (bf16[256,768]{1,0:T(8,128)(2,1)S(1)}, bf16[256,768]{1,0:T(8,128)(2,1)S(1)}, u32[]{:S(2)}, u32[]{:S(2)}) collective-permute-start(bf16[256,768]{1,0:T(8,128)(2,1)S(1)} %get-tuple-element.37.refs_0_), channel_id=1, source_target_pairs={{0,8},{1,33},{2,10},{3,35},{4,12},{5,37},{6,14},{7,39},{8,0},{9,41... | collective-permute-start | bytes 1179656 | tf_op jit(solution)/shard_map/ppermute | solution.py:59
  34.2 0.0 collective-permute-done.10.f_ref.refs_7_
  34.2 3.6 %residual.6 = (bf16[256,4096]{1,0:T(8,128)(2,1)S(1)}, bf16[256,768]{1,0:T(8,128)(2,1)S(1)}) custom-call(bf16[256,768]{1,0:T(8,128)(2,1)S(1)} %collective-permute-done.10.f_ref.refs_7_, bf16[2048,768]{1,0:T(8,128)(2,1)S(1)} %get-tuple-element.30.w0_ref, bf16[2048,768]{1,0:T(8,128)(2,1)S(1)} %collective-permute-done.7.w1_ref, ...), custom_call_target="tpu_custom_call" | custom-call | flops 524288 | tf_op jit(solution)/shard_map/residual/pallas_call | solution.py:215
  37.9 2.2 %collective-permute-start.12 = (bf16[256,768]{1,0:T(8,128)(2,1)S(1)}, bf16[256,768]{1,0:T(8,128)(2,1)S(1)}, u32[]{:S(2)}, u32[]{:S(2)}) collective-permute-start(bf16[256,768]{1,0:T(8,128)(2,1)S(1)} %get-tuple-element.38.refs_0_), channel_id=1, source_target_pairs={{0,24},{1,97},{2,26},{3,99},{4,28},{5,101},{6,30},{7,103},{8,16},{... | collective-permute-start | bytes 1179656 | tf_op jit(solution)/shard_map/ppermute | solution.py:59
  40.1 3.6 %residual.7 = (bf16[256,4096]{1,0:T(8,128)(2,1)S(1)}, bf16[256,768]{1,0:T(8,128)(2,1)S(1)}) custom-call(bf16[256,768]{1,0:T(8,128)(2,1)S(1)} %collective-permute-done.9.f_ref.refs_6_, bf16[2048,768]{1,0:T(8,128)(2,1)S(1)} %get-tuple-element.30.w0_ref, bf16[2048,768]{1,0:T(8,128)(2,1)S(1)} %collective-permute-done.7.w1_ref, ...), custom_call_target="tpu_custom_call" | custom-call | flops 524288 | tf_op jit(solution)/shard_map/residual/pallas_call | solution.py:215
  43.7 0.8 %collective-permute-start.15 = (bf16[256,768]{1,0:T(8,128)(2,1)S(1)}, bf16[256,768]{1,0:T(8,128)(2,1)S(1)}, u32[]{:S(2)}, u32[]{:S(2)}) collective-permute-start(bf16[256,768]{1,0:T(8,128)(2,1)S(1)} %get-tuple-element.41), channel_id=1, source_target_pairs={{0,16},{1,65},{2,18},{3,67},{4,20},{5,69},{6,22},{7,71},{8,24},{9,... | collective-permute-start | bytes 1179656 | tf_op jit(solution)/shard_map/ppermute | solution.py:59
  44.5 1.8 %weight_partial.3.refs_8_ = bf16[1024,768]{1,0:T(8,128)(2,1)S(1)} custom-call(bf16[256,4096]{1,0:T(8,128)(2,1)S(1)} %get-tuple-element.33.refs_0_, bf16[256,4096]{1,0:T(8,128)(2,1)S(1)} %get-tuple-element.35.refs_1_, bf16[256,4096]{1,0:T(8,128)(2,1)S(1)} %get-tuple-element.39.refs_2_, bf16[256,4096]{1,0:T(8,128)(2,1)S(1)} %get-tuple-element.40.refs_3_, ...), custom_call_target="tpu_custom_call" | custom-call | flops 65536 | tf_op jit(solution)/shard_map/weight_partial/pallas_call | solution.py:237
  46.3 0.1 collective-permute-start.14
  46.4 0.5 collective-permute-done.12.refs_8_.b_ref
  47.0 1.8 %weight_partial.4.refs_9_ = bf16[1024,768]{1,0:T(8,128)(2,1)S(1)} custom-call(bf16[256,4096]{1,0:T(8,128)(2,1)S(1)} %get-tuple-element.33.refs_0_, bf16[256,4096]{1,0:T(8,128)(2,1)S(1)} %get-tuple-element.35.refs_1_, bf16[256,4096]{1,0:T(8,128)(2,1)S(1)} %get-tuple-element.39.refs_2_, bf16[256,4096]{1,0:T(8,128)(2,1)S(1)} %get-tuple-element.40.refs_3_, ...), custom_call_target="tpu_custom_call" | custom-call | flops 65536 | tf_op jit(solution)/shard_map/weight_partial/pallas_call | solution.py:237
  48.8 0.1 collective-permute-start.13
  48.9 1.8 %weight_partial.5.refs_0_.mine_ref = f32[1024,768]{1,0:T(8,128)S(1)} custom-call(bf16[256,4096]{1,0:T(8,128)(2,1)S(1)} %get-tuple-element.33.refs_0_, bf16[256,4096]{1,0:T(8,128)(2,1)S(1)} %get-tuple-element.35.refs_1_, bf16[256,4096]{1,0:T(8,128)(2,1)S(1)} %get-tuple-element.39.refs_2_, bf16[256,4096]{1,0:T(8,128)(2,1)S(1)} %get-tuple-element.40.refs_3_, ...), custom_call_target="tpu_custom_call" | custom-call | flops 65536 | tf_op jit(solution)/shard_map/weight_partial/pallas_call | solution.py:237
  50.7 2.4 %collective-permute-done.15.c_ref = bf16[256,768]{1,0:T(8,128)(2,1)S(1)} collective-permute-done((bf16[256,768]{1,0:T(8,128)(2,1)S(1)}, bf16[256,768]{1,0:T(8,128)(2,1)S(1)}, u32[]{:S(2)}, u32[]{:S(2)}) %collective-permute-start.15) | collective-permute-done | bytes 393248 | tf_op jit(solution)/shard_map/ppermute | solution.py:59
  53.1 0.2 add.30
  53.2 0.6 collective-permute-start.16
  53.8 1.1 %collective-permute-start.17 = (bf16[64,768]{1,0:T(8,128)(2,1)S(1)}, bf16[64,768]{1,0:T(8,128)(2,1)S(1)}, u32[]{:S(2)}, u32[]{:S(2)}) collective-permute-start(bf16[64,768]{1,0:T(8,128)(2,1)S(1)} %get-tuple-element.42.refs_9_), channel_id=1, source_target_pairs={{0,32},{1,9},{2,34},{3,11},{4,36},{5,13},{6,38},{7,15},{8,40},{9,1... | collective-permute-start | bytes 294920 | tf_op jit(solution)/shard_map/ppermute | solution.py:76
  54.9 2.2 %collective-permute-start.18 = (bf16[64,768]{1,0:T(8,128)(2,1)S(1)}, bf16[64,768]{1,0:T(8,128)(2,1)S(1)}, u32[]{:S(2)}, u32[]{:S(2)}) collective-permute-start(bf16[64,768]{1,0:T(8,128)(2,1)S(1)} %get-tuple-element.44.refs_11_), channel_id=1, source_target_pairs={{0,96},{1,25},{2,98},{3,27},{4,100},{5,29},{6,102},{7,31},{8,104},... | collective-permute-start | bytes 294920 | tf_op jit(solution)/shard_map/ppermute | solution.py:76
  57.0 0.0 collective-permute-done.14.refs_8_
  57.0 2.8 %weight_rows.1 = (bf16[2048,768]{1,0:T(8,128)(2,1)}, f32[8,128]{1,0:T(8,128)S(1)}) custom-call(bf16[256,4096]{1,0:T(8,128)(2,1)S(1)} %get-tuple-element.33.refs_0_, bf16[256,4096]{1,0:T(8,128)(2,1)S(1)} %get-tuple-element.35.refs_1_, bf16[256,4096]{1,0:T(8,128)(2,1)S(1)} %get-tuple-element.39.refs_2_, bf16[256,4096]{1,0:T(8,128)(2,1)S(1)} %get-tuple-element.40.refs_3_, ...), custom_call_target="tpu_custom_call" | custom-call | flops 1610612736 | tf_op jit(solution)/shard_map/weight_rows/pallas_call | solution.py:270
  59.8 0.7 %collective-permute-done.17.b_ref = bf16[64,768]{1,0:T(8,128)(2,1)S(1)} collective-permute-done((bf16[64,768]{1,0:T(8,128)(2,1)S(1)}, bf16[64,768]{1,0:T(8,128)(2,1)S(1)}, u32[]{:S(2)}, u32[]{:S(2)}) %collective-permute-start.17) | collective-permute-done | bytes 98336 | tf_op jit(solution)/shard_map/ppermute | solution.py:76
  60.6 1.2 %collective-permute-start.19 = (bf16[16,768]{1,0:T(8,128)(2,1)S(1)}, bf16[16,768]{1,0:T(8,128)(2,1)S(1)}, u32[]{:S(2)}, u32[]{:S(2)}) collective-permute-start(bf16[16,768]{1,0:T(8,128)(2,1)S(1)} %get-tuple-element.49.refs_2_), channel_id=1, source_target_pairs={{0,4},{1,5},{2,6},{3,7},{4,0},{5,1},{6,2},{7,3},{8,12},{9,13},{10,... | collective-permute-start | bytes 73736 | tf_op jit(solution)/shard_map/ppermute | solution.py:76
  61.8 3.2 %collective-permute-start.21 = (bf16[16,768]{1,0:T(8,128)(2,1)S(1)}, bf16[16,768]{1,0:T(8,128)(2,1)S(1)}, u32[]{:S(2)}, u32[]{:S(2)}) collective-permute-start(bf16[16,768]{1,0:T(8,128)(2,1)S(1)} %get-tuple-element.50.refs_3_), channel_id=1, source_target_pairs={{0,6},{1,7},{2,0},{3,1},{4,2},{5,3},{6,4},{7,5},{8,14},{9,15},{10,... | collective-permute-start | bytes 73736 | tf_op jit(solution)/shard_map/ppermute | solution.py:76
  65.0 1.2 %finish_rows.1 = (bf16[2048,768]{1,0:T(8,128)(2,1)}, f32[8,128]{1,0:T(8,128)S(1)}) custom-call(f32[1024,768]{1,0:T(8,128)S(1)} %weight_partial.5.refs_0_.mine_ref, bf16[1024,768]{1,0:T(8,128)(2,1)S(1)} %collective-permute-done.13.other_ref, bf16[2048,768]{1,0:T(8,128)(2,1)} %get-tuple-element.45.refs_0_, ...), custom_call_target="tpu_custom_call", output_to_operand_aliasing={{0}: (2, {})} | custom-call | flops 1610612736 | tf_op jit(solution)/shard_map/finish_rows/pallas_call | solution.py:299
  66.3 0.5 collective-permute-done.20.b_ref
  66.8 0.6 add.32
  (13 shorter events, 0.1 us)
Async XLA Ops:
  0.6 7.5 %collective-permute-start = (bf16[16,768]{1,0:T(8,128)(2,1)}, bf16[16,768]{1,0:T(8,128)(2,1)S(1)}, u32[]{:S(2)}, u32[]{:S(2)}) collective-permute-start(bf16[16,768]{1,0:T(8,128)(2,1)} %x_ref.1), channel_id=1, source_target_pairs={{0,4},{1,5},{2,6},{3,7},{4,0},{5,1},{6,2},{7,3},{8,12},{9,13},{10,... | collective-permute-start | bytes 73736 | tf_op jit(solution)/shard_map/ppermute | solution.py:72
  4.7 4.0 %collective-permute-start.1 = (bf16[16,768]{1,0:T(8,128)(2,1)}, bf16[16,768]{1,0:T(8,128)(2,1)S(1)}, u32[]{:S(2)}, u32[]{:S(2)}) collective-permute-start(bf16[16,768]{1,0:T(8,128)(2,1)} %x_ref.1), channel_id=1, source_target_pairs={{0,6},{1,7},{2,0},{3,1},{4,2},{5,3},{6,4},{7,5},{8,14},{9,15},{10,... | collective-permute-start | bytes 73736 | tf_op jit(solution)/shard_map/ppermute | solution.py:72
  5.4 5.2 %collective-permute-start.2 = (bf16[16,768]{1,0:T(8,128)(2,1)}, bf16[16,768]{1,0:T(8,128)(2,1)S(1)}, u32[]{:S(2)}, u32[]{:S(2)}) collective-permute-start(bf16[16,768]{1,0:T(8,128)(2,1)} %x_ref.1), channel_id=1, source_target_pairs={{0,2},{1,3},{2,4},{3,5},{4,6},{5,7},{6,0},{7,1},{8,10},{9,11},{10,... | collective-permute-start | bytes 73736 | tf_op jit(solution)/shard_map/ppermute | solution.py:72
  6.7 1.4 %collective-permute-start.3 = (f32[1,2048]{1,0:T(1,128)}, f32[1,2048]{1,0:T(1,128)S(1)}, u32[]{:S(2)}, u32[]{:S(2)}) collective-permute-start(f32[1,2048]{1,0:T(1,128)} %bitcast.9), channel_id=1, source_target_pairs={{0,1},{1,0},{2,3},{3,2},{4,5},{5,4},{6,7},{7,6},{8,9},{9,8},{10,11... | collective-permute-start | bytes 24584 | tf_op jit(solution)/shard_map/ppermute | solution.py:83
  10.6 14.0 %collective-permute-start.7 = (bf16[2048,768]{1,0:T(8,128)(2,1)}, bf16[2048,768]{1,0:T(8,128)(2,1)S(1)}, u32[]{:S(2)}, u32[]{:S(2)}) collective-permute-start(bf16[2048,768]{1,0:T(8,128)(2,1)} %w_ref.1), channel_id=1, source_target_pairs={{0,1},{1,0},{2,3},{3,2},{4,5},{5,4},{6,7},{7,6},{8,9},{9,8},{10,11... | collective-permute-start | bytes 9437192 | tf_op jit(solution)/shard_map/ppermute | solution.py:83
  10.7 8.6 %collective-permute-start.4 = (bf16[64,768]{1,0:T(8,128)(2,1)S(1)}, bf16[64,768]{1,0:T(8,128)(2,1)S(1)}, u32[]{:S(2)}, u32[]{:S(2)}) collective-permute-start(bf16[64,768]{1,0:T(8,128)(2,1)S(1)} %join.2.refs_0_), channel_id=1, source_target_pairs={{0,64},{1,17},{2,66},{3,19},{4,68},{5,21},{6,70},{7,23},{8,72},{9,... | collective-permute-start | bytes 294920 | tf_op jit(solution)/shard_map/ppermute | solution.py:72
  14.0 5.3 %collective-permute-start.5 = (bf16[64,768]{1,0:T(8,128)(2,1)S(1)}, bf16[64,768]{1,0:T(8,128)(2,1)S(1)}, u32[]{:S(2)}, u32[]{:S(2)}) collective-permute-start(bf16[64,768]{1,0:T(8,128)(2,1)S(1)} %join.2.refs_0_), channel_id=1, source_target_pairs={{0,96},{1,25},{2,98},{3,27},{4,100},{5,29},{6,102},{7,31},{8,104},... | collective-permute-start | bytes 294920 | tf_op jit(solution)/shard_map/ppermute | solution.py:72
  15.1 5.8 %collective-permute-start.6 = (bf16[64,768]{1,0:T(8,128)(2,1)S(1)}, bf16[64,768]{1,0:T(8,128)(2,1)S(1)}, u32[]{:S(2)}, u32[]{:S(2)}) collective-permute-start(bf16[64,768]{1,0:T(8,128)(2,1)S(1)} %join.2.refs_0_), channel_id=1, source_target_pairs={{0,32},{1,9},{2,34},{3,11},{4,36},{5,13},{6,38},{7,15},{8,40},{9,1... | collective-permute-start | bytes 294920 | tf_op jit(solution)/shard_map/ppermute | solution.py:72
  20.9 8.0 %collective-permute-start.8 = (bf16[256,768]{1,0:T(8,128)(2,1)S(1)}, bf16[256,768]{1,0:T(8,128)(2,1)S(1)}, u32[]{:S(2)}, u32[]{:S(2)}) collective-permute-start(bf16[256,768]{1,0:T(8,128)(2,1)S(1)} %join.3.f_ref.refs_4_), channel_id=1, source_target_pairs={{0,8},{1,33},{2,10},{3,35},{4,12},{5,37},{6,14},{7,39},{8,0},{9,41... | collective-permute-start | bytes 1179656 | tf_op jit(solution)/shard_map/ppermute | solution.py:59
  22.5 11.7 %collective-permute-start.10 = (bf16[256,768]{1,0:T(8,128)(2,1)S(1)}, bf16[256,768]{1,0:T(8,128)(2,1)S(1)}, u32[]{:S(2)}, u32[]{:S(2)}) collective-permute-start(bf16[256,768]{1,0:T(8,128)(2,1)S(1)} %join.3.f_ref.refs_4_), channel_id=1, source_target_pairs={{0,24},{1,97},{2,26},{3,99},{4,28},{5,101},{6,30},{7,103},{8,16},{... | collective-permute-start | bytes 1179656 | tf_op jit(solution)/shard_map/ppermute | solution.py:59
  28.2 11.8 %collective-permute-start.9 = (bf16[256,768]{1,0:T(8,128)(2,1)S(1)}, bf16[256,768]{1,0:T(8,128)(2,1)S(1)}, u32[]{:S(2)}, u32[]{:S(2)}) collective-permute-start(bf16[256,768]{1,0:T(8,128)(2,1)S(1)} %get-tuple-element.36), channel_id=1, source_target_pairs={{0,16},{1,65},{2,18},{3,67},{4,20},{5,69},{6,22},{7,71},{8,24},{9,... | collective-permute-start | bytes 1179656 | tf_op jit(solution)/shard_map/ppermute | solution.py:59
  32.7 11.8 %collective-permute-start.11 = (bf16[256,768]{1,0:T(8,128)(2,1)S(1)}, bf16[256,768]{1,0:T(8,128)(2,1)S(1)}, u32[]{:S(2)}, u32[]{:S(2)}) collective-permute-start(bf16[256,768]{1,0:T(8,128)(2,1)S(1)} %get-tuple-element.37.refs_0_), channel_id=1, source_target_pairs={{0,8},{1,33},{2,10},{3,35},{4,12},{5,37},{6,14},{7,39},{8,0},{9,41... | collective-permute-start | bytes 1179656 | tf_op jit(solution)/shard_map/ppermute | solution.py:59
  37.9 9.1 %collective-permute-start.12 = (bf16[256,768]{1,0:T(8,128)(2,1)S(1)}, bf16[256,768]{1,0:T(8,128)(2,1)S(1)}, u32[]{:S(2)}, u32[]{:S(2)}) collective-permute-start(bf16[256,768]{1,0:T(8,128)(2,1)S(1)} %get-tuple-element.38.refs_0_), channel_id=1, source_target_pairs={{0,24},{1,97},{2,26},{3,99},{4,28},{5,101},{6,30},{7,103},{8,16},{... | collective-permute-start | bytes 1179656 | tf_op jit(solution)/shard_map/ppermute | solution.py:59
  43.7 9.4 %collective-permute-start.15 = (bf16[256,768]{1,0:T(8,128)(2,1)S(1)}, bf16[256,768]{1,0:T(8,128)(2,1)S(1)}, u32[]{:S(2)}, u32[]{:S(2)}) collective-permute-start(bf16[256,768]{1,0:T(8,128)(2,1)S(1)} %get-tuple-element.41), channel_id=1, source_target_pairs={{0,16},{1,65},{2,18},{3,67},{4,20},{5,69},{6,22},{7,71},{8,24},{9,... | collective-permute-start | bytes 1179656 | tf_op jit(solution)/shard_map/ppermute | solution.py:59
  46.3 10.7 %collective-permute-start.14 = (bf16[1024,768]{1,0:T(8,128)(2,1)S(1)}, bf16[1024,768]{1,0:T(8,128)(2,1)S(1)}, u32[]{:S(2)}, u32[]{:S(2)}) collective-permute-start(bf16[1024,768]{1,0:T(8,128)(2,1)S(1)} %weight_partial.3.refs_8_), channel_id=1, source_target_pairs={{0,1},{1,0},{2,3},{3,2},{4,5},{5,4},{6,7},{7,6},{8,9},{9,8},{10,11... | collective-permute-start | bytes 4718600 | tf_op jit(solution)/shard_map/ppermute | solution.py:83
  48.8 16.2 %collective-permute-start.13 = (bf16[1024,768]{1,0:T(8,128)(2,1)S(1)}, bf16[1024,768]{1,0:T(8,128)(2,1)S(1)}, u32[]{:S(2)}, u32[]{:S(2)}) collective-permute-start(bf16[1024,768]{1,0:T(8,128)(2,1)S(1)} %weight_partial.4.refs_9_), channel_id=1, source_target_pairs={{0,1},{1,0},{2,3},{3,2},{4,5},{5,4},{6,7},{7,6},{8,9},{9,8},{10,11... | collective-permute-start | bytes 4718600 | tf_op jit(solution)/shard_map/ppermute | solution.py:83
  53.2 6.6 %collective-permute-start.16 = (bf16[64,768]{1,0:T(8,128)(2,1)S(1)}, bf16[64,768]{1,0:T(8,128)(2,1)S(1)}, u32[]{:S(2)}, u32[]{:S(2)}) collective-permute-start(bf16[64,768]{1,0:T(8,128)(2,1)S(1)} %get-tuple-element.43.refs_10_), channel_id=1, source_target_pairs={{0,64},{1,17},{2,66},{3,19},{4,68},{5,21},{6,70},{7,23},{8,72},{9,... | collective-permute-start | bytes 294920 | tf_op jit(solution)/shard_map/ppermute | solution.py:76
  53.8 6.7 %collective-permute-start.17 = (bf16[64,768]{1,0:T(8,128)(2,1)S(1)}, bf16[64,768]{1,0:T(8,128)(2,1)S(1)}, u32[]{:S(2)}, u32[]{:S(2)}) collective-permute-start(bf16[64,768]{1,0:T(8,128)(2,1)S(1)} %get-tuple-element.42.refs_9_), channel_id=1, source_target_pairs={{0,32},{1,9},{2,34},{3,11},{4,36},{5,13},{6,38},{7,15},{8,40},{9,1... | collective-permute-start | bytes 294920 | tf_op jit(solution)/shard_map/ppermute | solution.py:76
  54.9 5.6 %collective-permute-start.18 = (bf16[64,768]{1,0:T(8,128)(2,1)S(1)}, bf16[64,768]{1,0:T(8,128)(2,1)S(1)}, u32[]{:S(2)}, u32[]{:S(2)}) collective-permute-start(bf16[64,768]{1,0:T(8,128)(2,1)S(1)} %get-tuple-element.44.refs_11_), channel_id=1, source_target_pairs={{0,96},{1,25},{2,98},{3,27},{4,100},{5,29},{6,102},{7,31},{8,104},... | collective-permute-start | bytes 294920 | tf_op jit(solution)/shard_map/ppermute | solution.py:76
  60.6 5.7 %collective-permute-start.19 = (bf16[16,768]{1,0:T(8,128)(2,1)S(1)}, bf16[16,768]{1,0:T(8,128)(2,1)S(1)}, u32[]{:S(2)}, u32[]{:S(2)}) collective-permute-start(bf16[16,768]{1,0:T(8,128)(2,1)S(1)} %get-tuple-element.49.refs_2_), channel_id=1, source_target_pairs={{0,4},{1,5},{2,6},{3,7},{4,0},{5,1},{6,2},{7,3},{8,12},{9,13},{10,... | collective-permute-start | bytes 73736 | tf_op jit(solution)/shard_map/ppermute | solution.py:76
  61.8 5.0 %collective-permute-start.20 = (bf16[16,768]{1,0:T(8,128)(2,1)S(1)}, bf16[16,768]{1,0:T(8,128)(2,1)S(1)}, u32[]{:S(2)}, u32[]{:S(2)}) collective-permute-start(bf16[16,768]{1,0:T(8,128)(2,1)S(1)} %get-tuple-element.48.refs_1_), channel_id=1, source_target_pairs={{0,2},{1,3},{2,4},{3,5},{4,6},{5,7},{6,0},{7,1},{8,10},{9,11},{10,... | collective-permute-start | bytes 73736 | tf_op jit(solution)/shard_map/ppermute | solution.py:76
  61.8 5.0 %collective-permute-start.21 = (bf16[16,768]{1,0:T(8,128)(2,1)S(1)}, bf16[16,768]{1,0:T(8,128)(2,1)S(1)}, u32[]{:S(2)}, u32[]{:S(2)}) collective-permute-start(bf16[16,768]{1,0:T(8,128)(2,1)S(1)} %get-tuple-element.50.refs_3_), channel_id=1, source_target_pairs={{0,6},{1,7},{2,0},{3,1},{4,2},{5,3},{6,4},{7,5},{8,14},{9,15},{10,... | collective-permute-start | bytes 73736 | tf_op jit(solution)/shard_map/ppermute | solution.py:76
